TPU v7x, 128 devices: a whole 4x4x4 slice. The times are simulated.
128 devices in a mesh: sub: 32 (over z, x, core), row: 4 (over y).
Axes of the slice: x: 4, y: 4, z: 4, core: 2. Of those that a mesh axis runs over, the one named last changes fastest.
Arguments:
- deflation: bfloat16 [128, 96, 3, 2, 8, 128], P('sub', None, None, None, 'row'), may hold values from -0.8984375 to 0.8984375
- center: float32 [128, 2, 8, 128], P('sub', None, 'row'), may hold values from 2 to 6
- stiffness: float32 [128, 26, 2, 8, 128], P('sub', None, None, 'row'), may hold values from 0.1 to 1
- coupling: float32 [26, 3, 3], replicated, may hold values from -3.5 to 3.5
- neighbours: int32 [128, 26], P('sub'), may hold values from -1 to 127, as said below
- shared_rows: int32 [128, 26, 1536], P('sub', None, 'row'), may hold values from 0 to 1535
Outputs:
- pair_blocks: float32 [128, 26, 9216], P('sub', None, 'row')
- self_blocks: float32 [128, 9216], P('sub', 'row')
Inputs may be any that keep to these rules, and one draw needn't show every extreme that they name: `neighbours`: subdomain i = 4 d + p belongs to device d along sub. Each list names each neighbour once and fills empty slots with -1; adjacency is symmetric. Subdomain 4 d + p is adjacent only to 4 d + (p xor 1), 4 d + (p xor 2) and subdomains of devices d + 1, d + 2, d + 3, d - 1, d - 2, d - 3 counted cyclically over the devices along sub. Some subdomain has all 26 slots filled.
All inputs are finite; a program needn't handle non-finite values.
Results may differ from a plain program's by a relative error of at most 0.0029.
Values may be sent and summed in bfloat16 or wider, within the bound.
No kernel may reach another device: no remote copies, remote signals or barrier semaphores. Data moves between devices by JAX's collectives and lax.ppermute only.
A program may use at most 320 MiB of HBM per device.

v0:
```python
import jax
import jax.numpy as jnp
from jax import lax
from jax.sharding import PartitionSpec as P

stencil_offsets = [
    (shift_x, shift_y, shift_z)
    for shift_x in (-1, 0, 1)
    for shift_y in (-1, 0, 1)
    for shift_z in (-1, 0, 1)
    if (shift_x, shift_y, shift_z) != (0, 0, 0)
]


def extended(x, sides, width):
    for axis, dim in sides:
        count, length = (lax.axis_size(axis), x.shape[dim])
        up = [(i, (i + 1) % count) for i in range(count - 1)]
        down = [(j, i) for i, j in up]
        last = lax.slice_in_dim(x, length - width, length, axis=dim)
        first = lax.slice_in_dim(x, 0, width, axis=dim)
        before = lax.ppermute(last, axis, up)
        after = lax.ppermute(first, axis, down)
        x = jnp.concatenate([before, x, after], axis=dim)
    return x


def passed_along(x, axis, by):
    count = lax.axis_size(axis)
    return lax.ppermute(x, axis, [(i, (i + by) % count) for i in range(count)])


def mix_components(shifted, matrix):
    mixed_parts = [
        matrix[component, 0] * shifted[:, 0]
        + matrix[component, 1] * shifted[:, 1]
        + matrix[component, 2] * shifted[:, 2]
        for component in range(3)
    ]
    return jnp.stack(mixed_parts, axis=1)


def apply_operator(padded, vectors, center, stiffness, coupling):
    size_x, size_y, size_z = (vectors.shape[2], vectors.shape[3], vectors.shape[4])
    terms = []
    for offset_index, (shift_x, shift_y, shift_z) in enumerate(stencil_offsets):
        shifted = padded[
            :,
            :,
            1 + shift_x : 1 + shift_x + size_x,
            1 + shift_y : 1 + shift_y + size_y,
            1 + shift_z : 1 + shift_z + size_z,
        ].astype(jnp.float32)
        terms.append(stiffness[offset_index] * mix_components(shifted, coupling[offset_index]))
    total = terms[0]
    for term in terms[1:]:
        total = total + term
    running = center * vectors.astype(jnp.float32) - total
    return running.astype(jnp.bfloat16)


def select_rows(row_major, index_rows):
    return row_major[index_rows]


def on_device(deflation, center, stiffness, coupling, neighbours, shared_rows):
    sub_count = lax.axis_size("sub")
    row_count = lax.axis_size("row")
    local_subs = deflation.shape[0]
    width_k = deflation.shape[1]
    slot_count = neighbours.shape[1]
    padded = extended(deflation, (("row", 4),), 1)
    padded = jnp.pad(padded, ((0, 0), (0, 0), (0, 0), (1, 1), (0, 0), (1, 1)))
    applied = jax.vmap(apply_operator, in_axes=(0, 0, 0, 0, None))(
        padded, deflation, center, stiffness, coupling
    )
    rows_dev = applied.shape[2] * applied.shape[3] * applied.shape[4] * applied.shape[5]
    applied_flat = applied.reshape(local_subs, width_k, rows_dev)
    vector_flat = deflation.reshape(local_subs, width_k, rows_dev)
    applied_major = jnp.transpose(applied_flat, (0, 2, 1))
    vector_major = jnp.transpose(vector_flat, (0, 2, 1))
    applied_rows = jax.vmap(select_rows)(applied_major, shared_rows)
    vector_rows = jax.vmap(select_rows)(vector_major, shared_rows)
    self_part = jnp.einsum(
        "skr,slr->skl", applied_flat, vector_flat, preferred_element_type=jnp.float32
    )
    local_ids = jnp.arange(local_subs, dtype=jnp.int32)
    own_index = lax.axis_index("sub")
    pieces = []
    source_list = []
    for offset_step in (0, 1, 2, 3, -1, -2, -3):
        targets = (own_index - offset_step) % sub_count * local_subs + local_ids
        chosen = (neighbours[:, None, :] == targets[None, :, None]).astype(jnp.bfloat16)
        send_block = jnp.einsum(
            "jqn,jnrk->jqrk", chosen, vector_rows, preferred_element_type=jnp.float32
        ).astype(jnp.bfloat16)
        if offset_step != 0:
            send_block = passed_along(send_block, "sub", -offset_step)
        pieces.append(send_block)
        source_list.append((own_index + offset_step) % sub_count)
    arrived = jnp.stack(pieces)
    sources = jnp.stack(source_list)
    sender_ids = sources[:, None] * local_subs + local_ids[None, :]
    matched = (neighbours[:, :, None, None] == sender_ids[None, None, :, :]).astype(jnp.bfloat16)
    partner = jnp.einsum(
        "qnsp,spqrk->qnrk", matched, arrived, preferred_element_type=jnp.float32
    ).astype(jnp.bfloat16)
    pair_part = jnp.einsum(
        "qnrk,qnrl->qnkl", applied_rows, partner, preferred_element_type=jnp.float32
    )
    pair_flat = pair_part.reshape(local_subs, slot_count, width_k * width_k)
    self_flat = self_part.reshape(local_subs, width_k * width_k)
    summed_pairs, summed_self = lax.psum((pair_flat, self_flat), "row")
    share_width = width_k * width_k // row_count
    start_col = lax.axis_index("row") * share_width
    pair_share = lax.dynamic_slice_in_dim(summed_pairs, start_col, share_width, 2)
    self_share = lax.dynamic_slice_in_dim(summed_self, start_col, share_width, 1)
    self_scale = float(rows_dev * row_count) ** (-0.5)
    return (pair_share, self_share * self_scale)


def solution(mesh):
    return jax.shard_map(
        on_device,
        mesh=mesh,
        in_specs=(
            P("sub", None, None, None, "row", None),
            P("sub", None, "row", None),
            P("sub", None, None, "row", None),
            P(),
            P("sub", None),
            P("sub", None, "row"),
        ),
        out_specs=(P("sub", None, "row"), P("sub", "row")),
        check_vma=False,
    )
```

profile of v0, /device:TPU:0, one launch (start us, length us, event | category | flops | bytes accessed | tf_op | source)
XLA Modules:
  0.0 1372.6 jit_solution(7249848031581667836)
XLA Ops:
  21.2 387.9 %gather_fusion.1 = bf16[39936,96]{1,0:T(8,128)(2,1)} fusion(bf16[4,1536,96]{2,1,0:T(8,128)(2,1)S(1)} %bitcast.379, s32[39936]{0:T(1024)S(1)} %reshape.154), kind=kCustom, calls=%fused_computation.1 | custom fusion | bytes 15654912 | tf_op jit(solution)/shard_map/vmap()/gather | solution.py:63
  409.2 15.5 %copy.44 = bf16[4,26,384,96]{2,1,3,0:T(8,128)(2,1)} copy(bf16[4,26,384,96]{3,2,1,0:T(8,128)(2,1)} %bitcast.383) | data formatting | bytes 15335424 | tf_op jit(solution)/shard_map/vmap()/gather | solution.py:63
  491.8 13.8 %select_maximum_fusion = bf16[4,96,3,4,4,130]{5,4,3,2,1,0:T(4,128)(2,1)S(1)} fusion(bf16[4,96,3,2,1,128]{5,4,3,2,1,0:T(2,128)(2,1)S(1)} %copy.38, bf16[4,96,3,2,2,128]{5,4,3,2,1,0:T(2,128)(2,1)S(1)} %copy-done.1, bf16[4,96,3,2,1,128]{5,4,3,2,1,0:T(2,128)(2,1)S(1)} %copy.37), kind=kLoop, calls=%fused_computation.12 | loop fusion | flops 45527040 | bytes 7151616 | tf_op jit(solution)/shard_map/concatenate | solution.py:24
  509.3 9.8 slice_convert_fusion.22
  519.1 44.5 %slice_convert_fusion.23 = (f32[4,96,3,2,2,128]{5,4,3,2,1,0:T(2,128)}, f32[4,96,3,2,2,128]{5,4,3,2,1,0:T(2,128)}, f32[4,96,3,2,2,128]{5,4,3,2,1,0:T(2,128)}, f32...) fusion(bf16[4,96,3,4,4,130]{5,4,3,2,1,0:T(4,128)(2,1)} %copy-done), kind=kLoop, calls=%fused_computation.105 | loop fusion | flops 11206656 | bytes 67239936 | tf_op jit(solution)/shard_map/vmap()/convert_element_type | solution.py:53
  666.4 7.6 multiply_add_fusion.41
  674.1 8.0 multiply_add_fusion.44
  682.1 8.3 multiply_add_fusion.47
  690.4 8.3 multiply_add_fusion.50
  698.8 8.3 multiply_add_fusion.53
  707.1 8.3 multiply_add_fusion.56
  715.4 8.2 multiply_add_fusion.59
  723.6 8.2 multiply_add_fusion.62
  731.8 8.2 multiply_add_fusion.65
  740.0 8.2 multiply_add_fusion.68
  748.2 8.3 multiply_add_fusion.71
  756.5 8.3 multiply_add_fusion.74
  764.8 8.0 multiply_add_fusion.77
  772.8 35.6 %subtract_convert_fusion = bf16[4,96,3,2,2,128]{5,4,3,2,1,0:T(2,128)(2,1)} fusion(bf16[4,96,3,2,2,128]{5,4,3,2,1,0:T(2,128)(2,1)S(1)} %copy-done.1, f32[4,96,1,2,2,128]{5,4,3,2,1,0:T(2,128)S(1)} %get-tuple-element.131, f32[4,96,1,2,2,128]{5,4,3,2,1,0:T(2,128)S(1)} %get-tuple-element.130, f32[4,96,1,2,2,128]{5,4,3,2,1,0:T(2,128)S(1)} %get-tuple-element.129, ...), kind=kLoop, calls=%fused_computation.68 | loop fusion | flops 63111168 | bytes 63922176 | tf_op jit(solution)/shard_map/vmap()/convert_element_type | solution.py:59
  811.9 388.0 %gather_fusion = bf16[39936,96]{1,0:T(8,128)(2,1)} fusion(bf16[4,1536,96]{2,1,0:T(8,128)(2,1)S(1)} %bitcast.382, s32[39936]{0:T(1024)S(1)} %reshape.154), kind=kCustom, calls=%fused_computation | custom fusion | bytes 15654912 | tf_op jit(solution)/shard_map/vmap()/gather | solution.py:63
  1215.6 16.5 %collective-permute-done.7 = bf16[4,4,384,96]{2,1,3,0:T(4,128)(2,1)S(1)} collective-permute-done((bf16[4,4,384,96]{2,1,3,0:T(4,128)(2,1)S(1)}, bf16[4,4,384,96]{2,1,3,0:T(4,128)(2,1)S(1)}, u32[]{:S(2)}, u32[]{:S(2)}) %collective-permute-start.7) | collective-permute-done | bytes 1179680 | tf_op jit(solution)/shard_map/ppermute | solution.py:30
  1233.5 23.0 %bitcast_convert_fusion = bf16[4,26,384,96]{2,1,3,0:T(8,128)(2,1)} fusion(bf16[7,4,4,384,96]{3,2,4,1,0:T(4,128)(2,1)} %bitcast_dynamic-update-slice_fusion, s32[7,4]{0,1:T(4,128)S(1)} %iota_add_fusion, s32[4,26]{1,0:T(4,128)S(1)} %copy-done.29), kind=kOutput, calls=%fused_computation.6 | convolution fusion | flops 218532704 | bytes 15925776 | tf_op jit(solution)/shard_map/qnsp,spqrk->qnrk/dot_general | solution.py:105
  1256.6 12.0 fusion.3
  1275.3 86.4 %all-reduce.4.cloned.1.call-done = (f32[4,26,9216]{2,0,1:T(4,128)}, f32[4,9216]{1,0:T(4,128)}) async-done(((f32[4,26,9216]{2,0,1:T(4,128)}, f32[4,9216]{1,0:T(4,128)}), (f32[4,26,9216]{2,0,1:T(4,128)}, f32[4,9216]{1,0:T(4,128)})) %all-reduce.4.cloned.1.call-update) | async-done | bytes 3981328 | tf_op jit(solution)/shard_map/psum | solution.py:113
  (162 shorter events, 218.1 us)
Async XLA Ops:
  7.2 1354.5 %all-reduce.4.cloned.1.call-start = ((), (), s32[]{:S(2)}) async-start(), calls=%async_computation | async-start | bytes 7962624 | tf_op jit(solution)/shard_map/psum | solution.py:113
  11.0 8.7 copy-start.1
  12.0 9.1 copy-start.32
  12.0 473.3 %collective-permute-start.1 = (bf16[4,96,3,2,1,128]{5,1,4,3,2,0:T(8,128)(2,1)}, bf16[4,96,3,2,1,128]{5,1,4,3,2,0:T(8,128)(2,1)}, u32[]{:S(2)}, u32[]{:S(2)}) collective-permute-start(bf16[4,96,3,2,1,128]{5,1,4,3,2,0:T(8,128)(2,1)} %copy.74), channel_id=1, source_target_pairs={{1,0},{2,1},{3,2},{5,4},{6,5},{7,6},{9,8},{10,9},{11,10},{13,12},{... | collective-permute-start | bytes 1769480 | tf_op jit(solution)/shard_map/ppermute | solution.py:23
  14.3 473.2 %collective-permute-start = (bf16[4,96,3,2,1,128]{5,1,4,3,2,0:T(8,128)(2,1)}, bf16[4,96,3,2,1,128]{5,1,4,3,2,0:T(8,128)(2,1)}, u32[]{:S(2)}, u32[]{:S(2)}) collective-permute-start(bf16[4,96,3,2,1,128]{5,1,4,3,2,0:T(8,128)(2,1)} %copy.73), channel_id=1, source_target_pairs={{0,1},{1,2},{2,3},{4,5},{5,6},{6,7},{8,9},{9,10},{10,11},{12,13},{... | collective-permute-start | bytes 1769480 | tf_op jit(solution)/shard_map/ppermute | solution.py:22
  409.2 15.5 %copy-start.29 = (s32[4,26]{1,0:T(4,128)S(1)}, s32[4,26]{1,0:T(4,128)}, u32[]{:S(2)}) copy-start(s32[4,26]{1,0:T(4,128)} %param.10) | copy-start | bytes 1252
  430.8 769.9 %collective-permute-start.2 = (bf16[4,4,384,96]{2,1,3,0:T(4,128)(2,1)}, bf16[4,4,384,96]{2,1,3,0:T(4,128)(2,1)}, u32[]{:S(2)}, u32[]{:S(2)}) collective-permute-start(bf16[4,4,384,96]{2,1,3,0:T(4,128)(2,1)} %convolution_convert_fusion.5), channel_id=1, source_target_pairs={{0,124},{4,0},{8,4},{12,8},{16,12},{20,16},{24,20},{28,24},{32,28}... | collective-permute-start | bytes 3538952 | tf_op jit(solution)/shard_map/ppermute | solution.py:30
  442.1 762.6 %collective-permute-start.3 = (bf16[4,4,384,96]{2,1,3,0:T(4,128)(2,1)}, bf16[4,4,384,96]{2,1,3,0:T(4,128)(2,1)}, u32[]{:S(2)}, u32[]{:S(2)}) collective-permute-start(bf16[4,4,384,96]{2,1,3,0:T(4,128)(2,1)} %convolution_convert_fusion.4), channel_id=1, source_target_pairs={{0,120},{4,124},{8,0},{12,4},{16,8},{20,12},{24,16},{28,20},{32,24... | collective-permute-start | bytes 3538952 | tf_op jit(solution)/shard_map/ppermute | solution.py:30
  449.4 758.0 %collective-permute-start.4 = (bf16[4,4,384,96]{2,1,3,0:T(4,128)(2,1)}, bf16[4,4,384,96]{2,1,3,0:T(4,128)(2,1)}, u32[]{:S(2)}, u32[]{:S(2)}) collective-permute-start(bf16[4,4,384,96]{2,1,3,0:T(4,128)(2,1)} %convolution_convert_fusion.3), channel_id=1, source_target_pairs={{0,116},{4,120},{8,124},{12,0},{16,4},{20,8},{24,12},{28,16},{32,2... | collective-permute-start | bytes 3538952 | tf_op jit(solution)/shard_map/ppermute | solution.py:30
  485.2 724.9 %collective-permute-start.5 = (bf16[4,4,384,96]{2,1,3,0:T(4,128)(2,1)}, bf16[4,4,384,96]{2,1,3,0:T(4,128)(2,1)}, u32[]{:S(2)}, u32[]{:S(2)}) collective-permute-start(bf16[4,4,384,96]{2,1,3,0:T(4,128)(2,1)} %convolution_convert_fusion.2), channel_id=1, source_target_pairs={{0,4},{4,8},{8,12},{12,16},{16,20},{20,24},{24,28},{28,32},{32,36}... | collective-permute-start | bytes 3538952 | tf_op jit(solution)/shard_map/ppermute | solution.py:30
  487.5 725.4 %collective-permute-start.6 = (bf16[4,4,384,96]{2,1,3,0:T(4,128)(2,1)}, bf16[4,4,384,96]{2,1,3,0:T(4,128)(2,1)}, u32[]{:S(2)}, u32[]{:S(2)}) collective-permute-start(bf16[4,4,384,96]{2,1,3,0:T(4,128)(2,1)} %convolution_convert_fusion.1), channel_id=1, source_target_pairs={{0,8},{4,12},{8,16},{12,20},{16,24},{20,28},{24,32},{28,36},{32,40... | collective-permute-start | bytes 3538952 | tf_op jit(solution)/shard_map/ppermute | solution.py:30
  682.1 8.3 copy-start.13
  690.4 8.3 copy-start.12
  698.8 8.3 copy-start.11
  707.1 8.3 copy-start.10
  723.6 8.2 copy-start.8
  731.8 8.2 copy-start.7
  748.2 8.3 copy-start.4
  756.5 8.3 copy-start.5
  811.9 388.8 %copy-start.30 = (bf16[4,4,384,96]{2,1,3,0:T(4,128)(2,1)S(1)}, bf16[4,4,384,96]{2,1,3,0:T(4,128)(2,1)}, u32[]{:S(2)}) copy-start(bf16[4,4,384,96]{2,1,3,0:T(4,128)(2,1)} %convolution_convert_fusion) | copy-start | bytes 3538948
  1200.7 31.4 %collective-permute-start.7 = (bf16[4,4,384,96]{2,1,3,0:T(4,128)(2,1)S(1)}, bf16[4,4,384,96]{2,1,3,0:T(4,128)(2,1)S(1)}, u32[]{:S(2)}, u32[]{:S(2)}) collective-permute-start(bf16[4,4,384,96]{2,1,3,0:T(4,128)(2,1)S(1)} %copy-done.30), channel_id=1, source_target_pairs={{0,12},{4,16},{8,20},{12,24},{16,28},{20,32},{24,36},{28,40},{32,4... | collective-permute-start | bytes 3538952 | tf_op jit(solution)/shard_map/ppermute | solution.py:30
  1232.1 24.5 %slice-start = ((s8[10223616]{0:T(1024)(128)(4,1)}), s8[4194304]{0:T(1024)(128)(4,1)S(1)}, s32[]{:S(2)}) async-start(s8[10223616]{0:T(1024)(128)(4,1)} %bitcast.384), calls=%async_computation.1 | async-start | bytes 8388608
  1233.5 23.0 %slice-start.1 = ((s8[10223616]{0:T(1024)(128)(4,1)}), s8[4194304]{0:T(1024)(128)(4,1)S(1)}, s32[]{:S(2)}) async-start(s8[10223616]{0:T(1024)(128)(4,1)} %bitcast.384), calls=%async_computation.2 | async-start | bytes 8388608
  1233.5 23.0 %slice-start.2 = ((s8[10223616]{0:T(1024)(128)(4,1)}), s8[1835008]{0:T(1024)(128)(4,1)S(1)}, s32[]{:S(2)}) async-start(s8[10223616]{0:T(1024)(128)(4,1)} %bitcast.384), calls=%async_computation.3 | async-start | bytes 3670016
  (22 other events, 149.6 us)
Sparse Core Ops, SparseCore 0:
  1275.4 86.2 all-reduce.3
where the time goes:
time: 1380 us; the launch traced here: 1370 us
  local copies, waits for them, and re-layouts  845 us (61%)
  other arithmetic  314 us (23%)
  waiting for transfers between devices  103 us (7%)
  matrix products  78.5 us (6%)
  starting transfers between devices  16.8 us (1%)
  between operations  15.2 us (1%)
    gather x5, local copies, waits for them, and re-layouts, select_rows(): return row_major[index_rows]  791 us
    add x26, other arithmetic, mix_components(): matrix[component, 0] * shifted[:, 0] + matrix[component, 1] * shifted[:, 1]  203 us
    psum x1, waiting for transfers between devices, on_device(): summed_pairs, summed_self = lax.psum((pair_flat, self_flat), 'row')  86.4 us
    convert_element_type x3, other arithmetic, apply_operator(): shifted = padded[:, :, 1 + shift_x:1 + shift_x + size_x, 1 + shift_y:1 +...  60.4 us
    dot_general x7, matrix products, on_device(): jnp.einsum('jqn,jnrk->jqrk', chosen, vector_rows, preferred_element_type=...  42.9 us
    convert_element_type x1, other arithmetic, apply_operator(): return running.astype(jnp.bfloat16)  35.6 us
  transfers between devices with their start and end apart: 9, of which 2 were waited for; matrix products, arithmetic and copies ran while one was open for 86% of the time, Pallas kernels for 0%

commit v1 on v0

v1 whole, which is shorter than its diff:
```python
import functools

import jax
import jax.numpy as jnp
from jax import lax
from jax.experimental import pallas as pl
from jax.experimental.pallas import tpu as pltpu
from jax.sharding import PartitionSpec as P

f32, bf16, i32, i16 = jnp.float32, jnp.bfloat16, jnp.int32, jnp.int16
K, SUBS, NB, OV, ROWS = 96, 4, 26, 384, 1536
G, L = 6, 256
SHARE = 24
VMEM = 48 << 20


def call(kernel, out_shape, grid_spec, flops, moved):
    return pl.pallas_call(
        kernel,
        out_shape=out_shape,
        grid_spec=grid_spec,
        compiler_params=pltpu.CompilerParams(vmem_limit_bytes=VMEM),
        cost_estimate=pl.CostEstimate(flops=flops, bytes_accessed=moved, transcendentals=0),
    )


def nt_dot(a, b):
    return lax.dot_general(a, b, (((1,), (1,)), ((), ())), preferred_element_type=f32)


def put_shares(row, block, scratch, outs, at):
    scratch[...] = block
    for step in range(4):
        start = pl.multiple_of(lax.rem(row + step, 4) * SHARE, 8)
        outs[step][at] = scratch[pl.ds(start, SHARE), :].astype(outs[step].dtype)


def offset_number(sx, sy, sz):
    flat = (sx + 1) * 9 + (sy + 1) * 3 + sz + 1
    return None if flat == 13 else flat - (flat > 13)


def stencil_kernel(meta, coup, v, below, above, stiff, center, a, s0, s1, s2, s3, scratch):
    distance = (
        lax.broadcasted_iota(i32, (128, 128), 0) - lax.broadcasted_iota(i32, (128, 128), 1)
    ).astype(i16)
    on_band = {sz: distance == sz for sz in (-1, 0, 1)}

    def tile(c, b, y, sy):
        columns = []
        for x in range(2):
            parts = []
            for x_in in range(2):
                block = jnp.zeros((128, 128), bf16)
                for sz in (-1, 0, 1):
                    o = offset_number(x_in - x, sy, sz)
                    if o is None:
                        continue
                    w = stiff[0, o, x, y : y + 1, :] * coup[o, c * 3 + b]
                    w = jnp.broadcast_to(w.astype(bf16), (128, 128))
                    block = jnp.where(on_band[sz], w, block)
                parts.append(block)
            columns.append(jnp.concatenate(parts, axis=0))
        return jnp.concatenate(columns, axis=1)

    def component(c, carry):
        for y in range(2):
            total = None
            for sy in (-1, 0, 1):
                for b in range(3):
                    y_in = y + sy
                    if y_in < 0:
                        lhs = below[0, b]
                    elif y_in > 1:
                        lhs = above[0, b]
                    else:
                        lhs = v[0, 2 * b + y_in]
                    part = jnp.dot(lhs, tile(c, b, y, sy), preferred_element_type=f32)
                    total = part if total is None else total + part
            diag = jnp.concatenate(
                [center[0, x, y : y + 1, :] for x in range(2)], axis=1
            )
            a[0, 2 * c + y] = (diag * v[0, 2 * c + y].astype(f32) - total).astype(bf16)
        return carry

    lax.fori_loop(0, 3, component, 0)
    own = None
    for g in range(G):
        part = nt_dot(a[0, g], v[0, g])
        own = part if own is None else own + part
    put_shares(meta[0], own, scratch, (s0, s1, s2, s3), 0)


def gather_columns(stacked, idx):
    low = (idx & 255).astype(i16)
    high = idx >> 8
    hot = jnp.where(
        lax.broadcasted_iota(i16, (L, idx.shape[1]), 0) == low, bf16(1), bf16(0)
    )
    found = jnp.dot(stacked, hot, preferred_element_type=f32)
    out = found[0:K]
    for g in range(1, G):
        out = jnp.where(high == g, found[g * K : g * K + K], out)
    return out.astype(bf16)


def gather_kernel(a, idx, out):
    stacked = a[0].reshape(G * K, L)
    for t in range(out.shape[2] // L):
        out[0, :, t * L : t * L + L] = gather_columns(stacked, idx[0, :, t * L : t * L + L])


def pair_kernel(meta, v, idx, a0, a1, s0, s1, s2, s3, scratch):
    stacked = v[0].reshape(G * K, L)
    found = jnp.concatenate(
        [gather_columns(stacked, idx[0, :, t * L : t * L + L]) for t in range(3)], axis=1
    )
    for half, rows in enumerate((a0, a1)):
        block = nt_dot(rows[0], found[:, half * OV : half * OV + OV])
        put_shares(meta[0], block, scratch.at[half], (s0, s1, s2, s3), half)


def final_kernel(count, table, *refs):
    pieces, self_pieces = refs[: 4 * count], refs[4 * count : 4 * count + 4]
    out, out_self, total = refs[4 * count + 4 :]
    for o in range(count):
        own, r1, r2, r3 = pieces[4 * o : 4 * o + 4]
        total[16 * o : 16 * o + 16] = (
            own[...] + r1[...].astype(f32) + r2[...].astype(f32) + r3[...].astype(f32)
        )
    own, r1, r2, r3 = self_pieces
    out_self[...] = (
        own[...] + r1[...].astype(f32) + r2[...].astype(f32) + r3[...].astype(f32)
    ) * float(ROWS * 4) ** (-0.5)

    def one(n, carry):
        for q in range(SUBS):
            spot = table[q * NB + n]
            value = total[jnp.maximum(spot, 0)]
            out[q, n] = jnp.where(spot >= 0, value, jnp.float32(0))
        return carry

    lax.fori_loop(0, NB, one, 0)


def share_shapes(count):
    return [jax.ShapeDtypeStruct((count, SHARE, K), f32 if s == 0 else bf16) for s in range(4)]


def row_exchange(shares):
    return [shares[0]] + [
        lax.ppermute(shares[s], "row", [(i, (i + s) % 4) for i in range(4)]) for s in (1, 2, 3)
    ]


def on_device(deflation, center, stiffness, coupling, neighbours, shared_rows):
    n_sub = lax.axis_size("sub")
    me = lax.axis_index("sub")
    row = lax.axis_index("row")
    vt = jnp.transpose(deflation, (0, 2, 4, 1, 3, 5)).reshape(SUBS, G, K, L)

    ring = lambda x, by: lax.ppermute(x, "sub", [(i, (i + by) % n_sub) for i in range(n_sub)])
    swap = lambda x: lax.ppermute(x, "sub", [(i, i ^ 1) for i in range(n_sub)])
    cross = [(i, (i - 1) % n_sub if i % 2 == 0 else (i + 1) % n_sub) for i in range(n_sub)]
    planes = vt.reshape(SUBS, 3, 2, K, L)
    below = lax.ppermute(planes[:, :, 1], "row", [(i, i + 1) for i in range(3)])
    above = lax.ppermute(planes[:, :, 0], "row", [(i + 1, i) for i in range(3)])
    other = swap(vt)
    plus2, minus2 = ring(vt, -2), ring(vt, 2)
    plus2x, minus2x = swap(plus2), swap(minus2)
    far = lax.ppermute(jnp.where(me % 2 == 0, plus2, minus2), "sub", cross)
    blocks = [vt, other, plus2, minus2, plus2x, minus2x, far]

    odd = me % 2
    flip = me + 1 - 2 * odd
    sources = jnp.stack([me, flip, me + 2, me - 2, flip + 2, flip - 2, me - 3 + 6 * odd]) % n_sub
    targets = jnp.stack(
        [me, flip, me - 2, me + 2, flip - 2, flip + 2, me - 3 + 6 * odd]
    ) % n_sub
    subs = jnp.arange(SUBS, dtype=i32)
    source_ids = (sources[:, None] * SUBS + subs).reshape(-1).astype(i32)
    target_ids = (targets[:, None] * SUBS + subs).reshape(-1).astype(i32)
    match = neighbours[:, None, :] == source_ids[None, :, None]
    slot = jnp.max(jnp.where(match, jnp.arange(NB, dtype=i32), -1), axis=2)
    order = (jnp.arange(28, dtype=i32) * 4)[None, :, None] + subs[:, None, None]
    table = jnp.max(jnp.where(match, order, -1), axis=1).reshape(-1)
    meta = jnp.concatenate([row[None].astype(i32), jnp.maximum(slot, 0).reshape(-1)])

    high = (shared_rows >> 9) * 2 + ((shared_rows >> 7) & 1)
    low = ((shared_rows >> 8) & 1) * 128 + (shared_rows & 127)
    idx = high * L + low
    mine = (neighbours[:, None, :] == target_ids[None, :, None]).astype(bf16)
    halves = jnp.concatenate([high, low], axis=2).astype(bf16)
    back = jnp.einsum("jtn,jnm->jtm", mine, halves, preferred_element_type=f32).astype(i32)
    back = (back[:, :, :OV] * L + back[:, :, OV:]).reshape(SUBS, 7, 1, SUBS * OV)
    back_sent = [back[:, o] for o in range(7)]
    back_idx = [
        back_sent[0],
        swap(back_sent[1]),
        ring(back_sent[2], -2),
        ring(back_sent[3], 2),
        lax.ppermute(back_sent[4], "sub", [(i, ((i - 2) % n_sub) ^ 1) for i in range(n_sub)]),
        lax.ppermute(back_sent[5], "sub", [(i, ((i + 2) % n_sub) ^ 1) for i in range(n_sub)]),
        lax.ppermute(
            back_sent[6],
            "sub",
            [(i, (i - 3) % n_sub if i % 2 == 0 else (i + 3) % n_sub) for i in range(n_sub)],
        ),
    ]

    smem = pl.BlockSpec(memory_space=pltpu.SMEM)
    share_specs = lambda n, at: [pl.BlockSpec((n, SHARE, K), at)] * 4
    applied, *self_shares = call(
        stencil_kernel,
        [jax.ShapeDtypeStruct((SUBS, G, K, L), bf16)] + share_shapes(SUBS),
        pltpu.PrefetchScalarGridSpec(
            num_scalar_prefetch=1,
            grid=(SUBS,),
            in_specs=[
                smem,
                pl.BlockSpec((1, G, K, L), lambda s, m: (s, 0, 0, 0)),
                pl.BlockSpec((1, 3, K, L), lambda s, m: (s, 0, 0, 0)),
                pl.BlockSpec((1, 3, K, L), lambda s, m: (s, 0, 0, 0)),
                pl.BlockSpec((1, 26, 2, 2, 128), lambda s, m: (s, 0, 0, 0, 0)),
                pl.BlockSpec((1, 2, 2, 128), lambda s, m: (s, 0, 0, 0)),
            ],
            out_specs=[pl.BlockSpec((1, G, K, L), lambda s, m: (s, 0, 0, 0))]
            + share_specs(1, lambda s, m: (s, 0, 0)),
            scratch_shapes=[pltpu.VMEM((K, K), f32)],
        ),
        4 * 54 * 2 * 256 * 256 * 256,
        8 << 20,
    )(meta[:1], coupling.reshape(26, 9), vt, below, above, stiffness, center)

    own_rows = call(
        gather_kernel,
        jax.ShapeDtypeStruct((SUBS, K, NB * OV), bf16),
        pl.GridSpec(
            grid=(SUBS, 13),
            in_specs=[
                pl.BlockSpec((1, G, K, L), lambda s, t: (s, 0, 0, 0)),
                pl.BlockSpec((1, 1, 3 * L), lambda s, t: (s, 0, t)),
            ],
            out_specs=pl.BlockSpec((1, K, 3 * L), lambda s, t: (s, 0, t)),
        ),
        25 * 10**9,
        16 << 20,
    )(applied, idx.reshape(SUBS, 1, NB * OV))

    pieces = []
    for o in range(7):
        a_spec = lambda half: pl.BlockSpec(
            (1, K, OV),
            lambda p, h, m, o=o: (2 * h + half, 0, m[1 + (2 * h + half) * 28 + o * 4 + p]),
        )
        shares = call(
            pair_kernel,
            share_shapes(16),
            pltpu.PrefetchScalarGridSpec(
                num_scalar_prefetch=1,
                grid=(SUBS, 2),
                in_specs=[
                    pl.BlockSpec((1, G, K, L), lambda p, h, m: (p, 0, 0, 0)),
                    pl.BlockSpec((1, 1, 3 * L), lambda p, h, m: (p, 0, h)),
                    a_spec(0),
                    a_spec(1),
                ],
                out_specs=share_specs(2, lambda p, h, m: (2 * p + h, 0, 0)),
                scratch_shapes=[pltpu.VMEM((2, K, K), f32)],
            ),
            5 * 10**9,
            5 << 20,
        )(meta, blocks[o], back_idx[o], own_rows, own_rows)
        pieces += row_exchange(shares)

    pairs, selfs = call(
        functools.partial(final_kernel, 7),
        [
            jax.ShapeDtypeStruct((SUBS, NB, SHARE, K), f32),
            jax.ShapeDtypeStruct((SUBS, SHARE, K), f32),
        ],
        pltpu.PrefetchScalarGridSpec(
            num_scalar_prefetch=1,
            grid=(),
            in_specs=[pl.BlockSpec(memory_space=pltpu.VMEM)] * 32,
            out_specs=[pl.BlockSpec(memory_space=pltpu.VMEM)] * 2,
            scratch_shapes=[pltpu.VMEM((112, SHARE, K), f32)],
        ),
        10**7,
        4 << 20,
    )(table, *pieces, *row_exchange(self_shares))
    return pairs.reshape(SUBS, NB, SHARE * K), selfs.reshape(SUBS, SHARE * K)


def solution(mesh):
    return jax.shard_map(
        on_device,
        mesh=mesh,
        in_specs=(
            P("sub", None, None, None, "row", None),
            P("sub", None, "row", None),
            P("sub", None, None, "row", None),
            P(),
            P("sub", None),
            P("sub", None, "row"),
        ),
        out_specs=(P("sub", None, "row"), P("sub", "row")),
        check_vma=False,
    )
```

time: 1380 us -> 219 us (0.16)
  local copies, waits for them, and re-layouts: 845 us -> 51.5 us
  other arithmetic: 314 us -> 6.03 us
  waiting for transfers between devices: 103 us -> 1.71 us
  Pallas kernels: 0 us -> 92.9 us
  matrix products: 78.5 us -> 0.9 us
  starting transfers between devices: 16.8 us -> 61.9 us
  between operations: 15.2 us -> 1.24 us
    gather x5 -> x0, local copies, waits for them, and re-layouts: 791 us -> none  [select_rows(): return row_major[index_rows]]
    add x34 -> x5, other arithmetic: 203 us -> 3.21 us  [the longest x1 1.68 us: on_device(): idx = high * L + low]
    convert_element_type x4 -> x0, other arithmetic: 96 us -> none  [the longest x3 60.4 us: apply_operator(): shifted = padded[:, :, 1 + shift_x:1 + shift_x + size_x, 1 + shift_y:1 +...]
    pallas_call x0 -> x10, Pallas kernels: none -> 92.9 us  [the longest x7 53.4 us: on_device(): call(pair_kernel, share_shapes(16), pltpu.PrefetchScalarGridSpec(num_scal...]
    psum x1 -> x0, waiting for transfers between devices: 86.4 us -> none  [on_device(): summed_pairs, summed_self = lax.psum((pair_flat, self_flat), 'row')]
    dot_general x10 -> x1, matrix products: 78.5 us -> 0.9 us  [on_device(): jnp.einsum('jtn,jnm->jtm', mine, halves, preferred_element_type=f32)]
    ppermute x8 -> x38, starting transfers between devices: 16.7 us -> 61.9 us  [the longest x24 36 us: row_exchange(): lax.ppermute(shares[s], 'row', [(i, (i + s) % 4) for i in range(4)])]
    ppermute x8 -> x38, waiting for transfers between devices: 16.5 us -> 1.71 us  [the longest x24 0.99 us: row_exchange(): lax.ppermute(shares[s], 'row', [(i, (i + s) % 4) for i in range(4)])]
  transfers between devices with their start and end apart: 9 -> 38, of which waited for: 2 -> 3; matrix products, arithmetic and copies ran while one was open for 86% -> 12% of each run, Pallas kernels for 0% -> 42%
where the time goes in v1:
time: 219 us; the launch traced here: 216 us
  Pallas kernels  92.9 us (42%)
  starting transfers between devices  61.9 us (28%)
  local copies, waits for them, and re-layouts  51.5 us (24%)
  other arithmetic  6.03 us (3%)
    pallas_call x7, Pallas kernels, on_device(): call(pair_kernel, share_shapes(16), pltpu.PrefetchScalarGridSpec(num_scal...  53.4 us
    ppermute x24, starting transfers between devices, row_exchange(): lax.ppermute(shares[s], 'row', [(i, (i + s) % 4) for i in range(4)])  36 us
    pallas_call x1, Pallas kernels, on_device(): call(gather_kernel, jax.ShapeDtypeStruct((SUBS, K, NB * OV), bf16), pl.Gr...  28.6 us
    unnamed x130, local copies, waits for them, and re-layouts  27 us
    ppermute x4, starting transfers between devices, on_device(): lax.ppermute(x, 'sub', [(i, (i + by) % n_sub) for i in range(n_sub)])  12 us
    pallas_call x1, Pallas kernels, on_device(): call(stencil_kernel, [jax.ShapeDtypeStruct((SUBS, G, K, L), bf16)] + shar...  9.62 us
    transpose x2, local copies, waits for them, and re-layouts, on_device(): vt = jnp.transpose(deflation, (0, 2, 4, 1, 3, 5)).reshape(SUBS, G, K, L)  5.53 us
    ppermute x1, starting transfers between devices, on_device(): below = lax.ppermute(planes[:, :, 1], 'row', [(i, i + 1) for i in range(3)])  4.44 us
  transfers between devices with their start and end apart: 38, of which 3 were waited for; matrix products, arithmetic and copies ran while one was open for 12% of the time, Pallas kernels for 42%

profile of v1, /device:TPU:0, one launch (start us, length us, event | category | flops | bytes accessed | tf_op | source)
XLA Modules:
  0.0 216.2 jit_solution(12391338579138985813)
XLA Ops:
  0.6 2.2 %copy.16 = bf16[4,3,2,96,2,128]{5,4,3,2,1,0:T(2,128)(2,1)S(1)} copy(bf16[4,3,2,96,2,128]{5,2,4,1,3,0:T(2,128)(2,1)} %bitcast.40) | data formatting | bytes 2359296 | tf_op jit(solution)/shard_map/transpose | solution.py:160
  3.7 6.4 %collective-permute-start.10 = (bf16[4,6,96,256]{3,2,1,0:T(8,128)(2,1)S(1)}, bf16[4,6,96,256]{3,2,1,0:T(8,128)(2,1)S(1)}, u32[]{:S(2)}, u32[]{:S(2)}) collective-permute-start(bf16[4,6,96,256]{3,2,1,0:T(8,128)(2,1)S(1)} %reshape.392.v), channel_id=1, source_target_pairs={{0,120},{4,124},{8,0},{12,4},{16,8},{20,12},{24,16},{28,20},{32,24... | collective-permute-start | bytes 3538952 | tf_op jit(solution)/shard_map/ppermute | solution.py:162
  10.1 3.3 %copy.22 = bf16[4,3,2,96,2,128]{5,4,3,1,0,2:T(2,128)(2,1)} copy(bf16[4,3,2,96,2,128]{5,2,4,1,3,0:T(2,128)(2,1)} %bitcast.41) | data formatting | bytes 2359296 | tf_op jit(solution)/shard_map/transpose | solution.py:160
  13.4 3.9 %reshape_reshape.3 = bf16[4,3,2,96,256]{4,3,1,0,2:T(8,128)(2,1)} reshape(bf16[4,3,2,96,2,128]{5,4,3,1,0,2:T(2,128)(2,1)} %copy.22) | data formatting | bytes 2359296 | tf_op jit(solution)/shard_map/reshape;reshape | solution.py:165
  17.2 2.3 %slice_bitcast_fusion = (bf16[4,3,96,256]{3,2,1,0:T(8,128)(2,1)}, bf16[4,3,96,256]{3,2,1,0:T(8,128)(2,1)}) fusion(bf16[4,3,2,96,256]{4,3,1,0,2:T(8,128)(2,1)} %reshape_reshape.3), kind=kLoop, calls=%fused_computation.2 | loop fusion | bytes 2359296 | tf_op jit(solution)/shard_map/squeeze | solution.py:167
  19.6 4.4 %collective-permute-start = (bf16[4,3,96,256]{3,2,1,0:T(8,128)(2,1)}, bf16[4,3,96,256]{3,2,1,0:T(8,128)(2,1)}, u32[]{:S(2)}, u32[]{:S(2)}) collective-permute-start(bf16[4,3,96,256]{3,2,1,0:T(8,128)(2,1)} %get-tuple-element.77), channel_id=1, source_target_pairs={{0,1},{1,2},{2,3},{4,5},{5,6},{6,7},{8,9},{9,10},{10,11},{12,13},{... | collective-permute-start | bytes 1769480 | tf_op jit(solution)/shard_map/ppermute | solution.py:166
  43.4 3.2 %collective-permute-start.21 = (s32[4,1,1536]{2,1,0:T(1,128)S(1)}, s32[4,1,1536]{2,1,0:T(1,128)S(1)}, u32[]{:S(2)}, u32[]{:S(2)}) collective-permute-start(s32[4,1,1536]{2,1,0:T(1,128)S(1)} %get-tuple-element.80), channel_id=1, source_target_pairs={{0,124},{4,120},{8,4},{12,0},{16,12},{20,8},{24,20},{28,16},{32,28... | collective-permute-start | bytes 73736 | tf_op jit(solution)/shard_map/ppermute | solution.py:202
  48.2 9.6 %shard_map.77 = (bf16[4,6,96,256]{3,2,1,0:T(8,128)(2,1)S(1)}, f32[4,24,96]{2,1,0:T(8,128)S(1)}, bf16[4,24,96]{2,1,0:T(8,128)(2,1)S(1)}, bf16[4,24,96]{2,1,0:T(8,128)(2,1)S(1)}, bf16[4,24,96]{2,1,0:T(8,128)(2,1)S(1)}) custom-call(s32[1]{0:T(128)} %bitcast.7.meta, f32[26,9]{1,0:T(8,128)S(1)} %copy.23.coup, bf16[4,6,96,256]{3,2,1,0:T(8,128)(2,1)S(1)} %reshape.392.v, ...), custom_call_target="tpu_custom_call" | custom-call | flops 7247757312 | bytes 8388608 | tf_op jit(solution)/shard_map/pallas_call | solution.py:213
  57.9 28.6 %shard_map.78.a0.a1 = bf16[4,96,9984]{2,1,0:T(8,128)(2,1)} custom-call(bf16[4,6,96,256]{3,2,1,0:T(8,128)(2,1)S(1)} %get-tuple-element.37.a, s32[4,1,9984]{2,1,0:T(1,128)S(1)} %copy-done.10), custom_call_target="tpu_custom_call" | custom-call | flops 24999999488 | bytes 16777216 | tf_op jit(solution)/shard_map/pallas_call | solution.py:235
  86.5 7.6 %shard_map.79 = (f32[16,24,96]{2,1,0:T(8,128)S(1)}, bf16[16,24,96]{2,1,0:T(8,128)(2,1)S(1)}, bf16[16,24,96]{2,1,0:T(8,128)(2,1)S(1)}, bf16[16,24,96]{2,1,0:T(8,128)(2,1)S(1)}) custom-call(s32[113]{0:T(128)S(1)} %pad_add_fusion.meta, bf16[4,6,96,256]{3,2,1,0:T(8,128)(2,1)S(1)} %reshape.392.v, s32[4,1,1536]{2,1,0:T(1,128)S(1)} %get-tuple-element.84.idx, ...), custom_call_target="tpu_custom_call" | custom-call | flops 5000000000 | bytes 5242880 | tf_op jit(solution)/shard_map/pallas_call | solution.py:256
  94.2 2.5 %collective-permute-start.16 = (s32[4,1,1536]{2,1,0:T(1,128)S(1)}, s32[4,1,1536]{2,1,0:T(1,128)S(1)}, u32[]{:S(2)}, u32[]{:S(2)}) collective-permute-start(s32[4,1,1536]{2,1,0:T(1,128)S(1)} %get-tuple-element.81), channel_id=1, source_target_pairs={{0,8},{4,12},{8,16},{12,20},{16,24},{20,28},{24,32},{28,36},{32,40... | collective-permute-start | bytes 73736 | tf_op jit(solution)/shard_map/ppermute | solution.py:162
  96.7 3.1 %collective-permute-start.11 = (s32[4,1,1536]{2,1,0:T(1,128)S(1)}, s32[4,1,1536]{2,1,0:T(1,128)S(1)}, u32[]{:S(2)}, u32[]{:S(2)}) collective-permute-start(s32[4,1,1536]{2,1,0:T(1,128)S(1)} %get-tuple-element.82), channel_id=1, source_target_pairs={{0,120},{4,124},{8,0},{12,4},{16,8},{20,12},{24,16},{28,20},{32,24... | collective-permute-start | bytes 73736 | tf_op jit(solution)/shard_map/ppermute | solution.py:162
  100.7 2.4 %collective-permute-start.35 = (bf16[4,24,96]{2,1,0:T(8,128)(2,1)S(1)}, bf16[4,24,96]{2,1,0:T(8,128)(2,1)S(1)}, u32[]{:S(2)}, u32[]{:S(2)}) collective-permute-start(bf16[4,24,96]{2,1,0:T(8,128)(2,1)S(1)} %get-tuple-element.67), channel_id=1, source_target_pairs={{0,1},{1,2},{2,3},{3,0},{4,5},{5,6},{6,7},{7,4},{8,9},{9,10},{10,1... | collective-permute-start | bytes 55304 | tf_op jit(solution)/shard_map/ppermute | solution.py:152
  103.1 2.9 %collective-permute-start.36 = (bf16[4,24,96]{2,1,0:T(8,128)(2,1)S(1)}, bf16[4,24,96]{2,1,0:T(8,128)(2,1)S(1)}, u32[]{:S(2)}, u32[]{:S(2)}) collective-permute-start(bf16[4,24,96]{2,1,0:T(8,128)(2,1)S(1)} %get-tuple-element.68), channel_id=1, source_target_pairs={{0,2},{1,3},{2,0},{3,1},{4,6},{5,7},{6,4},{7,5},{8,10},{9,11},{10,... | collective-permute-start | bytes 55304 | tf_op jit(solution)/shard_map/ppermute | solution.py:152
  106.8 2.5 %collective-permute-start.30 = (bf16[4,6,96,256]{3,2,1,0:T(8,128)(2,1)S(1)}, bf16[4,6,96,256]{3,2,1,0:T(8,128)(2,1)S(1)}, u32[]{:S(2)}, u32[]{:S(2)}) collective-permute-start(bf16[4,6,96,256]{3,2,1,0:T(8,128)(2,1)S(1)} %broadcast_select_fusion), channel_id=1, source_target_pairs={{0,124},{4,8},{8,4},{12,16},{16,12},{20,24},{24,20},{28,32},{32,28... | collective-permute-start | bytes 3538952 | tf_op jit(solution)/shard_map/ppermute | solution.py:171
  109.3 7.6 %shard_map.82 = (f32[16,24,96]{2,1,0:T(8,128)S(1)}, bf16[16,24,96]{2,1,0:T(8,128)(2,1)S(1)}, bf16[16,24,96]{2,1,0:T(8,128)(2,1)S(1)}, bf16[16,24,96]{2,1,0:T(8,128)(2,1)S(1)}) custom-call(s32[113]{0:T(128)S(1)} %pad_add_fusion.meta, bf16[4,6,96,256]{3,2,1,0:T(8,128)(2,1)S(1)} %collective-permute-done.15.v, s32[4,1,1536]{2,1,0:T(1,128)S(1)} %collective-permute-done.16.idx, ...), custom_call_target="tpu_custom_call" | custom-call | flops 5000000000 | bytes 5242880 | tf_op jit(solution)/shard_map/pallas_call | solution.py:256
  120.5 7.6 %shard_map.81 = (f32[16,24,96]{2,1,0:T(8,128)S(1)}, bf16[16,24,96]{2,1,0:T(8,128)(2,1)S(1)}, bf16[16,24,96]{2,1,0:T(8,128)(2,1)S(1)}, bf16[16,24,96]{2,1,0:T(8,128)(2,1)S(1)}) custom-call(s32[113]{0:T(128)S(1)} %pad_add_fusion.meta, bf16[4,6,96,256]{3,2,1,0:T(8,128)(2,1)S(1)} %collective-permute-done.10.v, s32[4,1,1536]{2,1,0:T(1,128)S(1)} %collective-permute-done.11.idx, ...), custom_call_target="tpu_custom_call" | custom-call | flops 5000000000 | bytes 5242880 | tf_op jit(solution)/shard_map/pallas_call | solution.py:256
  132.7 7.9 %shard_map.80 = (f32[16,24,96]{2,1,0:T(8,128)S(1)}, bf16[16,24,96]{2,1,0:T(8,128)(2,1)S(1)}, bf16[16,24,96]{2,1,0:T(8,128)(2,1)S(1)}, bf16[16,24,96]{2,1,0:T(8,128)(2,1)S(1)}) custom-call(s32[113]{0:T(128)S(1)} %pad_add_fusion.meta, bf16[4,6,96,256]{3,2,1,0:T(8,128)(2,1)} %collective-permute-done.5.v, s32[4,1,1536]{2,1,0:T(1,128)S(1)} %collective-permute-done.6.idx, ...), custom_call_target="tpu_custom_call" | custom-call | flops 5000000000 | bytes 5242880 | tf_op jit(solution)/shard_map/pallas_call | solution.py:256
  143.4 2.4 %collective-permute-start.19 = (bf16[16,24,96]{2,1,0:T(8,128)(2,1)S(1)}, bf16[16,24,96]{2,1,0:T(8,128)(2,1)S(1)}, u32[]{:S(2)}, u32[]{:S(2)}) collective-permute-start(bf16[16,24,96]{2,1,0:T(8,128)(2,1)S(1)} %get-tuple-element.53), channel_id=1, source_target_pairs={{0,3},{1,0},{2,1},{3,2},{4,7},{5,4},{6,5},{7,6},{8,11},{9,8},{10,9... | collective-permute-start | bytes 221192 | tf_op jit(solution)/shard_map/ppermute | solution.py:152
  145.8 7.6 %shard_map.85 = (f32[16,24,96]{2,1,0:T(8,128)S(1)}, bf16[16,24,96]{2,1,0:T(8,128)(2,1)S(1)}, bf16[16,24,96]{2,1,0:T(8,128)(2,1)S(1)}, bf16[16,24,96]{2,1,0:T(8,128)(2,1)S(1)}) custom-call(s32[113]{0:T(128)S(1)} %pad_add_fusion.meta, bf16[4,6,96,256]{3,2,1,0:T(8,128)(2,1)S(1)} %collective-permute-done.30.v, s32[4,1,1536]{2,1,0:T(1,128)S(1)} %collective-permute-done.31.idx, ...), custom_call_target="tpu_custom_call" | custom-call | flops 5000000000 | bytes 5242880 | tf_op jit(solution)/shard_map/pallas_call | solution.py:256
  160.4 7.6 %shard_map.83 = (f32[16,24,96]{2,1,0:T(8,128)S(1)}, bf16[16,24,96]{2,1,0:T(8,128)(2,1)S(1)}, bf16[16,24,96]{2,1,0:T(8,128)(2,1)S(1)}, bf16[16,24,96]{2,1,0:T(8,128)(2,1)S(1)}) custom-call(s32[113]{0:T(128)S(1)} %pad_add_fusion.meta, bf16[4,6,96,256]{3,2,1,0:T(8,128)(2,1)S(1)} %collective-permute-done.20.v, s32[4,1,1536]{2,1,0:T(1,128)S(1)} %collective-permute-done.21.idx, ...), custom_call_target="tpu_custom_call" | custom-call | flops 5000000000 | bytes 5242880 | tf_op jit(solution)/shard_map/pallas_call | solution.py:256
  168.0 2.6 %collective-permute-start.9 = (bf16[16,24,96]{2,1,0:T(8,128)(2,1)S(1)}, bf16[16,24,96]{2,1,0:T(8,128)(2,1)S(1)}, u32[]{:S(2)}, u32[]{:S(2)}) collective-permute-start(bf16[16,24,96]{2,1,0:T(8,128)(2,1)S(1)} %get-tuple-element.45), channel_id=1, source_target_pairs={{0,3},{1,0},{2,1},{3,2},{4,7},{5,4},{6,5},{7,6},{8,11},{9,8},{10,9... | collective-permute-start | bytes 221192 | tf_op jit(solution)/shard_map/ppermute | solution.py:152
  175.0 7.6 %shard_map.84 = (f32[16,24,96]{2,1,0:T(8,128)S(1)}, bf16[16,24,96]{2,1,0:T(8,128)(2,1)S(1)}, bf16[16,24,96]{2,1,0:T(8,128)(2,1)S(1)}, bf16[16,24,96]{2,1,0:T(8,128)(2,1)S(1)}) custom-call(s32[113]{0:T(128)S(1)} %pad_add_fusion.meta, bf16[4,6,96,256]{3,2,1,0:T(8,128)(2,1)S(1)} %collective-permute-done.25.v, s32[4,1,1536]{2,1,0:T(1,128)S(1)} %collective-permute-done.26.idx, ...), custom_call_target="tpu_custom_call" | custom-call | flops 5000000000 | bytes 5242880 | tf_op jit(solution)/shard_map/pallas_call | solution.py:256
  185.4 2.6 %collective-permute-start.24 = (bf16[16,24,96]{2,1,0:T(8,128)(2,1)S(1)}, bf16[16,24,96]{2,1,0:T(8,128)(2,1)S(1)}, u32[]{:S(2)}, u32[]{:S(2)}) collective-permute-start(bf16[16,24,96]{2,1,0:T(8,128)(2,1)S(1)} %get-tuple-element.57), channel_id=1, source_target_pairs={{0,3},{1,0},{2,1},{3,2},{4,7},{5,4},{6,5},{7,6},{8,11},{9,8},{10,9... | collective-permute-start | bytes 221192 | tf_op jit(solution)/shard_map/ppermute | solution.py:152
  (224 shorter events, 76.7 us)
Async XLA Ops:
  3.7 93.0 %collective-permute-start.10 = (bf16[4,6,96,256]{3,2,1,0:T(8,128)(2,1)S(1)}, bf16[4,6,96,256]{3,2,1,0:T(8,128)(2,1)S(1)}, u32[]{:S(2)}, u32[]{:S(2)}) collective-permute-start(bf16[4,6,96,256]{3,2,1,0:T(8,128)(2,1)S(1)} %reshape.392.v), channel_id=1, source_target_pairs={{0,120},{4,124},{8,0},{12,4},{16,8},{20,12},{24,16},{28,20},{32,24... | collective-permute-start | bytes 3538952 | tf_op jit(solution)/shard_map/ppermute | solution.py:162
  10.0 89.7 %collective-permute-start.15 = (bf16[4,6,96,256]{3,2,1,0:T(8,128)(2,1)S(1)}, bf16[4,6,96,256]{3,2,1,0:T(8,128)(2,1)S(1)}, u32[]{:S(2)}, u32[]{:S(2)}) collective-permute-start(bf16[4,6,96,256]{3,2,1,0:T(8,128)(2,1)S(1)} %reshape.392.v), channel_id=1, source_target_pairs={{0,8},{4,12},{8,16},{12,20},{16,24},{20,28},{24,32},{28,36},{32,40... | collective-permute-start | bytes 3538952 | tf_op jit(solution)/shard_map/ppermute | solution.py:162
  10.1 122.4 %collective-permute-start.5 = (bf16[4,6,96,256]{3,2,1,0:T(8,128)(2,1)S(1)}, bf16[4,6,96,256]{3,2,1,0:T(8,128)(2,1)}, u32[]{:S(2)}, u32[]{:S(2)}) collective-permute-start(bf16[4,6,96,256]{3,2,1,0:T(8,128)(2,1)S(1)} %reshape.392.v), channel_id=1, source_target_pairs={{0,4},{4,0},{8,12},{12,8},{16,20},{20,16},{24,28},{28,24},{32,36},... | collective-permute-start | bytes 3538952 | tf_op jit(solution)/shard_map/ppermute | solution.py:163
  19.6 21.6 %collective-permute-start = (bf16[4,3,96,256]{3,2,1,0:T(8,128)(2,1)}, bf16[4,3,96,256]{3,2,1,0:T(8,128)(2,1)}, u32[]{:S(2)}, u32[]{:S(2)}) collective-permute-start(bf16[4,3,96,256]{3,2,1,0:T(8,128)(2,1)} %get-tuple-element.77), channel_id=1, source_target_pairs={{0,1},{1,2},{2,3},{4,5},{5,6},{6,7},{8,9},{9,10},{10,11},{12,13},{... | collective-permute-start | bytes 1769480 | tf_op jit(solution)/shard_map/ppermute | solution.py:166
  24.0 19.4 %collective-permute-start.1 = (bf16[4,3,96,256]{3,2,1,0:T(8,128)(2,1)}, bf16[4,3,96,256]{3,2,1,0:T(8,128)(2,1)}, u32[]{:S(2)}, u32[]{:S(2)}) collective-permute-start(bf16[4,3,96,256]{3,2,1,0:T(8,128)(2,1)} %get-tuple-element.76), channel_id=1, source_target_pairs={{1,0},{2,1},{3,2},{5,4},{6,5},{7,6},{9,8},{10,9},{11,10},{13,12},{... | collective-permute-start | bytes 1769480 | tf_op jit(solution)/shard_map/ppermute | solution.py:167
  41.2 52.9 %collective-permute-start.31 = (s32[4,1,1536]{2,1,0:T(1,128)S(1)}, s32[4,1,1536]{2,1,0:T(1,128)S(1)}, u32[]{:S(2)}, u32[]{:S(2)}) collective-permute-start(s32[4,1,1536]{2,1,0:T(1,128)S(1)} %get-tuple-element.78), channel_id=1, source_target_pairs={{0,116},{4,16},{8,124},{12,24},{16,4},{20,32},{24,12},{28,40},{32,... | collective-permute-start | bytes 73736 | tf_op jit(solution)/shard_map/ppermute | solution.py:204
  43.4 50.7 %collective-permute-start.21 = (s32[4,1,1536]{2,1,0:T(1,128)S(1)}, s32[4,1,1536]{2,1,0:T(1,128)S(1)}, u32[]{:S(2)}, u32[]{:S(2)}) collective-permute-start(s32[4,1,1536]{2,1,0:T(1,128)S(1)} %get-tuple-element.80), channel_id=1, source_target_pairs={{0,124},{4,120},{8,4},{12,0},{16,12},{20,8},{24,20},{28,16},{32,28... | collective-permute-start | bytes 73736 | tf_op jit(solution)/shard_map/ppermute | solution.py:202
  100.7 16.8 %collective-permute-start.35 = (bf16[4,24,96]{2,1,0:T(8,128)(2,1)S(1)}, bf16[4,24,96]{2,1,0:T(8,128)(2,1)S(1)}, u32[]{:S(2)}, u32[]{:S(2)}) collective-permute-start(bf16[4,24,96]{2,1,0:T(8,128)(2,1)S(1)} %get-tuple-element.67), channel_id=1, source_target_pairs={{0,1},{1,2},{2,3},{3,0},{4,5},{5,6},{6,7},{7,4},{8,9},{9,10},{10,1... | collective-permute-start | bytes 55304 | tf_op jit(solution)/shard_map/ppermute | solution.py:152
  103.1 15.1 %collective-permute-start.36 = (bf16[4,24,96]{2,1,0:T(8,128)(2,1)S(1)}, bf16[4,24,96]{2,1,0:T(8,128)(2,1)S(1)}, u32[]{:S(2)}, u32[]{:S(2)}) collective-permute-start(bf16[4,24,96]{2,1,0:T(8,128)(2,1)S(1)} %get-tuple-element.68), channel_id=1, source_target_pairs={{0,2},{1,3},{2,0},{3,1},{4,6},{5,7},{6,4},{7,5},{8,10},{9,11},{10,... | collective-permute-start | bytes 55304 | tf_op jit(solution)/shard_map/ppermute | solution.py:152
  106.0 14.6 %collective-permute-start.37 = (bf16[4,24,96]{2,1,0:T(8,128)(2,1)S(1)}, bf16[4,24,96]{2,1,0:T(8,128)(2,1)S(1)}, u32[]{:S(2)}, u32[]{:S(2)}) collective-permute-start(bf16[4,24,96]{2,1,0:T(8,128)(2,1)S(1)} %get-tuple-element.69), channel_id=1, source_target_pairs={{0,3},{1,0},{2,1},{3,2},{4,7},{5,4},{6,5},{7,6},{8,11},{9,8},{10,9... | collective-permute-start | bytes 55304 | tf_op jit(solution)/shard_map/ppermute | solution.py:152
  106.8 39.0 %collective-permute-start.30 = (bf16[4,6,96,256]{3,2,1,0:T(8,128)(2,1)S(1)}, bf16[4,6,96,256]{3,2,1,0:T(8,128)(2,1)S(1)}, u32[]{:S(2)}, u32[]{:S(2)}) collective-permute-start(bf16[4,6,96,256]{3,2,1,0:T(8,128)(2,1)S(1)} %broadcast_select_fusion), channel_id=1, source_target_pairs={{0,124},{4,8},{8,4},{12,16},{16,12},{20,24},{24,20},{28,32},{32,28... | collective-permute-start | bytes 3538952 | tf_op jit(solution)/shard_map/ppermute | solution.py:171
  118.8 12.5 %collective-permute-start.3 = (bf16[16,24,96]{2,1,0:T(8,128)(2,1)S(1)}, bf16[16,24,96]{2,1,0:T(8,128)(2,1)S(1)}, u32[]{:S(2)}, u32[]{:S(2)}) collective-permute-start(bf16[16,24,96]{2,1,0:T(8,128)(2,1)S(1)} %get-tuple-element.40), channel_id=1, source_target_pairs={{0,2},{1,3},{2,0},{3,1},{4,6},{5,7},{6,4},{7,5},{8,10},{9,11},{10,... | collective-permute-start | bytes 221192 | tf_op jit(solution)/shard_map/ppermute | solution.py:152
  120.5 37.8 %collective-permute-start.20 = (bf16[4,6,96,256]{3,2,1,0:T(8,128)(2,1)S(1)}, bf16[4,6,96,256]{3,2,1,0:T(8,128)(2,1)S(1)}, u32[]{:S(2)}, u32[]{:S(2)}) collective-permute-start(bf16[4,6,96,256]{3,2,1,0:T(8,128)(2,1)S(1)} %collective-permute-done.10.v), channel_id=1, source_target_pairs={{0,4},{4,0},{8,12},{12,8},{16,20},{20,16},{24,28},{28,24},{32,36},... | collective-permute-start | bytes 3538952 | tf_op jit(solution)/shard_map/ppermute | solution.py:163
  132.5 41.7 %collective-permute-start.25 = (bf16[4,6,96,256]{3,2,1,0:T(8,128)(2,1)S(1)}, bf16[4,6,96,256]{3,2,1,0:T(8,128)(2,1)S(1)}, u32[]{:S(2)}, u32[]{:S(2)}) collective-permute-start(bf16[4,6,96,256]{3,2,1,0:T(8,128)(2,1)S(1)} %collective-permute-done.15.v), channel_id=1, source_target_pairs={{0,4},{4,0},{8,12},{12,8},{16,20},{20,16},{24,28},{28,24},{32,36},... | collective-permute-start | bytes 3538952 | tf_op jit(solution)/shard_map/ppermute | solution.py:163
  141.3 12.8 %collective-permute-start.18 = (bf16[16,24,96]{2,1,0:T(8,128)(2,1)S(1)}, bf16[16,24,96]{2,1,0:T(8,128)(2,1)S(1)}, u32[]{:S(2)}, u32[]{:S(2)}) collective-permute-start(bf16[16,24,96]{2,1,0:T(8,128)(2,1)S(1)} %get-tuple-element.52), channel_id=1, source_target_pairs={{0,2},{1,3},{2,0},{3,1},{4,6},{5,7},{6,4},{7,5},{8,10},{9,11},{10,... | collective-permute-start | bytes 221192 | tf_op jit(solution)/shard_map/ppermute | solution.py:152
  154.1 13.9 %collective-permute-start.13 = (bf16[16,24,96]{2,1,0:T(8,128)(2,1)S(1)}, bf16[16,24,96]{2,1,0:T(8,128)(2,1)S(1)}, u32[]{:S(2)}, u32[]{:S(2)}) collective-permute-start(bf16[16,24,96]{2,1,0:T(8,128)(2,1)S(1)} %get-tuple-element.48), channel_id=1, source_target_pairs={{0,2},{1,3},{2,0},{3,1},{4,6},{5,7},{6,4},{7,5},{8,10},{9,11},{10,... | collective-permute-start | bytes 221192 | tf_op jit(solution)/shard_map/ppermute | solution.py:152
  155.7 15.0 %collective-permute-start.14 = (bf16[16,24,96]{2,1,0:T(8,128)(2,1)S(1)}, bf16[16,24,96]{2,1,0:T(8,128)(2,1)S(1)}, u32[]{:S(2)}, u32[]{:S(2)}) collective-permute-start(bf16[16,24,96]{2,1,0:T(8,128)(2,1)S(1)} %get-tuple-element.49), channel_id=1, source_target_pairs={{0,3},{1,0},{2,1},{3,2},{4,7},{5,4},{6,5},{7,6},{8,11},{9,8},{10,9... | collective-permute-start | bytes 221192 | tf_op jit(solution)/shard_map/ppermute | solution.py:152
  157.6 13.0 %collective-permute-start.7 = (bf16[16,24,96]{2,1,0:T(8,128)(2,1)S(1)}, bf16[16,24,96]{2,1,0:T(8,128)(2,1)S(1)}, u32[]{:S(2)}, u32[]{:S(2)}) collective-permute-start(bf16[16,24,96]{2,1,0:T(8,128)(2,1)S(1)} %get-tuple-element.43), channel_id=1, source_target_pairs={{0,1},{1,2},{2,3},{3,0},{4,5},{5,6},{6,7},{7,4},{8,9},{9,10},{10,1... | collective-permute-start | bytes 221192 | tf_op jit(solution)/shard_map/ppermute | solution.py:152
  158.3 13.9 %collective-permute-start.8 = (bf16[16,24,96]{2,1,0:T(8,128)(2,1)S(1)}, bf16[16,24,96]{2,1,0:T(8,128)(2,1)S(1)}, u32[]{:S(2)}, u32[]{:S(2)}) collective-permute-start(bf16[16,24,96]{2,1,0:T(8,128)(2,1)S(1)} %get-tuple-element.44), channel_id=1, source_target_pairs={{0,2},{1,3},{2,0},{3,1},{4,6},{5,7},{6,4},{7,5},{8,10},{9,11},{10,... | collective-permute-start | bytes 221192 | tf_op jit(solution)/shard_map/ppermute | solution.py:152
  168.0 14.6 %collective-permute-start.9 = (bf16[16,24,96]{2,1,0:T(8,128)(2,1)S(1)}, bf16[16,24,96]{2,1,0:T(8,128)(2,1)S(1)}, u32[]{:S(2)}, u32[]{:S(2)}) collective-permute-start(bf16[16,24,96]{2,1,0:T(8,128)(2,1)S(1)} %get-tuple-element.45), channel_id=1, source_target_pairs={{0,3},{1,0},{2,1},{3,2},{4,7},{5,4},{6,5},{7,6},{8,11},{9,8},{10,9... | collective-permute-start | bytes 221192 | tf_op jit(solution)/shard_map/ppermute | solution.py:152
  170.6 14.1 %collective-permute-start.32 = (bf16[16,24,96]{2,1,0:T(8,128)(2,1)S(1)}, bf16[16,24,96]{2,1,0:T(8,128)(2,1)S(1)}, u32[]{:S(2)}, u32[]{:S(2)}) collective-permute-start(bf16[16,24,96]{2,1,0:T(8,128)(2,1)S(1)} %get-tuple-element.63), channel_id=1, source_target_pairs={{0,1},{1,2},{2,3},{3,0},{4,5},{5,6},{6,7},{7,4},{8,9},{9,10},{10,1... | collective-permute-start | bytes 221192 | tf_op jit(solution)/shard_map/ppermute | solution.py:152
  170.7 17.3 %collective-permute-start.33 = (bf16[16,24,96]{2,1,0:T(8,128)(2,1)S(1)}, bf16[16,24,96]{2,1,0:T(8,128)(2,1)S(1)}, u32[]{:S(2)}, u32[]{:S(2)}) collective-permute-start(bf16[16,24,96]{2,1,0:T(8,128)(2,1)S(1)} %get-tuple-element.64), channel_id=1, source_target_pairs={{0,2},{1,3},{2,0},{3,1},{4,6},{5,7},{6,4},{7,5},{8,10},{9,11},{10,... | collective-permute-start | bytes 221192 | tf_op jit(solution)/shard_map/ppermute | solution.py:152
  172.2 16.4 %collective-permute-start.34 = (bf16[16,24,96]{2,1,0:T(8,128)(2,1)S(1)}, bf16[16,24,96]{2,1,0:T(8,128)(2,1)S(1)}, u32[]{:S(2)}, u32[]{:S(2)}) collective-permute-start(bf16[16,24,96]{2,1,0:T(8,128)(2,1)S(1)} %get-tuple-element.65), channel_id=1, source_target_pairs={{0,3},{1,0},{2,1},{3,2},{4,7},{5,4},{6,5},{7,6},{8,11},{9,8},{10,9... | collective-permute-start | bytes 221192 | tf_op jit(solution)/shard_map/ppermute | solution.py:152
  174.3 16.5 %collective-permute-start.22 = (bf16[16,24,96]{2,1,0:T(8,128)(2,1)S(1)}, bf16[16,24,96]{2,1,0:T(8,128)(2,1)S(1)}, u32[]{:S(2)}, u32[]{:S(2)}) collective-permute-start(bf16[16,24,96]{2,1,0:T(8,128)(2,1)S(1)} %get-tuple-element.55), channel_id=1, source_target_pairs={{0,1},{1,2},{2,3},{3,0},{4,5},{5,6},{6,7},{7,4},{8,9},{9,10},{10,1... | collective-permute-start | bytes 221192 | tf_op jit(solution)/shard_map/ppermute | solution.py:152
  (79 other events, 641.9 us)

commit v2 on v0

v2 whole, which is shorter than its diff:
```python
import functools

import jax
import jax.numpy as jnp
from jax import lax
from jax.experimental import pallas as pl
from jax.experimental.pallas import tpu as pltpu
from jax.sharding import PartitionSpec as P

f32, bf16, i32, i16 = jnp.float32, jnp.bfloat16, jnp.int32, jnp.int16
K, SUBS, NB, OV, ROWS = 96, 4, 26, 384, 1536
G, L = 6, 256
SHARE = K * K // 4
TILES = 13
VMEM = 28 << 20

SOURCE_EVEN = (0, 1, 2, -2, 3, -1, -3)
TARGET_EVEN = (0, 1, -2, 2, -1, 3, -3)
SOURCE_ODD = (0, -1, 2, -2, 1, -3, 3)
TARGET_ODD = (0, -1, -2, 2, -3, 1, 3)
CHUNKS = (64, 32, 16)


def call(kernel, out_shape, grid_spec, flops, moved, aliases={}):
    return pl.pallas_call(
        kernel,
        out_shape=out_shape,
        grid_spec=grid_spec,
        input_output_aliases=aliases,
        compiler_params=pltpu.CompilerParams(vmem_limit_bytes=VMEM),
        cost_estimate=pl.CostEstimate(flops=flops, bytes_accessed=moved, transcendentals=0),
    )


def nt_dot(a, b):
    return lax.dot_general(a, b, (((1,), (1,)), ((), ())), preferred_element_type=f32)


def put_shares(blocks, flat, outs):
    n = blocks.shape[0]
    lane = lax.broadcasted_iota(i32, (n, 128), 1)
    for a in range(K // 4):
        x0, x1, x2, x3 = (blocks[:, 4 * a + i, :] for i in range(4))
        x1, x2, x3 = pltpu.roll(x1, 96, 1), pltpu.roll(x2, 64, 1), pltpu.roll(x3, 32, 1)
        flat[:, 384 * a : 384 * a + 128] = jnp.where(lane < 96, x0, x1)
        flat[:, 384 * a + 128 : 384 * a + 256] = jnp.where(lane < 64, x1, x2)
        flat[:, 384 * a + 256 : 384 * a + 384] = jnp.where(lane < 32, x2, x3)
    row = lax.axis_index("row")
    for step in range(4):
        start = pl.multiple_of(lax.rem(row + step, 4) * SHARE, 128)
        outs[step][...] = flat[:, pl.ds(start, SHARE)].astype(outs[step].dtype)


def wide(ref, s, g):
    return jnp.concatenate([ref[s, 2 * g], ref[s, 2 * g + 1]], axis=1)


def offset_number(sx, sy, sz):
    flat = (sx + 1) * 9 + (sy + 1) * 3 + sz + 1
    return None if flat == 13 else flat - (flat > 13)


def band_tile(on_band, coup, stiff, c, b, y, sy):
    columns = []
    for x in range(2):
        parts = []
        for x_in in range(2):
            block = jnp.zeros((128, 128), bf16)
            for sz in (-1, 0, 1):
                o = offset_number(x_in - x, sy, sz)
                if o is None:
                    continue
                w = stiff[0, o, x, y : y + 1, :] * coup[o, c * 3 + b]
                block = jnp.where(
                    on_band[sz], jnp.broadcast_to(w.astype(bf16), (128, 128)), block
                )
            parts.append(block)
        columns.append(jnp.concatenate(parts, axis=0))
    return jnp.concatenate(columns, axis=1)


def bands():
    distance = (
        lax.broadcasted_iota(i32, (128, 128), 0) - lax.broadcasted_iota(i32, (128, 128), 1)
    ).astype(i16)
    return {sz: distance == sz for sz in (-1, 0, 1)}


def inner_kernel(coup, v, stiff, center, out):
    on_band = bands()

    def component(c, carry):
        for y in range(2):
            mid = wide(v, 0, 2 * c + y)
            diag = jnp.concatenate([center[0, x, y : y + 1, :] for x in range(2)], axis=1)
            total = diag * mid.astype(f32)
            for y_in in range(2):
                for b in range(3):
                    tile = band_tile(on_band, coup, stiff, c, b, y, y_in - y)
                    total -= jnp.dot(
                        wide(v, 0, 2 * b + y_in), tile, preferred_element_type=f32
                    )
            out[0, 2 * c + y] = total
        return carry

    lax.fori_loop(0, 3, component, 0)


def outer_kernel(coup, inner, below, above, stiff, out):
    on_band = bands()

    def component(c, carry):
        for y in range(2):
            total = inner[0, 2 * c + y]
            for b in range(3):
                lhs = wide(above, 0, b) if y else wide(below, 0, b)
                tile = band_tile(on_band, coup, stiff, c, b, y, 2 * y - 1)
                total -= jnp.dot(lhs, tile, preferred_element_type=f32)
            out[0, 2 * c + y] = total.astype(bf16)
        return carry

    lax.fori_loop(0, 3, component, 0)


def gather_columns(stacked, high, low):
    tiles = []
    for t in range(high.shape[1] // L):
        part = high[:, t * L : t * L + L]
        hot = jnp.where(
            lax.broadcasted_iota(i16, (L, L), 0) == low[:, t * L : t * L + L].astype(i16),
            bf16(1),
            bf16(0),
        )
        found = jnp.dot(stacked, hot, preferred_element_type=f32)
        out = found[0:K]
        for g in range(1, G):
            out = jnp.where(part == g, found[g * K : g * K + K], out)
        tiles.append(out.astype(bf16))
    return jnp.concatenate(tiles, axis=1)


def stack_groups(v, s):
    return jnp.concatenate([wide(v, s, g) for g in range(G)], axis=0)


def coded(rows):
    h = rows >> 7
    e = jnp.where(h >= 6, h - 6, h)
    value = 1.0 + (rows & 127).astype(f32) * (1.0 / 128)
    for i in range(1, 6):
        value = jnp.where(e >= i, value * 2, value)
    return jnp.where(h >= 6, -value, value)


def decoded(value):
    size = jnp.abs(value)
    h = jnp.where(value < 0, 6, 0)
    for i in range(1, 6):
        more = size >= 2
        h += more.astype(i32)
        size = jnp.where(more, size * 0.5, size)
    return h * 128 + ((size - 1.0) * 128).astype(i32)


def lines(held, first, count):
    return jnp.concatenate([held[first + t : first + t + 1] for t in range(count)], axis=1)


def gather_sent(v, s, route):
    held = decoded(v[s, 12, 16 * (route - 1) : 16 * route, :].astype(f32))
    rows = lines(held, 0, 12)
    return gather_columns(stack_groups(v, s), rows >> 8, rows & 255)


def own_rows_kernel(s, a, idx, out):
    stacked = a[0].reshape(G * K, L)

    def two_slots(t, carry):
        rows = jnp.concatenate([idx[2 * t, s : s + 1, :], idx[2 * t + 1, s : s + 1, :]], axis=1)
        out[:, pl.ds(pl.multiple_of(t * 2 * OV, 128), 2 * OV)] = gather_columns(
            stacked, rows >> 8, rows & 255
        )
        return carry

    lax.fori_loop(0, NB // 2, two_slots, 0)


def early_kernel(v, v_other, back, out):
    p = pl.program_id(0)
    held = decoded(back[0])
    line = [lines(held, 3 * q, 3) for q in range(SUBS)]
    odd = p % 2 == 1
    swapped = [jnp.where(odd, line[a ^ 1], line[a]) for a in range(SUBS)]
    first = jnp.where(p < 2, swapped[1], swapped[3])
    second = jnp.where(p < 2, swapped[2], swapped[0])
    rows = jnp.concatenate([first, second], axis=1)
    out[0, :, : 2 * OV] = gather_columns(stack_groups(v, 0), rows >> 8, rows & 255)
    out[0, :, 2 * OV :] = gather_sent(v_other, 0, 1)


def first_pairs_kernel(slots, found, a, v, *refs):
    own_rows, outs, (blocks, flat) = refs[:24], refs[24:28], refs[28:]
    for p in range(SUBS):
        for j in range(6):
            blocks[p * 8 + j, :, :K] = nt_dot(
                own_rows[p * 6 + j][...], found[p, :, j * OV : j * OV + OV]
            )
        own = None
        for g in range(G):
            part = nt_dot(a[p, g], wide(v, p, g))
            own = part if own is None else own + part
        blocks[p * 8 + 6, :, :K] = own
        blocks[p * 8 + 7, :, :] = jnp.zeros((K, 128), f32)
    put_shares(blocks, flat, outs)


def pairs_kernel(routes, earlier, slots, *refs):
    n = len(routes)
    v, own_rows = refs[:n], refs[n : n + 16]
    refs = refs[n + 16 + earlier :]
    outs, (blocks, flat) = refs[:4], refs[4:]
    for p in range(4 // n):
        for r in range(n):
            found = gather_sent(v[r], p, routes[r])
            for q in range(SUBS):
                j = (p * n + r) * 4 + q
                blocks[j, :, :K] = nt_dot(own_rows[j][...], found[:, q * OV : q * OV + OV])
    put_shares(blocks, flat, outs)


def tables_kernel(neighbours, maps, rows, vt, idx, back, sent_v, slots, order, held, codes):
    value = rows[...]
    high = (value >> 9) * 2 + ((value >> 7) & 1)
    value = high * L + ((value >> 8) & 1) * 128 + (value & 127)
    idx[...] = value
    codes[...] = coded(value)
    held[...] = jnp.ones_like(held)
    me = lax.axis_index("sub")
    base = lax.rem(me, 2) * 64
    lane = lax.broadcasted_iota(i32, (1, 128), 1)
    for i in range(112):
        slots[i] = 0

    def two(half, carry):
        for n in (2 * half, 2 * half + 1):
            for j in range(SUBS):
                named = neighbours[j, n]
                none = named < 0
                step = ((named >> 2) - me) & 31
                other = named & 3
                sent = jnp.where(none, 7, maps[base + step])
                source = maps[base + 32 + step]
                at = ((sent - 1) & 7) * 16 + other * 3
                line = codes[n, j : j + 1, :]
                for t in range(3):
                    held[j, pl.ds(at + t, 1), :] = line[:, 128 * t : 128 * t + 128]
                slots[jnp.where(none, 112, source * 16 + other * 4 + j)] = n
                near = other * 8 + jnp.where(source == 0, (other ^ j) - 1, 2 + j)
                later = (source >> 1) * 32 + other * 8 + (source & 1) * 4 + j
                spot = jnp.where(source < 6, later, 96 + other * 4 + j)
                spot = jnp.where(none, -1, jnp.where(source < 2, near, spot))
                order[pl.ds(n * 4 + j, 1), :] = (lane == spot).astype(f32)
        return carry

    lax.fori_loop(0, NB // 2, two, 0)
    back[...] = held[:, 112:, :]
    sent_v[:, :12] = vt[...]
    sent_v[:, 12] = held[:, :K, :].astype(bf16)


def final_kernel(order, *refs):
    pieces, (out, out_self, total) = refs[:-3], refs[-3:]
    start = 0
    for chunk, count in enumerate(CHUNKS):
        own, r1, r2, r3 = pieces[4 * chunk : 4 * chunk + 4]
        total[start : start + count, :] = (
            own[...] + r1[...].astype(f32) + r2[...].astype(f32) + r3[...].astype(f32)
        )
        start += count
    total[start:, :] = jnp.zeros((128 - start, SHARE), f32)
    for s in range(SUBS):
        out_self[s : s + 1, :] = total[s * 8 + 6 : s * 8 + 7, :] * float(ROWS * 4) ** (-0.5)
    which = order[...].astype(bf16)
    rest = total[...]
    placed = None
    for _ in range(3):
        part = rest.astype(bf16)
        rest = rest - part.astype(f32)
        taken = jnp.dot(which, part, preferred_element_type=f32)
        placed = taken if placed is None else placed + taken
    for n in range(NB):
        out[n] = placed[4 * n : 4 * n + 4]


def share_shapes(count):
    return [jax.ShapeDtypeStruct((count, SHARE), f32 if s == 0 else bf16) for s in range(4)]


def row_exchange(shares):
    return [shares[0]] + [
        lax.ppermute(shares[s], "row", [(i, (i + s) % 4) for i in range(4)]) for s in (1, 2, 3)
    ]


def whole(shape):
    return pl.BlockSpec(shape, lambda *_: (0,) * len(shape))


def on_device(deflation, center, stiffness, coupling, neighbours, shared_rows):
    n_sub = lax.axis_size("sub")
    smem = pl.BlockSpec(memory_space=pltpu.SMEM)
    vt = jnp.transpose(deflation, (0, 2, 4, 3, 1, 5))
    vt = lax.optimization_barrier(vt)
    halo = (SUBS, 6, K, 128)
    below = lax.ppermute(vt[:, :, 1], "row", [(i, i + 1) for i in range(3)]).reshape(halo)
    above = lax.ppermute(vt[:, :, 0], "row", [(i + 1, i) for i in range(3)]).reshape(halo)

    maps = []
    for tables in ((TARGET_EVEN, SOURCE_EVEN), (TARGET_ODD, SOURCE_ODD)):
        for offsets in tables:
            line = [0] * 32
            for route, offset in enumerate(offsets):
                line[offset % n_sub] = route
            maps += line
    idx, back, sent_v, slots, order = call(
        tables_kernel,
        [
            jax.ShapeDtypeStruct((NB, SUBS, OV), i32),
            jax.ShapeDtypeStruct((SUBS, 16, 128), f32),
            jax.ShapeDtypeStruct((SUBS, TILES, K, 128), bf16),
            jax.ShapeDtypeStruct((128,), i32),
            jax.ShapeDtypeStruct((SUBS * NB, 128), f32),
        ],
        pltpu.PrefetchScalarGridSpec(
            num_scalar_prefetch=2,
            grid=(1,),
            in_specs=[whole((NB, SUBS, OV)), whole((SUBS, 12, K, 128))],
            out_specs=[
                whole((NB, SUBS, OV)),
                whole((SUBS, 16, 128)),
                whole((SUBS, TILES, K, 128)),
                smem,
                whole((SUBS * NB, 128)),
            ],
            scratch_shapes=[
                pltpu.VMEM((SUBS, 128, 128), f32),
                pltpu.VMEM((NB, SUBS, OV), f32),
            ],
        ),
        2 * 10**9,
        3 << 20,
    )(
        neighbours,
        jnp.array(maps, i32),
        jnp.transpose(shared_rows, (1, 0, 2)),
        vt.reshape(SUBS, 12, K, 128),
    )

    ring = lambda x, by: lax.ppermute(x, "sub", [(i, (i + by) % n_sub) for i in range(n_sub)])
    swap = lambda x: lax.ppermute(x, "sub", [(i, i ^ 1) for i in range(n_sub)])
    plus2, minus2 = ring(sent_v, -2), ring(sent_v, 2)
    other = swap(sent_v)

    coup = coupling.reshape(26, 9)
    v_spec = pl.BlockSpec((1, TILES, K, 128), lambda s, *_: (s, 0, 0, 0))
    halo_spec = pl.BlockSpec((1, 6, K, 128), lambda s, *_: (s, 0, 0, 0))
    a_spec = pl.BlockSpec((1, G, K, L), lambda s, *_: (s, 0, 0, 0))
    stiff_spec = pl.BlockSpec((1, 26, 2, 2, 128), lambda s, *_: (s, 0, 0, 0, 0))
    inner = call(
        inner_kernel,
        jax.ShapeDtypeStruct((SUBS, G, K, L), f32),
        pl.GridSpec(
            grid=(SUBS,),
            in_specs=[
                smem,
                v_spec,
                stiff_spec,
                pl.BlockSpec((1, 2, 2, 128), lambda s: (s, 0, 0, 0)),
            ],
            out_specs=a_spec,
        ),
        5 * 10**9,
        5 << 20,
    )(coup, sent_v, stiffness, center)

    found = call(
        early_kernel,
        jax.ShapeDtypeStruct((SUBS, K, 6 * OV), bf16),
        pl.GridSpec(
            grid=(SUBS,),
            in_specs=[v_spec, v_spec, pl.BlockSpec((1, 16, 128), lambda s: (s, 0, 0))],
            out_specs=pl.BlockSpec((1, K, 6 * OV), lambda s: (s, 0, 0)),
        ),
        5 * 10**9,
        5 << 20,
    )(sent_v, other, back)

    below, above, found = lax.optimization_barrier((below, above, found))
    applied = call(
        outer_kernel,
        jax.ShapeDtypeStruct((SUBS, G, K, L), bf16),
        pl.GridSpec(
            grid=(SUBS,),
            in_specs=[smem, a_spec, halo_spec, halo_spec, stiff_spec],
            out_specs=a_spec,
        ),
        3 * 10**9,
        6 << 20,
    )(coup, inner, below, above, stiffness)

    def take_rows(s, idx):
        return call(
            functools.partial(own_rows_kernel, s),
            jax.ShapeDtypeStruct((K, NB * OV), bf16),
            pl.GridSpec(
                grid=(1,),
                in_specs=[
                    pl.BlockSpec((1, G, K, L), lambda i: (s, 0, 0, 0)),
                    whole((NB, SUBS, OV)),
                ],
                out_specs=whole((K, NB * OV)),
            ),
            6 * 10**9,
            4 << 20,
        )(applied, idx)

    own_rows = [take_rows(s, idx) for s in range(HOLD)]
    idx, plus2, minus2, own_rows[HOLD - 1] = lax.optimization_barrier(
        (idx, plus2, minus2, own_rows[HOLD - 1])
    )
    own_rows += [take_rows(s, idx) for s in range(HOLD, SUBS)]
    far = lax.ppermute(
        jnp.where(lax.axis_index("sub") % 2 == 0, plus2, minus2),
        "sub",
        [(i, (i - 1) % n_sub if i % 2 == 0 else (i + 1) % n_sub) for i in range(n_sub)],
    )
    plus2x, minus2x = swap(plus2), swap(minus2)

    def row_spec(route, p, step, q):
        return pl.BlockSpec((K, OV), lambda i, t: (0, t[route * 16 + (p + step * i) * 4 + q]))

    share_specs = lambda n: [pl.BlockSpec((n, SHARE), lambda i, *_: (i, 0))] * 4
    scratch = lambda n: [pltpu.VMEM((n, K, 128), f32), pltpu.VMEM((n, K * K), f32)]
    near = [
        (route, p, 0, q)
        for p in range(SUBS)
        for route, q in [(0, p ^ 1), (0, p ^ 2)] + [(1, q) for q in range(SUBS)]
    ]
    near_shares = call(
        first_pairs_kernel,
        share_shapes(CHUNKS[0]),
        pltpu.PrefetchScalarGridSpec(
            num_scalar_prefetch=1,
            grid=(1,),
            in_specs=[
                whole((SUBS, K, 6 * OV)),
                whole((SUBS, G, K, L)),
                whole((SUBS, TILES, K, 128)),
            ]
            + [row_spec(*spot) for spot in near],
            out_specs=share_specs(32),
            scratch_shapes=scratch(32),
        ),
        3 * 10**9,
        8 << 20,
    )(slots, found, applied, sent_v, *[own_rows[spot[3]] for spot in near])

    blocks = [sent_v, other, plus2, minus2, plus2x, minus2x, far]
    pieces = []
    for routes in ((2, 3), (4, 5), (6,)):
        n = len(routes)
        rows = [
            (route, p, 4 // n, q) for p in range(4 // n) for route in routes for q in range(SUBS)
        ]
        earlier = near_shares if routes[0] == 2 else []
        skip = len(earlier) // 2
        shares = call(
            functools.partial(pairs_kernel, routes, len(earlier)),
            share_shapes(16 * (n + skip)),
            pltpu.PrefetchScalarGridSpec(
                num_scalar_prefetch=1,
                grid=(n,),
                in_specs=[pl.BlockSpec((4 // n, TILES, K, 128), lambda i, t: (i, 0, 0, 0))] * n
                + [row_spec(*spot) for spot in rows]
                + [pl.BlockSpec(memory_space=pl.ANY)] * len(earlier),
                out_specs=[pl.BlockSpec((16, SHARE), lambda i, t, skip=skip: (i + skip, 0))] * 4,
                scratch_shapes=scratch(16),
            ),
            n * 5 * 10**9,
            n * 5 << 20,
            {1 + n + 16 + s: s for s in range(len(earlier))},
        )(slots, *[blocks[o] for o in routes], *[own_rows[spot[3]] for spot in rows], *earlier)
        pieces += row_exchange(shares)

    pairs, selfs = call(
        final_kernel,
        [
            jax.ShapeDtypeStruct((NB, SUBS, SHARE), f32),
            jax.ShapeDtypeStruct((SUBS, SHARE), f32),
        ],
        pl.GridSpec(
            grid=(1,),
            in_specs=[whole((SUBS * NB, 128))]
            + [whole((count, SHARE)) for count in CHUNKS for _ in range(4)],
            out_specs=[whole((NB, SUBS, SHARE)), whole((SUBS, SHARE))],
            scratch_shapes=[pltpu.VMEM((128, SHARE), f32)],
        ),
        10**7,
        4 << 20,
    )(order, *pieces)
    return jnp.transpose(pairs, (1, 0, 2)), selfs


HOLD = 3


def solution(mesh):
    return jax.shard_map(
        on_device,
        mesh=mesh,
        in_specs=(
            P("sub", None, None, None, "row", None),
            P("sub", None, "row", None),
            P("sub", None, None, "row", None),
            P(),
            P("sub", None),
            P("sub", None, "row"),
        ),
        out_specs=(P("sub", None, "row"), P("sub", "row")),
        check_vma=False,
    )
```

time: 1380 us -> 110 us (0.08)
  local copies, waits for them, and re-layouts: 845 us -> 5.06 us
  other arithmetic: 314 us -> 0.13 us
  waiting for transfers between devices: 103 us -> 4.43 us
  matrix products: 78.5 us -> 0 us
  Pallas kernels: 0 us -> 66.8 us
  starting transfers between devices: 16.8 us -> 31.8 us
  between operations: 15.2 us -> 0.9 us
    gather x5 -> x0, local copies, waits for them, and re-layouts: 791 us -> none  [select_rows(): return row_major[index_rows]]
    add x34 -> x0, other arithmetic: 203 us -> none  [the longest x26 203 us: mix_components(): matrix[component, 0] * shifted[:, 0] + matrix[component, 1] * shifted[:, 1]]
    convert_element_type x4 -> x0, other arithmetic: 96 us -> none  [the longest x3 60.4 us: apply_operator(): shifted = padded[:, :, 1 + shift_x:1 + shift_x + size_x, 1 + shift_y:1 +...]
    psum x1 -> x0, waiting for transfers between devices: 86.4 us -> none  [on_device(): summed_pairs, summed_self = lax.psum((pair_flat, self_flat), 'row')]
    dot_general x10 -> x0, matrix products: 78.5 us -> none  [the longest x7 42.9 us: on_device(): jnp.einsum('jqn,jnrk->jqrk', chosen, vector_rows, preferred_element_type=...]
    pallas_call x0 -> x13, Pallas kernels: none -> 66.8 us  [the longest x4 21.5 us: take_rows(): call(functools.partial(own_rows_kernel, s), jax.ShapeDtypeStruct((K, NB *...]
    unnamed x82 -> x21, local copies, waits for them, and re-layouts: 21.6 us -> 3.78 us
    ppermute x8 -> x17, starting transfers between devices: 16.7 us -> 31.8 us  [the longest x9 15.1 us: row_exchange(): lax.ppermute(shares[s], 'row', [(i, (i + s) % 4) for i in range(4)])]
  transfers between devices with their start and end apart: 9 -> 17, of which waited for: 2 -> 3; matrix products, arithmetic and copies ran while one was open for 86% -> 1% of each run, Pallas kernels for 0% -> 52%
where the time goes in v2:
time: 110 us; the launch traced here: 109 us
  Pallas kernels  66.8 us (61%)
  starting transfers between devices  31.8 us (29%)
  local copies, waits for them, and re-layouts  5.06 us (5%)
  waiting for transfers between devices  4.43 us (4%)
    pallas_call x4, Pallas kernels, take_rows(): call(functools.partial(own_rows_kernel, s), jax.ShapeDtypeStruct((K, NB *...  21.5 us
    pallas_call x3, Pallas kernels, on_device(): call(functools.partial(pairs_kernel, routes, len(earlier)), share_shapes(...  19.5 us
    ppermute x9, starting transfers between devices, row_exchange(): lax.ppermute(shares[s], 'row', [(i, (i + s) % 4) for i in range(4)])  15.1 us
    pallas_call x1, Pallas kernels, on_device(): call(inner_kernel, jax.ShapeDtypeStruct((SUBS, G, K, L), f32), pl.GridSpe...  7.05 us
    ppermute x2, starting transfers between devices, on_device(): lax.ppermute(x, 'sub', [(i, (i + by) % n_sub) for i in range(n_sub)])  6.39 us
    pallas_call x1, Pallas kernels, on_device(): call(early_kernel, jax.ShapeDtypeStruct((SUBS, K, 6 * OV), bf16), pl.Grid...  5.03 us
    pallas_call x1, Pallas kernels, on_device(): call(outer_kernel, jax.ShapeDtypeStruct((SUBS, G, K, L), bf16), pl.GridSp...  5.01 us
    ppermute x1, starting transfers between devices, on_device(): lax.ppermute(jnp.where(lax.axis_index('sub') % 2 == 0, plus2, minus2), 's...  4.85 us
  transfers between devices with their start and end apart: 17, of which 3 were waited for; matrix products, arithmetic and copies ran while one was open for 1% of the time, Pallas kernels for 52%

profile of v2, /device:TPU:0, one launch (start us, length us, event | category | flops | bytes accessed | tf_op | source)
XLA Modules:
  0.0 109.1 jit_solution(2747002872633169730)
XLA Ops:
  0.6 1.5 %copy.22 = bf16[4,96,3,2,2,128]{5,1,3,2,0,4:T(8,128)(2,1)S(1)} copy(bf16[4,96,3,2,2,128]{5,4,3,2,1,0:T(2,128)(2,1)} %param.7) | data formatting | bytes 2359296 | tf_op args[0]
  3.1 3.4 %shard_map.86 = (s32[26,4,384]{2,1,0:T(4,128)S(1)}, f32[4,16,128]{2,1,0:T(8,128)S(1)}, bf16[4,13,96,128]{3,2,1,0:T(8,128)(2,1)}, s32[128]{0:T(128)S(1)}, f32[104,128]{1,0:T(8,128)S(1)}) custom-call(s32[4,26]{1,0:T(4,128)S(1)} %copy-done.3, s32[128]{0:T(128)S(1)} %copy-done.4, s32[26,4,384]{2,1,0:T(4,128)S(1)} %bitcast.16, bf16[4,12,96,128]{3,2,1,0:T(8,128)(2,1)S(1)} %bitcast.14), custom_call_target="tpu_custom_call" | custom-call | flops 2000000000 | bytes 3145728 | tf_op jit(solution)/shard_map/pallas_call | solution.py:325
  6.6 6.4 %collective-permute-start = (bf16[4,13,96,128]{3,2,1,0:T(8,128)(2,1)}, bf16[4,13,96,128]{3,2,1,0:T(8,128)(2,1)S(1)}, u32[]{:S(2)}, u32[]{:S(2)}) collective-permute-start(bf16[4,13,96,128]{3,2,1,0:T(8,128)(2,1)} %get-tuple-element.35.v), channel_id=1, source_target_pairs={{0,120},{4,124},{8,0},{12,4},{16,8},{20,12},{24,16},{28,20},{32,24... | collective-permute-start | bytes 3833864 | tf_op jit(solution)/shard_map/ppermute | solution.py:359
  14.1 3.5 %collective-permute-start.2 = (bf16[4,3,2,96,128]{4,3,2,1,0:T(8,128)(2,1)}, bf16[4,3,2,96,128]{4,3,2,1,0:T(8,128)(2,1)S(1)}, u32[]{:S(2)}, u32[]{:S(2)}) collective-permute-start(bf16[4,3,2,96,128]{4,3,2,1,0:T(8,128)(2,1)} %get-tuple-element.63), channel_id=1, source_target_pairs={{0,1},{1,2},{2,3},{4,5},{5,6},{6,7},{8,9},{9,10},{10,11},{12,13},{... | collective-permute-start | bytes 1769480 | tf_op jit(solution)/shard_map/ppermute | solution.py:315
  19.1 7.1 %shard_map.87.inner = f32[4,6,96,256]{3,2,1,0:T(8,128)S(1)} custom-call(f32[26,9]{1,0:T(8,128)S(1)} %copy.20.coup, bf16[4,13,96,128]{3,2,1,0:T(8,128)(2,1)} %get-tuple-element.35.v, f32[4,26,2,2,128]{4,3,2,1,0:T(2,128)S(1)} %copy-done, f32[4,2,2,128]{3,2,1,0:T(2,128)S(1)} %copy-done.2), custom_call_target="tpu_custom_call" | custom-call | flops 5000000000 | bytes 5242880 | tf_op jit(solution)/shard_map/pallas_call | solution.py:369
  26.1 1.4 %copy-done.5 = f32[4,6,96,256]{3,2,1,0:T(8,128)} copy-done((f32[4,6,96,256]{3,2,1,0:T(8,128)}, f32[4,6,96,256]{3,2,1,0:T(8,128)S(1)}, u32[]{:S(2)}) %copy-start.5) | copy-done | bytes 2359320
  27.5 5.0 %shard_map.88.found = bf16[4,96,2304]{2,1,0:T(8,128)(2,1)S(1)} custom-call(bf16[4,13,96,128]{3,2,1,0:T(8,128)(2,1)} %get-tuple-element.35.v, bf16[4,13,96,128]{3,2,1,0:T(8,128)(2,1)} %collective-permute-done.4.v_other, f32[4,16,128]{2,1,0:T(8,128)S(1)} %get-tuple-element.36.back), custom_call_target="tpu_custom_call" | custom-call | flops 5000000000 | bytes 5242880 | tf_op jit(solution)/shard_map/pallas_call | solution.py:386
  32.6 2.4 %collective-permute-done.3 = bf16[4,3,2,96,128]{4,3,2,1,0:T(8,128)(2,1)} collective-permute-done((bf16[4,3,2,96,128]{4,3,2,1,0:T(8,128)(2,1)}, bf16[4,3,2,96,128]{4,3,2,1,0:T(8,128)(2,1)}, u32[]{:S(2)}, u32[]{:S(2)}) %collective-permute-start.3) | collective-permute-done | bytes 589856 | tf_op jit(solution)/shard_map/ppermute | solution.py:316
  35.0 5.0 %shard_map.89.a = bf16[4,6,96,256]{3,2,1,0:T(8,128)(2,1)S(1)} custom-call(f32[26,9]{1,0:T(8,128)S(1)} %copy.20.coup, f32[4,6,96,256]{3,2,1,0:T(8,128)S(1)} %copy-done.6, bf16[4,6,96,128]{3,2,1,0:T(8,128)(2,1)S(1)} %bitcast.15, bf16[4,6,96,128]{3,2,1,0:T(8,128)(2,1)} %bitcast.6.above, f32[4,26,2,2,128]{4,3,2,1,0:T(2,128)S(1)} %copy-done), custom_call_target="tpu_custom_call" | custom-call | flops 3000000000 | bytes 6291456 | tf_op jit(solution)/shard_map/pallas_call | solution.py:399
  40.0 5.4 %shard_map.90.refs_1_.refs_4_.refs_10_.refs_16_.refs_18_.refs_22_.refs_8_.refs_12_.refs_3_.refs_7_.refs_11_.refs_15_ = bf16[96,9984]{1,0:T(8,128)(2,1)S(1)} custom-call(bf16[4,6,96,256]{3,2,1,0:T(8,128)(2,1)S(1)} %shard_map.89.a, s32[26,4,384]{2,1,0:T(4,128)S(1)} %copy-done.8), custom_call_target="tpu_custom_call" | custom-call | flops 6000000000 | bytes 4194304 | tf_op jit(solution)/shard_map/pallas_call | solution.py:412
  45.4 5.4 %shard_map.91.refs_2_.refs_6_.refs_8_.refs_13_.refs_14_.refs_20_.refs_10_.refs_1_.refs_5_.refs_9_ = bf16[96,9984]{1,0:T(8,128)(2,1)S(1)} custom-call(bf16[4,6,96,256]{3,2,1,0:T(8,128)(2,1)S(1)} %shard_map.89.a, s32[26,4,384]{2,1,0:T(4,128)S(1)} %copy-done.8), custom_call_target="tpu_custom_call" | custom-call | flops 6000000000 | bytes 4194304 | tf_op jit(solution)/shard_map/pallas_call | solution.py:412
  50.8 5.4 %shard_map.92.refs_0_.refs_3_.refs_9_.refs_15_.refs_19_.refs_21_.refs_7_.refs_11_.refs_2_.refs_6_.refs_10_.refs_14_ = bf16[96,9984]{1,0:T(8,128)(2,1)S(1)} custom-call(bf16[4,6,96,256]{3,2,1,0:T(8,128)(2,1)S(1)} %shard_map.89.a, s32[26,4,384]{2,1,0:T(4,128)S(1)} %copy-done.8), custom_call_target="tpu_custom_call" | custom-call | flops 6000000000 | bytes 4194304 | tf_op jit(solution)/shard_map/pallas_call | solution.py:412
  56.2 5.4 %shard_map.93.refs_5_.refs_7_.refs_11_.refs_12_.refs_17_.refs_23_.refs_9_.refs_13_.refs_4_.refs_8_.refs_16_ = bf16[96,9984]{1,0:T(8,128)(2,1)S(1)} custom-call(bf16[4,6,96,256]{3,2,1,0:T(8,128)(2,1)S(1)} %shard_map.89.a, s32[26,4,384]{2,1,0:T(4,128)S(1)} %copy-done.8), custom_call_target="tpu_custom_call" | custom-call | flops 6000000000 | bytes 4194304 | tf_op jit(solution)/shard_map/pallas_call | solution.py:412
  62.3 4.8 %collective-permute-start.13 = (bf16[4,13,96,128]{3,2,1,0:T(8,128)(2,1)S(1)}, bf16[4,13,96,128]{3,2,1,0:T(8,128)(2,1)S(1)}, u32[]{:S(2)}, u32[]{:S(2)}) collective-permute-start(bf16[4,13,96,128]{3,2,1,0:T(8,128)(2,1)S(1)} %broadcast_select_fusion), channel_id=1, source_target_pairs={{0,124},{4,8},{8,4},{12,16},{16,12},{20,24},{24,20},{28,32},{32,28... | collective-permute-start | bytes 3833864 | tf_op jit(solution)/shard_map/ppermute | solution.py:432
  67.1 3.6 %shard_map.94 = (f32[64,2304]{1,0:T(8,128)S(1)}, bf16[64,2304]{1,0:T(8,128)(2,1)S(1)}, bf16[64,2304]{1,0:T(8,128)(2,1)S(1)}, bf16[64,2304]{1,0:T(8,128)(2,1)S(1)}) custom-call(s32[128]{0:T(128)S(1)} %get-tuple-element.33.slots, bf16[4,96,2304]{2,1,0:T(8,128)(2,1)S(1)} %shard_map.88.found, bf16[4,6,96,256]{3,2,1,0:T(8,128)(2,1)S(1)} %shard_map.89.a, ...), custom_call_target="tpu_custom_call" | custom-call | flops 3000000000 | bytes 8388608 | tf_op jit(solution)/shard_map/pallas_call | solution.py:449
  70.7 7.8 %shard_map.95 = (f32[64,2304]{1,0:T(8,128)S(1)}, bf16[64,2304]{1,0:T(8,128)(2,1)S(1)}, bf16[64,2304]{1,0:T(8,128)(2,1)S(1)}, bf16[64,2304]{1,0:T(8,128)(2,1)S(1)}) custom-call(s32[128]{0:T(128)S(1)} %get-tuple-element.33.slots, ...), custom_call_target="tpu_custom_call", output_to_operand_aliasing={{0}: (19, {}), {1}: (20, {}), {2}: (21, {}), {3}: (22, {})} | custom-call | flops 10000000000 | bytes 10485760 | tf_op jit(solution)/shard_map/pallas_call | solution.py:477
  78.6 1.6 %collective-permute-start.5 = (bf16[64,2304]{1,0:T(8,128)(2,1)S(1)}, bf16[64,2304]{1,0:T(8,128)(2,1)S(1)}, u32[]{:S(2)}, u32[]{:S(2)}) collective-permute-start(bf16[64,2304]{1,0:T(8,128)(2,1)S(1)} %get-tuple-element.49), channel_id=1, source_target_pairs={{0,1},{1,2},{2,3},{3,0},{4,5},{5,6},{6,7},{7,4},{8,9},{9,10},{10,1... | collective-permute-start | bytes 884744 | tf_op jit(solution)/shard_map/ppermute | solution.py:301
  80.2 2.8 %collective-permute-start.6 = (bf16[64,2304]{1,0:T(8,128)(2,1)S(1)}, bf16[64,2304]{1,0:T(8,128)(2,1)S(1)}, u32[]{:S(2)}, u32[]{:S(2)}) collective-permute-start(bf16[64,2304]{1,0:T(8,128)(2,1)S(1)} %get-tuple-element.50), channel_id=1, source_target_pairs={{0,2},{1,3},{2,0},{3,1},{4,6},{5,7},{6,4},{7,5},{8,10},{9,11},{10,... | collective-permute-start | bytes 884744 | tf_op jit(solution)/shard_map/ppermute | solution.py:301
  84.2 7.9 %shard_map.96 = (f32[32,2304]{1,0:T(8,128)S(1)}, bf16[32,2304]{1,0:T(8,128)(2,1)S(1)}, bf16[32,2304]{1,0:T(8,128)(2,1)S(1)}, bf16[32,2304]{1,0:T(8,128)(2,1)S(1)}) custom-call(s32[128]{0:T(128)S(1)} %get-tuple-element.33.slots, bf16[4,13,96,128]{3,2,1,0:T(8,128)(2,1)S(1)} %collective-permute-done.8.refs_0_, ...), custom_call_target="tpu_custom_call" | custom-call | flops 10000000000 | bytes 10485760 | tf_op jit(solution)/shard_map/pallas_call | solution.py:477
  93.0 3.8 %shard_map.97 = (f32[16,2304]{1,0:T(8,128)S(1)}, bf16[16,2304]{1,0:T(8,128)(2,1)S(1)}, bf16[16,2304]{1,0:T(8,128)(2,1)S(1)}, bf16[16,2304]{1,0:T(8,128)(2,1)S(1)}) custom-call(s32[128]{0:T(128)S(1)} %get-tuple-element.33.slots, bf16[4,13,96,128]{3,2,1,0:T(8,128)(2,1)S(1)} %collective-permute-done.13.refs_0_, ...), custom_call_target="tpu_custom_call" | custom-call | flops 5000000000 | bytes 5242880 | tf_op jit(solution)/shard_map/pallas_call | solution.py:477
  96.9 3.8 %collective-permute-start.11 = (bf16[32,2304]{1,0:T(8,128)(2,1)S(1)}, bf16[32,2304]{1,0:T(8,128)(2,1)S(1)}, u32[]{:S(2)}, u32[]{:S(2)}) collective-permute-start(bf16[32,2304]{1,0:T(8,128)(2,1)S(1)} %get-tuple-element.54), channel_id=1, source_target_pairs={{0,2},{1,3},{2,0},{3,1},{4,6},{5,7},{6,4},{7,5},{8,10},{9,11},{10,... | collective-permute-start | bytes 442376 | tf_op jit(solution)/shard_map/ppermute | solution.py:301
  100.7 2.3 %collective-permute-start.15 = (bf16[16,2304]{1,0:T(8,128)(2,1)S(1)}, bf16[16,2304]{1,0:T(8,128)(2,1)S(1)}, u32[]{:S(2)}, u32[]{:S(2)}) collective-permute-start(bf16[16,2304]{1,0:T(8,128)(2,1)S(1)} %get-tuple-element.58), channel_id=1, source_target_pairs={{0,2},{1,3},{2,0},{3,1},{4,6},{5,7},{6,4},{7,5},{8,10},{9,11},{10,... | collective-permute-start | bytes 221192 | tf_op jit(solution)/shard_map/ppermute | solution.py:301
  103.1 2.4 %collective-permute-start.16 = (bf16[16,2304]{1,0:T(8,128)(2,1)S(1)}, bf16[16,2304]{1,0:T(8,128)(2,1)S(1)}, u32[]{:S(2)}, u32[]{:S(2)}) collective-permute-start(bf16[16,2304]{1,0:T(8,128)(2,1)S(1)} %get-tuple-element.59), channel_id=1, source_target_pairs={{0,3},{1,0},{2,1},{3,2},{4,7},{5,4},{6,5},{7,6},{8,11},{9,8},{10,9... | collective-permute-start | bytes 221192 | tf_op jit(solution)/shard_map/ppermute | solution.py:301
  107.5 1.7 %shard_map.98 = (f32[26,4,2304]{2,1,0:T(4,128)}, f32[4,2304]{1,0:T(4,128)}) custom-call(f32[104,128]{1,0:T(8,128)S(1)} %get-tuple-element.32.order, f32[64,2304]{1,0:T(8,128)S(1)} %get-tuple-element.48.refs_0_, bf16[64,2304]{1,0:T(8,128)(2,1)S(1)} %collective-permute-done.5.refs_1_, bf16[64,2304]{1,0:T(8,128)(2,1)S(1)} %collective-permute-done.6.refs_2_, ...), custom_call_target="tpu_custom_call" | custom-call | flops 10000000 | bytes 4194304 | tf_op jit(solution)/shard_map/pallas_call | solution.py:495
  (49 shorter events, 8.5 us)
Async XLA Ops:
  6.5 7.6 %copy-start.7 = (s32[26,4,384]{2,1,0:T(4,128)}, s32[26,4,384]{2,1,0:T(4,128)S(1)}, u32[]{:S(2)}) copy-start(s32[26,4,384]{2,1,0:T(4,128)S(1)} %get-tuple-element.42.idx) | copy-start | bytes 479236
  6.5 12.4 %copy-start.9 = (f32[26,3,3]{0,2,1:T(4,128)S(1)}, f32[26,3,3]{0,2,1:T(4,128)}, u32[]{:S(2)}) copy-start(f32[26,3,3]{0,2,1:T(4,128)} %param.10) | copy-start | bytes 2812
  6.5 12.5 %copy-start = (f32[4,26,2,2,128]{4,3,2,1,0:T(2,128)S(1)}, f32[4,26,2,2,128]{4,3,2,1,0:T(2,128)}, u32[]{:S(2)}) copy-start(f32[4,26,2,2,128]{4,3,2,1,0:T(2,128)} %stiff.3) | copy-start | bytes 638980
  6.5 12.5 %copy-start.2 = (f32[4,2,2,128]{3,2,1,0:T(2,128)S(1)}, f32[4,2,2,128]{3,2,1,0:T(2,128)}, u32[]{:S(2)}) copy-start(f32[4,2,2,128]{3,2,1,0:T(2,128)} %center.1) | copy-start | bytes 24580
  6.5 21.0 %collective-permute-start.4 = (bf16[4,13,96,128]{3,2,1,0:T(8,128)(2,1)}, bf16[4,13,96,128]{3,2,1,0:T(8,128)(2,1)}, u32[]{:S(2)}, u32[]{:S(2)}) collective-permute-start(bf16[4,13,96,128]{3,2,1,0:T(8,128)(2,1)} %get-tuple-element.35.v), channel_id=1, source_target_pairs={{0,4},{4,0},{8,12},{12,8},{16,20},{20,16},{24,28},{28,24},{32,36},... | collective-permute-start | bytes 3833864 | tf_op jit(solution)/shard_map/ppermute | solution.py:360
  6.6 49.5 %collective-permute-start = (bf16[4,13,96,128]{3,2,1,0:T(8,128)(2,1)}, bf16[4,13,96,128]{3,2,1,0:T(8,128)(2,1)S(1)}, u32[]{:S(2)}, u32[]{:S(2)}) collective-permute-start(bf16[4,13,96,128]{3,2,1,0:T(8,128)(2,1)} %get-tuple-element.35.v), channel_id=1, source_target_pairs={{0,120},{4,124},{8,0},{12,4},{16,8},{20,12},{24,16},{28,20},{32,24... | collective-permute-start | bytes 3833864 | tf_op jit(solution)/shard_map/ppermute | solution.py:359
  13.0 43.2 %collective-permute-start.1 = (bf16[4,13,96,128]{3,2,1,0:T(8,128)(2,1)}, bf16[4,13,96,128]{3,2,1,0:T(8,128)(2,1)S(1)}, u32[]{:S(2)}, u32[]{:S(2)}) collective-permute-start(bf16[4,13,96,128]{3,2,1,0:T(8,128)(2,1)} %get-tuple-element.35.v), channel_id=1, source_target_pairs={{0,8},{4,12},{8,16},{12,20},{16,24},{20,28},{24,32},{28,36},{32,40... | collective-permute-start | bytes 3833864 | tf_op jit(solution)/shard_map/ppermute | solution.py:359
  14.1 18.5 %collective-permute-start.2 = (bf16[4,3,2,96,128]{4,3,2,1,0:T(8,128)(2,1)}, bf16[4,3,2,96,128]{4,3,2,1,0:T(8,128)(2,1)S(1)}, u32[]{:S(2)}, u32[]{:S(2)}) collective-permute-start(bf16[4,3,2,96,128]{4,3,2,1,0:T(8,128)(2,1)} %get-tuple-element.63), channel_id=1, source_target_pairs={{0,1},{1,2},{2,3},{4,5},{5,6},{6,7},{8,9},{9,10},{10,11},{12,13},{... | collective-permute-start | bytes 1769480 | tf_op jit(solution)/shard_map/ppermute | solution.py:315
  17.6 17.3 %collective-permute-start.3 = (bf16[4,3,2,96,128]{4,3,2,1,0:T(8,128)(2,1)}, bf16[4,3,2,96,128]{4,3,2,1,0:T(8,128)(2,1)}, u32[]{:S(2)}, u32[]{:S(2)}) collective-permute-start(bf16[4,3,2,96,128]{4,3,2,1,0:T(8,128)(2,1)} %get-tuple-element.62), channel_id=1, source_target_pairs={{1,0},{2,1},{3,2},{5,4},{6,5},{7,6},{9,8},{10,9},{11,10},{13,12},{... | collective-permute-start | bytes 1769480 | tf_op jit(solution)/shard_map/ppermute | solution.py:316
  26.1 1.4 %copy-start.5 = (f32[4,6,96,256]{3,2,1,0:T(8,128)}, f32[4,6,96,256]{3,2,1,0:T(8,128)S(1)}, u32[]{:S(2)}) copy-start(f32[4,6,96,256]{3,2,1,0:T(8,128)S(1)} %shard_map.87.inner) | copy-start | bytes 7077892
  27.5 7.4 %copy-start.6 = (f32[4,6,96,256]{3,2,1,0:T(8,128)S(1)}, f32[4,6,96,256]{3,2,1,0:T(8,128)}, u32[]{:S(2)}) copy-start(f32[4,6,96,256]{3,2,1,0:T(8,128)} %copy-done.5) | copy-start | bytes 7077892
  35.0 5.0 %copy-start.8 = (s32[26,4,384]{2,1,0:T(4,128)S(1)}, s32[26,4,384]{2,1,0:T(4,128)}, u32[]{:S(2)}) copy-start(s32[26,4,384]{2,1,0:T(4,128)} %copy-done.7) | copy-start | bytes 479236
  61.6 21.5 %collective-permute-start.8 = (bf16[4,13,96,128]{3,2,1,0:T(8,128)(2,1)S(1)}, bf16[4,13,96,128]{3,2,1,0:T(8,128)(2,1)S(1)}, u32[]{:S(2)}, u32[]{:S(2)}) collective-permute-start(bf16[4,13,96,128]{3,2,1,0:T(8,128)(2,1)S(1)} %collective-permute-done.refs_0_), channel_id=1, source_target_pairs={{0,4},{4,0},{8,12},{12,8},{16,20},{20,16},{24,28},{28,24},{32,36},... | collective-permute-start | bytes 3833864 | tf_op jit(solution)/shard_map/ppermute | solution.py:360
  61.6 22.5 %collective-permute-start.9 = (bf16[4,13,96,128]{3,2,1,0:T(8,128)(2,1)S(1)}, bf16[4,13,96,128]{3,2,1,0:T(8,128)(2,1)S(1)}, u32[]{:S(2)}, u32[]{:S(2)}) collective-permute-start(bf16[4,13,96,128]{3,2,1,0:T(8,128)(2,1)S(1)} %collective-permute-done.1.refs_1_), channel_id=1, source_target_pairs={{0,4},{4,0},{8,12},{12,8},{16,20},{20,16},{24,28},{28,24},{32,36},... | collective-permute-start | bytes 3833864 | tf_op jit(solution)/shard_map/ppermute | solution.py:360
  62.3 30.7 %collective-permute-start.13 = (bf16[4,13,96,128]{3,2,1,0:T(8,128)(2,1)S(1)}, bf16[4,13,96,128]{3,2,1,0:T(8,128)(2,1)S(1)}, u32[]{:S(2)}, u32[]{:S(2)}) collective-permute-start(bf16[4,13,96,128]{3,2,1,0:T(8,128)(2,1)S(1)} %broadcast_select_fusion), channel_id=1, source_target_pairs={{0,124},{4,8},{8,4},{12,16},{16,12},{20,24},{24,20},{28,32},{32,28... | collective-permute-start | bytes 3833864 | tf_op jit(solution)/shard_map/ppermute | solution.py:432
  78.6 18.4 %collective-permute-start.5 = (bf16[64,2304]{1,0:T(8,128)(2,1)S(1)}, bf16[64,2304]{1,0:T(8,128)(2,1)S(1)}, u32[]{:S(2)}, u32[]{:S(2)}) collective-permute-start(bf16[64,2304]{1,0:T(8,128)(2,1)S(1)} %get-tuple-element.49), channel_id=1, source_target_pairs={{0,1},{1,2},{2,3},{3,0},{4,5},{5,6},{6,7},{7,4},{8,9},{9,10},{10,1... | collective-permute-start | bytes 884744 | tf_op jit(solution)/shard_map/ppermute | solution.py:301
  80.2 20.5 %collective-permute-start.6 = (bf16[64,2304]{1,0:T(8,128)(2,1)S(1)}, bf16[64,2304]{1,0:T(8,128)(2,1)S(1)}, u32[]{:S(2)}, u32[]{:S(2)}) collective-permute-start(bf16[64,2304]{1,0:T(8,128)(2,1)S(1)} %get-tuple-element.50), channel_id=1, source_target_pairs={{0,2},{1,3},{2,0},{3,1},{4,6},{5,7},{6,4},{7,5},{8,10},{9,11},{10,... | collective-permute-start | bytes 884744 | tf_op jit(solution)/shard_map/ppermute | solution.py:301
  83.0 17.7 %collective-permute-start.7 = (bf16[64,2304]{1,0:T(8,128)(2,1)S(1)}, bf16[64,2304]{1,0:T(8,128)(2,1)S(1)}, u32[]{:S(2)}, u32[]{:S(2)}) collective-permute-start(bf16[64,2304]{1,0:T(8,128)(2,1)S(1)} %get-tuple-element.51), channel_id=1, source_target_pairs={{0,3},{1,0},{2,1},{3,2},{4,7},{5,4},{6,5},{7,6},{8,11},{9,8},{10,9... | collective-permute-start | bytes 884744 | tf_op jit(solution)/shard_map/ppermute | solution.py:301
  92.0 15.4 %collective-permute-start.10 = (bf16[32,2304]{1,0:T(8,128)(2,1)S(1)}, bf16[32,2304]{1,0:T(8,128)(2,1)S(1)}, u32[]{:S(2)}, u32[]{:S(2)}) collective-permute-start(bf16[32,2304]{1,0:T(8,128)(2,1)S(1)} %get-tuple-element.53), channel_id=1, source_target_pairs={{0,1},{1,2},{2,3},{3,0},{4,5},{5,6},{6,7},{7,4},{8,9},{9,10},{10,1... | collective-permute-start | bytes 442376 | tf_op jit(solution)/shard_map/ppermute | solution.py:301
  96.8 6.2 %collective-permute-start.14 = (bf16[16,2304]{1,0:T(8,128)(2,1)S(1)}, bf16[16,2304]{1,0:T(8,128)(2,1)S(1)}, u32[]{:S(2)}, u32[]{:S(2)}) collective-permute-start(bf16[16,2304]{1,0:T(8,128)(2,1)S(1)} %get-tuple-element.57), channel_id=1, source_target_pairs={{0,1},{1,2},{2,3},{3,0},{4,5},{5,6},{6,7},{7,4},{8,9},{9,10},{10,1... | collective-permute-start | bytes 221192 | tf_op jit(solution)/shard_map/ppermute | solution.py:301
  96.9 10.5 %collective-permute-start.11 = (bf16[32,2304]{1,0:T(8,128)(2,1)S(1)}, bf16[32,2304]{1,0:T(8,128)(2,1)S(1)}, u32[]{:S(2)}, u32[]{:S(2)}) collective-permute-start(bf16[32,2304]{1,0:T(8,128)(2,1)S(1)} %get-tuple-element.54), channel_id=1, source_target_pairs={{0,2},{1,3},{2,0},{3,1},{4,6},{5,7},{6,4},{7,5},{8,10},{9,11},{10,... | collective-permute-start | bytes 442376 | tf_op jit(solution)/shard_map/ppermute | solution.py:301
  100.7 6.7 %collective-permute-start.12 = (bf16[32,2304]{1,0:T(8,128)(2,1)S(1)}, bf16[32,2304]{1,0:T(8,128)(2,1)S(1)}, u32[]{:S(2)}, u32[]{:S(2)}) collective-permute-start(bf16[32,2304]{1,0:T(8,128)(2,1)S(1)} %get-tuple-element.55), channel_id=1, source_target_pairs={{0,3},{1,0},{2,1},{3,2},{4,7},{5,4},{6,5},{7,6},{8,11},{9,8},{10,9... | collective-permute-start | bytes 442376 | tf_op jit(solution)/shard_map/ppermute | solution.py:301
  100.7 5.9 %collective-permute-start.15 = (bf16[16,2304]{1,0:T(8,128)(2,1)S(1)}, bf16[16,2304]{1,0:T(8,128)(2,1)S(1)}, u32[]{:S(2)}, u32[]{:S(2)}) collective-permute-start(bf16[16,2304]{1,0:T(8,128)(2,1)S(1)} %get-tuple-element.58), channel_id=1, source_target_pairs={{0,2},{1,3},{2,0},{3,1},{4,6},{5,7},{6,4},{7,5},{8,10},{9,11},{10,... | collective-permute-start | bytes 221192 | tf_op jit(solution)/shard_map/ppermute | solution.py:301
  103.1 4.4 %collective-permute-start.16 = (bf16[16,2304]{1,0:T(8,128)(2,1)S(1)}, bf16[16,2304]{1,0:T(8,128)(2,1)S(1)}, u32[]{:S(2)}, u32[]{:S(2)}) collective-permute-start(bf16[16,2304]{1,0:T(8,128)(2,1)S(1)} %get-tuple-element.59), channel_id=1, source_target_pairs={{0,3},{1,0},{2,1},{3,2},{4,7},{5,4},{6,5},{7,6},{8,11},{9,8},{10,9... | collective-permute-start | bytes 221192 | tf_op jit(solution)/shard_map/ppermute | solution.py:301
  (3 other events, 2.7 us)

commit v3 on v2

--- a/solution.py
+++ b/solution.py
@@ -12,22 +12,21 @@
 G, L = 6, 256
 SHARE = K * K // 4
 TILES = 13
-VMEM = 28 << 20
 
 SOURCE_EVEN = (0, 1, 2, -2, 3, -1, -3)
 TARGET_EVEN = (0, 1, -2, 2, -1, 3, -3)
 SOURCE_ODD = (0, -1, 2, -2, 1, -3, 3)
 TARGET_ODD = (0, -1, -2, 2, -3, 1, 3)
-CHUNKS = (64, 32, 16)
-
-
-def call(kernel, out_shape, grid_spec, flops, moved, aliases={}):
+CHUNKS = (32, 48, 32)
+
+
+def call(kernel, out_shape, grid_spec, mib, flops, moved, aliases={}):
     return pl.pallas_call(
         kernel,
         out_shape=out_shape,
         grid_spec=grid_spec,
         input_output_aliases=aliases,
-        compiler_params=pltpu.CompilerParams(vmem_limit_bytes=VMEM),
+        compiler_params=pltpu.CompilerParams(vmem_limit_bytes=mib << 20),
         cost_estimate=pl.CostEstimate(flops=flops, bytes_accessed=moved, transcendentals=0),
     )
 
@@ -60,30 +59,34 @@
     return None if flat == 13 else flat - (flat > 13)
 
 
-def band_tile(on_band, coup, stiff, c, b, y, sy):
-    columns = []
+def band_tile(distance, coup, stiff, c, b, y, sy):
+    weights = {}
     for x in range(2):
-        parts = []
         for x_in in range(2):
-            block = jnp.zeros((128, 128), bf16)
             for sz in (-1, 0, 1):
                 o = offset_number(x_in - x, sy, sz)
-                if o is None:
-                    continue
-                w = stiff[0, o, x, y : y + 1, :] * coup[o, c * 3 + b]
-                block = jnp.where(
-                    on_band[sz], jnp.broadcast_to(w.astype(bf16), (128, 128)), block
-                )
-            parts.append(block)
-        columns.append(jnp.concatenate(parts, axis=0))
-    return jnp.concatenate(columns, axis=1)
+                if o is not None:
+                    w = jnp.broadcast_to(stiff[0, o, x, y : y + 1, :], (16, 128))
+                    weights[x, x_in, sz] = (w * coup[o, c * 3 + b]).astype(bf16)
+    lines = [[], []]
+    for t in range(8):
+        on_band = {sz: distance == sz - 16 * t for sz in (-1, 0, 1)}
+        for x_in in range(2):
+            parts = []
+            for x in range(2):
+                block = jnp.zeros((16, 128), bf16)
+                for sz in (-1, 0, 1):
+                    if (x, x_in, sz) in weights:
+                        block = jnp.where(on_band[sz], weights[x, x_in, sz], block)
+                parts.append(block)
+            lines[x_in].append(jnp.concatenate(parts, axis=1))
+    return jnp.concatenate(lines[0] + lines[1], axis=0)
 
 
 def bands():
-    distance = (
-        lax.broadcasted_iota(i32, (128, 128), 0) - lax.broadcasted_iota(i32, (128, 128), 1)
+    return (
+        lax.broadcasted_iota(i32, (16, 128), 0) - lax.broadcasted_iota(i32, (16, 128), 1)
     ).astype(i16)
-    return {sz: distance == sz for sz in (-1, 0, 1)}
 
 
 def inner_kernel(coup, v, stiff, center, out):
@@ -93,14 +96,11 @@
         for y in range(2):
             mid = wide(v, 0, 2 * c + y)
             diag = jnp.concatenate([center[0, x, y : y + 1, :] for x in range(2)], axis=1)
-            total = diag * mid.astype(f32)
-            for y_in in range(2):
-                for b in range(3):
-                    tile = band_tile(on_band, coup, stiff, c, b, y, y_in - y)
-                    total -= jnp.dot(
-                        wide(v, 0, 2 * b + y_in), tile, preferred_element_type=f32
-                    )
-            out[0, 2 * c + y] = total
+            spots = [(y_in, b) for y_in in range(2) for b in range(3)]
+            lhs = jnp.concatenate([wide(v, 0, 2 * b + y_in) for y_in, b in spots], axis=1)
+            tiles = [band_tile(on_band, coup, stiff, c, b, y, y_in - y) for y_in, b in spots]
+            total = jnp.dot(lhs, jnp.concatenate(tiles, axis=0), preferred_element_type=f32)
+            out[0, 2 * c + y] = diag * mid.astype(f32) - total
         return carry
 
     lax.fori_loop(0, 3, component, 0)
@@ -111,12 +111,10 @@
 
     def component(c, carry):
         for y in range(2):
-            total = inner[0, 2 * c + y]
-            for b in range(3):
-                lhs = wide(above, 0, b) if y else wide(below, 0, b)
-                tile = band_tile(on_band, coup, stiff, c, b, y, 2 * y - 1)
-                total -= jnp.dot(lhs, tile, preferred_element_type=f32)
-            out[0, 2 * c + y] = total.astype(bf16)
+            lhs = jnp.concatenate([wide(above if y else below, 0, b) for b in range(3)], axis=1)
+            tiles = [band_tile(on_band, coup, stiff, c, b, y, 2 * y - 1) for b in range(3)]
+            total = jnp.dot(lhs, jnp.concatenate(tiles, axis=0), preferred_element_type=f32)
+            out[0, 2 * c + y] = (inner[0, 2 * c + y] - total).astype(bf16)
         return carry
 
     lax.fori_loop(0, 3, component, 0)
@@ -175,14 +173,17 @@
 def own_rows_kernel(s, a, idx, out):
     stacked = a[0].reshape(G * K, L)
 
-    def two_slots(t, carry):
-        rows = jnp.concatenate([idx[2 * t, s : s + 1, :], idx[2 * t + 1, s : s + 1, :]], axis=1)
-        out[:, pl.ds(pl.multiple_of(t * 2 * OV, 128), 2 * OV)] = gather_columns(
-            stacked, rows >> 8, rows & 255
-        )
+    def take(first, count):
+        rows = jnp.concatenate([idx[first + t, s : s + 1, :] for t in range(count)], axis=1)
+        at = pl.ds(pl.multiple_of(first * OV, 128), count * OV)
+        out[:, at] = gather_columns(stacked, rows >> 8, rows & 255)
+
+    def four_slots(t, carry):
+        take(4 * t, 4)
         return carry
 
-    lax.fori_loop(0, NB // 2, two_slots, 0)
+    lax.fori_loop(0, NB // 4, four_slots, 0)
+    take(NB - 2, 2)
 
 
 def early_kernel(v, v_other, back, out):
@@ -228,7 +229,9 @@
     put_shares(blocks, flat, outs)
 
 
-def tables_kernel(neighbours, maps, rows, vt, idx, back, sent_v, slots, order, held, codes):
+def tables_kernel(
+    neighbours, maps, rows, vt, idx, back, sent_v, low, up, slots, order, held, codes
+):
     value = rows[...]
     high = (value >> 9) * 2 + ((value >> 7) & 1)
     value = high * L + ((value >> 8) & 1) * 128 + (value & 127)
@@ -256,8 +259,8 @@
                     held[j, pl.ds(at + t, 1), :] = line[:, 128 * t : 128 * t + 128]
                 slots[jnp.where(none, 112, source * 16 + other * 4 + j)] = n
                 near = other * 8 + jnp.where(source == 0, (other ^ j) - 1, 2 + j)
-                later = (source >> 1) * 32 + other * 8 + (source & 1) * 4 + j
-                spot = jnp.where(source < 6, later, 96 + other * 4 + j)
+                later = jnp.where(source < 4, 32, 80) + other * 8 + (source & 1) * 4 + j
+                spot = jnp.where(source < 6, later, 64 + other * 4 + j)
                 spot = jnp.where(none, -1, jnp.where(source < 2, near, spot))
                 order[pl.ds(n * 4 + j, 1), :] = (lane == spot).astype(f32)
         return carry
@@ -265,6 +268,9 @@
     lax.fori_loop(0, NB // 2, two, 0)
     back[...] = held[:, 112:, :]
     sent_v[:, :12] = vt[...]
+    for c in range(3):
+        low[:, 2 * c : 2 * c + 2] = vt[:, 4 * c : 4 * c + 2]
+        up[:, 2 * c : 2 * c + 2] = vt[:, 4 * c + 2 : 4 * c + 4]
     sent_v[:, 12] = held[:, :K, :].astype(bf16)
 
 
@@ -310,11 +316,6 @@
     n_sub = lax.axis_size("sub")
     smem = pl.BlockSpec(memory_space=pltpu.SMEM)
     vt = jnp.transpose(deflation, (0, 2, 4, 3, 1, 5))
-    vt = lax.optimization_barrier(vt)
-    halo = (SUBS, 6, K, 128)
-    below = lax.ppermute(vt[:, :, 1], "row", [(i, i + 1) for i in range(3)]).reshape(halo)
-    above = lax.ppermute(vt[:, :, 0], "row", [(i + 1, i) for i in range(3)]).reshape(halo)
-
     maps = []
     for tables in ((TARGET_EVEN, SOURCE_EVEN), (TARGET_ODD, SOURCE_ODD)):
         for offsets in tables:
@@ -322,12 +323,14 @@
             for route, offset in enumerate(offsets):
                 line[offset % n_sub] = route
             maps += line
-    idx, back, sent_v, slots, order = call(
+    idx, back, sent_v, low, up, slots, order = call(
         tables_kernel,
         [
             jax.ShapeDtypeStruct((NB, SUBS, OV), i32),
             jax.ShapeDtypeStruct((SUBS, 16, 128), f32),
             jax.ShapeDtypeStruct((SUBS, TILES, K, 128), bf16),
+            jax.ShapeDtypeStruct((SUBS, 6, K, 128), bf16),
+            jax.ShapeDtypeStruct((SUBS, 6, K, 128), bf16),
             jax.ShapeDtypeStruct((128,), i32),
             jax.ShapeDtypeStruct((SUBS * NB, 128), f32),
         ],
@@ -339,6 +342,8 @@
                 whole((NB, SUBS, OV)),
                 whole((SUBS, 16, 128)),
                 whole((SUBS, TILES, K, 128)),
+                whole((SUBS, 6, K, 128)),
+                whole((SUBS, 6, K, 128)),
                 smem,
                 whole((SUBS * NB, 128)),
             ],
@@ -347,6 +352,7 @@
                 pltpu.VMEM((NB, SUBS, OV), f32),
             ],
         ),
+        12,
         2 * 10**9,
         3 << 20,
     )(
@@ -359,6 +365,8 @@
     ring = lambda x, by: lax.ppermute(x, "sub", [(i, (i + by) % n_sub) for i in range(n_sub)])
     swap = lambda x: lax.ppermute(x, "sub", [(i, i ^ 1) for i in range(n_sub)])
     plus2, minus2 = ring(sent_v, -2), ring(sent_v, 2)
+    below = lax.ppermute(up, "row", [(i, i + 1) for i in range(3)])
+    above = lax.ppermute(low, "row", [(i + 1, i) for i in range(3)])
     other = swap(sent_v)
 
     coup = coupling.reshape(26, 9)
@@ -366,6 +374,20 @@
     halo_spec = pl.BlockSpec((1, 6, K, 128), lambda s, *_: (s, 0, 0, 0))
     a_spec = pl.BlockSpec((1, G, K, L), lambda s, *_: (s, 0, 0, 0))
     stiff_spec = pl.BlockSpec((1, 26, 2, 2, 128), lambda s, *_: (s, 0, 0, 0, 0))
+    found = call(
+        early_kernel,
+        jax.ShapeDtypeStruct((SUBS, K, 6 * OV), bf16),
+        pl.GridSpec(
+            grid=(SUBS,),
+            in_specs=[v_spec, v_spec, pl.BlockSpec((1, 16, 128), lambda s: (s, 0, 0))],
+            out_specs=pl.BlockSpec((1, K, 6 * OV), lambda s: (s, 0, 0)),
+        ),
+        10,
+        5 * 10**9,
+        5 << 20,
+    )(sent_v, other, back)
+
+    stiffness, found = lax.optimization_barrier((stiffness, found))
     inner = call(
         inner_kernel,
         jax.ShapeDtypeStruct((SUBS, G, K, L), f32),
@@ -379,23 +401,12 @@
             ],
             out_specs=a_spec,
         ),
+        10,
         5 * 10**9,
         5 << 20,
     )(coup, sent_v, stiffness, center)
 
-    found = call(
-        early_kernel,
-        jax.ShapeDtypeStruct((SUBS, K, 6 * OV), bf16),
-        pl.GridSpec(
-            grid=(SUBS,),
-            in_specs=[v_spec, v_spec, pl.BlockSpec((1, 16, 128), lambda s: (s, 0, 0))],
-            out_specs=pl.BlockSpec((1, K, 6 * OV), lambda s: (s, 0, 0)),
-        ),
-        5 * 10**9,
-        5 << 20,
-    )(sent_v, other, back)
-
-    below, above, found = lax.optimization_barrier((below, above, found))
+    below, above, inner = lax.optimization_barrier((below, above, inner))
     applied = call(
         outer_kernel,
         jax.ShapeDtypeStruct((SUBS, G, K, L), bf16),
@@ -404,6 +415,7 @@
             in_specs=[smem, a_spec, halo_spec, halo_spec, stiff_spec],
             out_specs=a_spec,
         ),
+        10,
         3 * 10**9,
         6 << 20,
     )(coup, inner, below, above, stiffness)
@@ -420,6 +432,7 @@
                 ],
                 out_specs=whole((K, NB * OV)),
             ),
+            12,
             6 * 10**9,
             4 << 20,
         )(applied, idx)
@@ -439,16 +452,15 @@
     def row_spec(route, p, step, q):
         return pl.BlockSpec((K, OV), lambda i, t: (0, t[route * 16 + (p + step * i) * 4 + q]))
 
-    share_specs = lambda n: [pl.BlockSpec((n, SHARE), lambda i, *_: (i, 0))] * 4
     scratch = lambda n: [pltpu.VMEM((n, K, 128), f32), pltpu.VMEM((n, K * K), f32)]
     near = [
         (route, p, 0, q)
         for p in range(SUBS)
         for route, q in [(0, p ^ 1), (0, p ^ 2)] + [(1, q) for q in range(SUBS)]
     ]
-    near_shares = call(
+    near_shares, plus2, minus2, plus2x, minus2x = lax.optimization_barrier((call(
         first_pairs_kernel,
-        share_shapes(CHUNKS[0]),
+        share_shapes(32),
         pltpu.PrefetchScalarGridSpec(
             num_scalar_prefetch=1,
             grid=(1,),
@@ -458,38 +470,45 @@
                 whole((SUBS, TILES, K, 128)),
             ]
             + [row_spec(*spot) for spot in near],
-            out_specs=share_specs(32),
+            out_specs=[pl.BlockSpec((32, SHARE), lambda i, *_: (i, 0))] * 4,
             scratch_shapes=scratch(32),
         ),
+        24,
         3 * 10**9,
         8 << 20,
-    )(slots, found, applied, sent_v, *[own_rows[spot[3]] for spot in near])
+    )(slots, found, applied, sent_v, *[own_rows[spot[3]] for spot in near]), plus2, minus2, plus2x, minus2x))
+    pieces = row_exchange(near_shares)
 
     blocks = [sent_v, other, plus2, minus2, plus2x, minus2x, far]
-    pieces = []
-    for routes in ((2, 3), (4, 5), (6,)):
+    def later_pairs(routes, total, earlier=()):
         n = len(routes)
+        skip = total // 16 - n if earlier else 0
         rows = [
             (route, p, 4 // n, q) for p in range(4 // n) for route in routes for q in range(SUBS)
         ]
-        earlier = near_shares if routes[0] == 2 else []
-        skip = len(earlier) // 2
-        shares = call(
+        return call(
             functools.partial(pairs_kernel, routes, len(earlier)),
-            share_shapes(16 * (n + skip)),
+            share_shapes(total),
             pltpu.PrefetchScalarGridSpec(
                 num_scalar_prefetch=1,
                 grid=(n,),
                 in_specs=[pl.BlockSpec((4 // n, TILES, K, 128), lambda i, t: (i, 0, 0, 0))] * n
                 + [row_spec(*spot) for spot in rows]
                 + [pl.BlockSpec(memory_space=pl.ANY)] * len(earlier),
-                out_specs=[pl.BlockSpec((16, SHARE), lambda i, t, skip=skip: (i + skip, 0))] * 4,
+                out_specs=[pl.BlockSpec((16, SHARE), lambda i, t: (i + skip, 0))] * 4,
                 scratch_shapes=scratch(16),
             ),
+            18,
             n * 5 * 10**9,
             n * 5 << 20,
             {1 + n + 16 + s: s for s in range(len(earlier))},
         )(slots, *[blocks[o] for o in routes], *[own_rows[spot[3]] for spot in rows], *earlier)
+
+    shares = later_pairs((6,), 48, later_pairs((2, 3), 48))
+    shares, blocks[4], blocks[5] = lax.optimization_barrier((shares, blocks[4], blocks[5]))
+    for shares in (list(shares), list(later_pairs((4, 5), 32))):
+        for s in (1, 2, 3):
+            shares[s], pieces[s - 4] = lax.optimization_barrier((shares[s], pieces[s - 4]))
         pieces += row_exchange(shares)
 
     pairs, selfs = call(
@@ -505,6 +524,7 @@
             out_specs=[whole((NB, SUBS, SHARE)), whole((SUBS, SHARE))],
             scratch_shapes=[pltpu.VMEM((128, SHARE), f32)],
         ),
+        16,
         10**7,
         4 << 20,
     )(order, *pieces)

time: 110 us -> 105 us (0.955)
  waiting for transfers between devices: 4.43 us -> 10.9 us
  Pallas kernels: 66.8 us -> 61.5 us
  local copies, waits for them, and re-layouts: 5.06 us -> 1.69 us
  starting transfers between devices: 31.8 us -> 29.3 us
    pallas_call x4, Pallas kernels: 21.5 us -> 17.1 us  [take_rows(): call(functools.partial(own_rows_kernel, s), jax.ShapeDtypeStruct((K, NB *...]
    ppermute x9, waiting for transfers between devices: 2.03 us -> 6.37 us  [row_exchange(): lax.ppermute(shares[s], 'row', [(i, (i + s) % 4) for i in range(4)])]
    unnamed x21 -> x12, local copies, waits for them, and re-layouts: 3.78 us -> 0.03 us
    ppermute x9, starting transfers between devices: 15.1 us -> 11.9 us  [row_exchange(): lax.ppermute(shares[s], 'row', [(i, (i + s) % 4) for i in range(4)])]
    ppermute x2, waiting for transfers between devices: 2.38 us -> 4.56 us  [the longest x1 4.55 us: on_device(): above = lax.ppermute(low, 'row', [(i + 1, i) for i in range(3)])]
    transpose x0 -> x1, local copies, waits for them, and re-layouts: none -> 1.56 us  [on_device(): vt = jnp.transpose(deflation, (0, 2, 4, 3, 1, 5))]
  transfers between devices with their start and end apart: 17 -> 17, of which waited for: 3 -> 4; matrix products, arithmetic and copies ran while one was open for 1% -> 0% of each run, Pallas kernels for 52% -> 54%
where the time goes in v3:
time: 105 us
  Pallas kernels  61.5 us (59%)
  starting transfers between devices  29.3 us (28%)
  waiting for transfers between devices  10.9 us (10%)
  local copies, waits for them, and re-layouts  1.69 us (2%)
    pallas_call x3, Pallas kernels, later_pairs(): call(functools.partial(pairs_kernel, routes, len(earlier)), share_shapes(...  19.5 us
    pallas_call x4, Pallas kernels, take_rows(): call(functools.partial(own_rows_kernel, s), jax.ShapeDtypeStruct((K, NB *...  17.1 us
    ppermute x9, starting transfers between devices, row_exchange(): lax.ppermute(shares[s], 'row', [(i, (i + s) % 4) for i in range(4)])  11.9 us
    ppermute x2, starting transfers between devices, on_device(): lax.ppermute(x, 'sub', [(i, (i + by) % n_sub) for i in range(n_sub)])  6.39 us
    ppermute x9, waiting for transfers between devices, row_exchange(): lax.ppermute(shares[s], 'row', [(i, (i + s) % 4) for i in range(4)])  6.37 us
    pallas_call x1, Pallas kernels, on_device(): call(inner_kernel, jax.ShapeDtypeStruct((SUBS, G, K, L), f32), pl.GridSpe...  6.15 us
    pallas_call x1, Pallas kernels, on_device(): call(early_kernel, jax.ShapeDtypeStruct((SUBS, K, 6 * OV), bf16), pl.Grid...  4.93 us
    pallas_call x1, Pallas kernels, on_device(): call(outer_kernel, jax.ShapeDtypeStruct((SUBS, G, K, L), bf16), pl.GridSp...  4.88 us
  transfers between devices with their start and end apart: 17, of which 4 were waited for; matrix products, arithmetic and copies ran while one was open for 0% of the time, Pallas kernels for 54%

profile of v3, /device:TPU:0, one launch (start us, length us, event | category | flops | bytes accessed | tf_op | source)
XLA Modules:
  0.0 104.6 jit_solution(8022640289475885084)
XLA Ops:
  2.3 3.7 %shard_map.86 = (s32[26,4,384]{2,1,0:T(4,128)S(1)}, f32[4,16,128]{2,1,0:T(8,128)S(1)}, bf16[4,13,96,128]{3,2,1,0:T(8,128)(2,1)}, bf16[4,6,96,128]{3,2,1,0:T(8,12...) custom-call(s32[4,26]{1,0:T(4,128)S(1)} %copy-done.3, s32[128]{0:T(128)S(1)} %copy-done.4, ...), custom_call_target="tpu_custom_call" | custom-call | flops 2000000000 | bytes 3145728 | tf_op jit(solution)/shard_map/pallas_call | solution.py:326
  6.0 6.4 %collective-permute-start.3 = (bf16[4,13,96,128]{3,2,1,0:T(8,128)(2,1)}, bf16[4,13,96,128]{3,2,1,0:T(8,128)(2,1)S(1)}, u32[]{:S(2)}, u32[]{:S(2)}) collective-permute-start(bf16[4,13,96,128]{3,2,1,0:T(8,128)(2,1)} %get-tuple-element.64.v), channel_id=1, source_target_pairs={{0,120},{4,124},{8,0},{12,4},{16,8},{20,12},{24,16},{28,20},{32,24... | collective-permute-start | bytes 3833864 | tf_op jit(solution)/shard_map/ppermute | solution.py:365
  12.4 4.3 %collective-permute-start.1 = (bf16[4,6,96,128]{3,2,1,0:T(8,128)(2,1)}, bf16[4,6,96,128]{3,2,1,0:T(8,128)(2,1)}, u32[]{:S(2)}, u32[]{:S(2)}) collective-permute-start(bf16[4,6,96,128]{3,2,1,0:T(8,128)(2,1)} %get-tuple-element.67), channel_id=1, source_target_pairs={{0,1},{1,2},{2,3},{4,5},{5,6},{6,7},{8,9},{9,10},{10,11},{12,13},{... | collective-permute-start | bytes 1769480 | tf_op jit(solution)/shard_map/ppermute | solution.py:368
  18.2 4.9 %shard_map.87.found = bf16[4,96,2304]{2,1,0:T(8,128)(2,1)S(1)} custom-call(bf16[4,13,96,128]{3,2,1,0:T(8,128)(2,1)} %get-tuple-element.64.v, bf16[4,13,96,128]{3,2,1,0:T(8,128)(2,1)} %collective-permute-done.v_other, f32[4,16,128]{2,1,0:T(8,128)S(1)} %get-tuple-element.65.back), custom_call_target="tpu_custom_call" | custom-call | flops 5000000000 | bytes 5242880 | tf_op jit(solution)/shard_map/pallas_call | solution.py:377
  23.1 6.1 %shard_map.88.inner = f32[4,6,96,256]{3,2,1,0:T(8,128)S(1)} custom-call(f32[26,9]{1,0:T(8,128)S(1)} %copy.17.coup, bf16[4,13,96,128]{3,2,1,0:T(8,128)(2,1)} %get-tuple-element.64.v, f32[4,26,2,2,128]{4,3,2,1,0:T(2,128)S(1)} %copy-done, f32[4,2,2,128]{3,2,1,0:T(2,128)S(1)} %copy-done.2), custom_call_target="tpu_custom_call" | custom-call | flops 5000000000 | bytes 5242880 | tf_op jit(solution)/shard_map/pallas_call | solution.py:391
  29.3 4.6 %collective-permute-done.2.above = bf16[4,6,96,128]{3,2,1,0:T(8,128)(2,1)} collective-permute-done((bf16[4,6,96,128]{3,2,1,0:T(8,128)(2,1)S(1)}, bf16[4,6,96,128]{3,2,1,0:T(8,128)(2,1)}, u32[]{:S(2)}, u32[]{:S(2)}) %collective-permute-start.2) | collective-permute-done | bytes 589856 | tf_op jit(solution)/shard_map/ppermute | solution.py:369
  33.8 4.9 %shard_map.89.a = bf16[4,6,96,256]{3,2,1,0:T(8,128)(2,1)S(1)} custom-call(f32[26,9]{1,0:T(8,128)S(1)} %copy.17.coup, f32[4,6,96,256]{3,2,1,0:T(8,128)S(1)} %shard_map.88.inner, bf16[4,6,96,128]{3,2,1,0:T(8,128)(2,1)} %collective-permute-done.1.below, bf16[4,6,96,128]{3,2,1,0:T(8,128)(2,1)} %collective-permute-done.2.above, f32[4,26,2,2,128]{4,3,2,1,0:T(2,128)S(1)} %copy-done), custom_call_target="tpu_custom_call" | custom-call | flops 3000000000 | bytes 6291456 | tf_op jit(solution)/shard_map/pallas_call | solution.py:410
  38.7 4.3 %shard_map.91.refs_1_.refs_4_.refs_10_.refs_16_.refs_18_.refs_22_.refs_8_.refs_12_.refs_3_.refs_7_.refs_11_.refs_15_ = bf16[96,9984]{1,0:T(8,128)(2,1)S(1)} custom-call(bf16[4,6,96,256]{3,2,1,0:T(8,128)(2,1)S(1)} %shard_map.89.a, s32[26,4,384]{2,1,0:T(4,128)S(1)} %get-tuple-element.75.idx), custom_call_target="tpu_custom_call" | custom-call | flops 6000000000 | bytes 4194304 | tf_op jit(solution)/shard_map/pallas_call | solution.py:424
  43.0 4.3 %shard_map.92.refs_2_.refs_6_.refs_8_.refs_13_.refs_14_.refs_20_.refs_10_.refs_1_.refs_5_.refs_9_ = bf16[96,9984]{1,0:T(8,128)(2,1)S(1)} custom-call(bf16[4,6,96,256]{3,2,1,0:T(8,128)(2,1)S(1)} %shard_map.89.a, s32[26,4,384]{2,1,0:T(4,128)S(1)} %get-tuple-element.75.idx), custom_call_target="tpu_custom_call" | custom-call | flops 6000000000 | bytes 4194304 | tf_op jit(solution)/shard_map/pallas_call | solution.py:424
  48.0 4.9 %collective-permute-start.7 = (bf16[4,13,96,128]{3,2,1,0:T(8,128)(2,1)S(1)}, bf16[4,13,96,128]{3,2,1,0:T(8,128)(2,1)S(1)}, u32[]{:S(2)}, u32[]{:S(2)}) collective-permute-start(bf16[4,13,96,128]{3,2,1,0:T(8,128)(2,1)S(1)} %broadcast_select_fusion), channel_id=1, source_target_pairs={{0,124},{4,8},{8,4},{12,16},{16,12},{20,24},{24,20},{28,32},{32,28... | collective-permute-start | bytes 3833864 | tf_op jit(solution)/shard_map/ppermute | solution.py:445
  52.9 4.3 %shard_map.90.refs_0_.refs_3_.refs_9_.refs_15_.refs_19_.refs_21_.refs_7_.refs_11_.refs_2_.refs_6_.refs_10_.refs_14_ = bf16[96,9984]{1,0:T(8,128)(2,1)S(1)} custom-call(bf16[4,6,96,256]{3,2,1,0:T(8,128)(2,1)S(1)} %shard_map.89.a, s32[26,4,384]{2,1,0:T(4,128)S(1)} %get-tuple-element.75.idx), custom_call_target="tpu_custom_call" | custom-call | flops 6000000000 | bytes 4194304 | tf_op jit(solution)/shard_map/pallas_call | solution.py:424
  57.2 4.3 %shard_map.93.refs_5_.refs_7_.refs_11_.refs_12_.refs_17_.refs_23_.refs_9_.refs_13_.refs_4_.refs_8_.refs_16_ = bf16[96,9984]{1,0:T(8,128)(2,1)S(1)} custom-call(bf16[4,6,96,256]{3,2,1,0:T(8,128)(2,1)S(1)} %shard_map.89.a, s32[26,4,384]{2,1,0:T(4,128)S(1)} %get-tuple-element.75.idx), custom_call_target="tpu_custom_call" | custom-call | flops 6000000000 | bytes 4194304 | tf_op jit(solution)/shard_map/pallas_call | solution.py:424
  61.5 3.6 %shard_map.94 = (f32[32,2304]{1,0:T(8,128)S(1)}, bf16[32,2304]{1,0:T(8,128)(2,1)S(1)}, bf16[32,2304]{1,0:T(8,128)(2,1)S(1)}, bf16[32,2304]{1,0:T(8,128)(2,1)S(1)}) custom-call(s32[128]{0:T(128)S(1)} %get-tuple-element.63.slots, bf16[4,96,2304]{2,1,0:T(8,128)(2,1)S(1)} %shard_map.87.found, bf16[4,6,96,256]{3,2,1,0:T(8,128)(2,1)S(1)} %shard_map.89.a, ...), custom_call_target="tpu_custom_call" | custom-call | flops 3000000000 | bytes 8388608 | tf_op jit(solution)/shard_map/pallas_call | solution.py:461
  65.3 2.7 %collective-permute-start.9 = (bf16[32,2304]{1,0:T(8,128)(2,1)S(1)}, bf16[32,2304]{1,0:T(8,128)(2,1)S(1)}, u32[]{:S(2)}, u32[]{:S(2)}) collective-permute-start(bf16[32,2304]{1,0:T(8,128)(2,1)S(1)} %get-tuple-element.99), channel_id=1, source_target_pairs={{0,2},{1,3},{2,0},{3,1},{4,6},{5,7},{6,4},{7,5},{8,10},{9,11},{10,... | collective-permute-start | bytes 442376 | tf_op jit(solution)/shard_map/ppermute | solution.py:307
  68.7 7.8 %shard_map.95 = (f32[48,2304]{1,0:T(8,128)S(1)}, bf16[48,2304]{1,0:T(8,128)(2,1)S(1)}, bf16[48,2304]{1,0:T(8,128)(2,1)S(1)}, bf16[48,2304]{1,0:T(8,128)(2,1)S(1)}) custom-call(s32[128]{0:T(128)S(1)} %get-tuple-element.63.slots, bf16[4,13,96,128]{3,2,1,0:T(8,128)(2,1)S(1)} %collective-permute-done.3.refs_0_, ...), custom_call_target="tpu_custom_call" | custom-call | flops 10000000000 | bytes 10485760 | tf_op jit(solution)/shard_map/pallas_call | solution.py:489
  76.5 3.8 %shard_map.96 = (f32[48,2304]{1,0:T(8,128)S(1)}, bf16[48,2304]{1,0:T(8,128)(2,1)S(1)}, bf16[48,2304]{1,0:T(8,128)(2,1)S(1)}, bf16[48,2304]{1,0:T(8,128)(2,1)S(1)}) custom-call(s32[128]{0:T(128)S(1)} %get-tuple-element.63.slots, ...), custom_call_target="tpu_custom_call", output_to_operand_aliasing={{0}: (18, {}), {1}: (19, {}), {2}: (20, {}), {3}: (21, {})} | custom-call | flops 5000000000 | bytes 5242880 | tf_op jit(solution)/shard_map/pallas_call | solution.py:489
  80.4 2.6 %collective-permute-start.13 = (bf16[48,2304]{1,0:T(8,128)(2,1)S(1)}, bf16[48,2304]{1,0:T(8,128)(2,1)S(1)}, u32[]{:S(2)}, u32[]{:S(2)}) collective-permute-start(bf16[48,2304]{1,0:T(8,128)(2,1)S(1)} %get-tuple-element.114), channel_id=1, source_target_pairs={{0,3},{1,0},{2,1},{3,2},{4,7},{5,4},{6,5},{7,6},{8,11},{9,8},{10,9... | collective-permute-start | bytes 663560 | tf_op jit(solution)/shard_map/ppermute | solution.py:307
  84.5 7.9 %shard_map.97 = (f32[32,2304]{1,0:T(8,128)S(1)}, bf16[32,2304]{1,0:T(8,128)(2,1)S(1)}, bf16[32,2304]{1,0:T(8,128)(2,1)S(1)}, bf16[32,2304]{1,0:T(8,128)(2,1)S(1)}) custom-call(s32[128]{0:T(128)S(1)} %get-tuple-element.63.slots, bf16[4,13,96,128]{3,2,1,0:T(8,128)(2,1)S(1)} %collective-permute-done.5.refs_0_, ...), custom_call_target="tpu_custom_call" | custom-call | flops 10000000000 | bytes 10485760 | tf_op jit(solution)/shard_map/pallas_call | solution.py:489
  92.4 2.0 %collective-permute-start.16 = (bf16[32,2304]{1,0:T(8,128)(2,1)S(1)}, bf16[32,2304]{1,0:T(8,128)(2,1)S(1)}, u32[]{:S(2)}, u32[]{:S(2)}) collective-permute-start(bf16[32,2304]{1,0:T(8,128)(2,1)S(1)} %get-tuple-element.119), channel_id=1, source_target_pairs={{0,3},{1,0},{2,1},{3,2},{4,7},{5,4},{6,5},{7,6},{8,11},{9,8},{10,9... | collective-permute-start | bytes 442376 | tf_op jit(solution)/shard_map/ppermute | solution.py:307
  94.4 2.1 %collective-permute-start.15 = (bf16[32,2304]{1,0:T(8,128)(2,1)S(1)}, bf16[32,2304]{1,0:T(8,128)(2,1)S(1)}, u32[]{:S(2)}, u32[]{:S(2)}) collective-permute-start(bf16[32,2304]{1,0:T(8,128)(2,1)S(1)} %get-tuple-element.118), channel_id=1, source_target_pairs={{0,2},{1,3},{2,0},{3,1},{4,6},{5,7},{6,4},{7,5},{8,10},{9,11},{10,... | collective-permute-start | bytes 442376 | tf_op jit(solution)/shard_map/ppermute | solution.py:307
  96.5 2.1 %collective-permute-done.16.refs_11_ = bf16[32,2304]{1,0:T(8,128)(2,1)S(1)} collective-permute-done((bf16[32,2304]{1,0:T(8,128)(2,1)S(1)}, bf16[32,2304]{1,0:T(8,128)(2,1)S(1)}, u32[]{:S(2)}, u32[]{:S(2)}) %collective-permute-start.16) | collective-permute-done | bytes 147488 | tf_op jit(solution)/shard_map/ppermute | solution.py:307
  98.7 2.4 %collective-permute-done.15.refs_10_ = bf16[32,2304]{1,0:T(8,128)(2,1)S(1)} collective-permute-done((bf16[32,2304]{1,0:T(8,128)(2,1)S(1)}, bf16[32,2304]{1,0:T(8,128)(2,1)S(1)}, u32[]{:S(2)}, u32[]{:S(2)}) %collective-permute-start.15) | collective-permute-done | bytes 147488 | tf_op jit(solution)/shard_map/ppermute | solution.py:307
  101.0 1.8 %collective-permute-done.14.refs_9_ = bf16[32,2304]{1,0:T(8,128)(2,1)S(1)} collective-permute-done((bf16[32,2304]{1,0:T(8,128)(2,1)S(1)}, bf16[32,2304]{1,0:T(8,128)(2,1)S(1)}, u32[]{:S(2)}, u32[]{:S(2)}) %collective-permute-start.14) | collective-permute-done | bytes 147488 | tf_op jit(solution)/shard_map/ppermute | solution.py:307
  102.9 1.7 %shard_map.98 = (f32[26,4,2304]{2,1,0:T(4,128)}, f32[4,2304]{1,0:T(4,128)}) custom-call(f32[104,128]{1,0:T(8,128)S(1)} %get-tuple-element.62.order, f32[32,2304]{1,0:T(8,128)S(1)} %get-tuple-element.82.refs_0_, bf16[32,2304]{1,0:T(8,128)(2,1)S(1)} %collective-permute-done.8.refs_1_, bf16[32,2304]{1,0:T(8,128)(2,1)S(1)} %collective-permute-done.9.refs_2_, ...), custom_call_target="tpu_custom_call" | custom-call | flops 10000000 | bytes 4194304 | tf_op jit(solution)/shard_map/pallas_call | solution.py:514
  (39 shorter events, 6.2 us)
Async XLA Ops:
  0.6 1.6 %copy-start.4 = (s32[128]{0:T(128)S(1)}, s32[128]{0:T(128)}, u32[]{:S(2)}) copy-start(s32[128]{0:T(128)} %constant.22.clone.maps) | copy-start | bytes 1540
  0.6 1.6 %copy-start.1 = (s32[4,26,384]{2,0,1:T(4,128)S(1)}, s32[4,26,384]{2,0,1:T(4,128)}, u32[]{:S(2)}) copy-start(s32[4,26,384]{2,0,1:T(4,128)} %param.12) | copy-start | bytes 479236
  0.7 1.6 %copy-start.3 = (s32[4,26]{1,0:T(4,128)S(1)}, s32[4,26]{1,0:T(4,128)}, u32[]{:S(2)}) copy-start(s32[4,26]{1,0:T(4,128)} %neighbours.1) | copy-start | bytes 1252
  2.3 15.8 %copy-start.5 = (f32[26,3,3]{0,2,1:T(4,128)S(1)}, f32[26,3,3]{0,2,1:T(4,128)}, u32[]{:S(2)}) copy-start(f32[26,3,3]{0,2,1:T(4,128)} %param.10) | copy-start | bytes 2812
  6.0 12.2 %collective-permute-start = (bf16[4,13,96,128]{3,2,1,0:T(8,128)(2,1)}, bf16[4,13,96,128]{3,2,1,0:T(8,128)(2,1)}, u32[]{:S(2)}, u32[]{:S(2)}) collective-permute-start(bf16[4,13,96,128]{3,2,1,0:T(8,128)(2,1)} %get-tuple-element.64.v), channel_id=1, source_target_pairs={{0,4},{4,0},{8,12},{12,8},{16,20},{20,16},{24,28},{28,24},{32,36},... | collective-permute-start | bytes 3833864 | tf_op jit(solution)/shard_map/ppermute | solution.py:366
  6.0 41.3 %collective-permute-start.3 = (bf16[4,13,96,128]{3,2,1,0:T(8,128)(2,1)}, bf16[4,13,96,128]{3,2,1,0:T(8,128)(2,1)S(1)}, u32[]{:S(2)}, u32[]{:S(2)}) collective-permute-start(bf16[4,13,96,128]{3,2,1,0:T(8,128)(2,1)} %get-tuple-element.64.v), channel_id=1, source_target_pairs={{0,120},{4,124},{8,0},{12,4},{16,8},{20,12},{24,16},{28,20},{32,24... | collective-permute-start | bytes 3833864 | tf_op jit(solution)/shard_map/ppermute | solution.py:365
  12.4 34.9 %collective-permute-start.4 = (bf16[4,13,96,128]{3,2,1,0:T(8,128)(2,1)}, bf16[4,13,96,128]{3,2,1,0:T(8,128)(2,1)S(1)}, u32[]{:S(2)}, u32[]{:S(2)}) collective-permute-start(bf16[4,13,96,128]{3,2,1,0:T(8,128)(2,1)} %get-tuple-element.64.v), channel_id=1, source_target_pairs={{0,8},{4,12},{8,16},{12,20},{16,24},{20,28},{24,32},{28,36},{32,40... | collective-permute-start | bytes 3833864 | tf_op jit(solution)/shard_map/ppermute | solution.py:365
  12.4 16.8 %collective-permute-start.1 = (bf16[4,6,96,128]{3,2,1,0:T(8,128)(2,1)}, bf16[4,6,96,128]{3,2,1,0:T(8,128)(2,1)}, u32[]{:S(2)}, u32[]{:S(2)}) collective-permute-start(bf16[4,6,96,128]{3,2,1,0:T(8,128)(2,1)} %get-tuple-element.67), channel_id=1, source_target_pairs={{0,1},{1,2},{2,3},{4,5},{5,6},{6,7},{8,9},{9,10},{10,11},{12,13},{... | collective-permute-start | bytes 1769480 | tf_op jit(solution)/shard_map/ppermute | solution.py:368
  16.7 17.1 %collective-permute-start.2 = (bf16[4,6,96,128]{3,2,1,0:T(8,128)(2,1)S(1)}, bf16[4,6,96,128]{3,2,1,0:T(8,128)(2,1)}, u32[]{:S(2)}, u32[]{:S(2)}) collective-permute-start(bf16[4,6,96,128]{3,2,1,0:T(8,128)(2,1)S(1)} %get-tuple-element.68), channel_id=1, source_target_pairs={{1,0},{2,1},{3,2},{5,4},{6,5},{7,6},{9,8},{10,9},{11,10},{13,12},{... | collective-permute-start | bytes 1769480 | tf_op jit(solution)/shard_map/ppermute | solution.py:369
  18.2 4.9 %copy-start = (f32[4,26,2,2,128]{4,3,2,1,0:T(2,128)S(1)}, f32[4,26,2,2,128]{4,3,2,1,0:T(2,128)}, u32[]{:S(2)}) copy-start(f32[4,26,2,2,128]{4,3,2,1,0:T(2,128)} %stiff.1) | copy-start | bytes 638980
  18.2 5.0 %copy-start.2 = (f32[4,2,2,128]{3,2,1,0:T(2,128)S(1)}, f32[4,2,2,128]{3,2,1,0:T(2,128)}, u32[]{:S(2)}) copy-start(f32[4,2,2,128]{3,2,1,0:T(2,128)} %center.1) | copy-start | bytes 24580
  47.3 17.8 %collective-permute-start.5 = (bf16[4,13,96,128]{3,2,1,0:T(8,128)(2,1)S(1)}, bf16[4,13,96,128]{3,2,1,0:T(8,128)(2,1)S(1)}, u32[]{:S(2)}, u32[]{:S(2)}) collective-permute-start(bf16[4,13,96,128]{3,2,1,0:T(8,128)(2,1)S(1)} %collective-permute-done.3.refs_0_), channel_id=1, source_target_pairs={{0,4},{4,0},{8,12},{12,8},{16,20},{20,16},{24,28},{28,24},{32,36},... | collective-permute-start | bytes 3833864 | tf_op jit(solution)/shard_map/ppermute | solution.py:366
  47.4 17.7 %collective-permute-start.6 = (bf16[4,13,96,128]{3,2,1,0:T(8,128)(2,1)S(1)}, bf16[4,13,96,128]{3,2,1,0:T(8,128)(2,1)S(1)}, u32[]{:S(2)}, u32[]{:S(2)}) collective-permute-start(bf16[4,13,96,128]{3,2,1,0:T(8,128)(2,1)S(1)} %collective-permute-done.4.refs_1_), channel_id=1, source_target_pairs={{0,4},{4,0},{8,12},{12,8},{16,20},{20,16},{24,28},{28,24},{32,36},... | collective-permute-start | bytes 3833864 | tf_op jit(solution)/shard_map/ppermute | solution.py:366
  48.0 28.5 %collective-permute-start.7 = (bf16[4,13,96,128]{3,2,1,0:T(8,128)(2,1)S(1)}, bf16[4,13,96,128]{3,2,1,0:T(8,128)(2,1)S(1)}, u32[]{:S(2)}, u32[]{:S(2)}) collective-permute-start(bf16[4,13,96,128]{3,2,1,0:T(8,128)(2,1)S(1)} %broadcast_select_fusion), channel_id=1, source_target_pairs={{0,124},{4,8},{8,4},{12,16},{16,12},{20,24},{24,20},{28,32},{32,28... | collective-permute-start | bytes 3833864 | tf_op jit(solution)/shard_map/ppermute | solution.py:445
  65.1 15.2 %collective-permute-start.10 = (bf16[32,2304]{1,0:T(8,128)(2,1)S(1)}, bf16[32,2304]{1,0:T(8,128)(2,1)S(1)}, u32[]{:S(2)}, u32[]{:S(2)}) collective-permute-start(bf16[32,2304]{1,0:T(8,128)(2,1)S(1)} %get-tuple-element.102), channel_id=1, source_target_pairs={{0,3},{1,0},{2,1},{3,2},{4,7},{5,4},{6,5},{7,6},{8,11},{9,8},{10,9... | collective-permute-start | bytes 442376 | tf_op jit(solution)/shard_map/ppermute | solution.py:307
  65.3 17.7 %collective-permute-start.9 = (bf16[32,2304]{1,0:T(8,128)(2,1)S(1)}, bf16[32,2304]{1,0:T(8,128)(2,1)S(1)}, u32[]{:S(2)}, u32[]{:S(2)}) collective-permute-start(bf16[32,2304]{1,0:T(8,128)(2,1)S(1)} %get-tuple-element.99), channel_id=1, source_target_pairs={{0,2},{1,3},{2,0},{3,1},{4,6},{5,7},{6,4},{7,5},{8,10},{9,11},{10,... | collective-permute-start | bytes 442376 | tf_op jit(solution)/shard_map/ppermute | solution.py:307
  68.0 15.2 %collective-permute-start.8 = (bf16[32,2304]{1,0:T(8,128)(2,1)S(1)}, bf16[32,2304]{1,0:T(8,128)(2,1)S(1)}, u32[]{:S(2)}, u32[]{:S(2)}) collective-permute-start(bf16[32,2304]{1,0:T(8,128)(2,1)S(1)} %get-tuple-element.96), channel_id=1, source_target_pairs={{0,1},{1,2},{2,3},{3,0},{4,5},{5,6},{6,7},{7,4},{8,9},{9,10},{10,1... | collective-permute-start | bytes 442376 | tf_op jit(solution)/shard_map/ppermute | solution.py:307
  80.4 12.0 %collective-permute-start.13 = (bf16[48,2304]{1,0:T(8,128)(2,1)S(1)}, bf16[48,2304]{1,0:T(8,128)(2,1)S(1)}, u32[]{:S(2)}, u32[]{:S(2)}) collective-permute-start(bf16[48,2304]{1,0:T(8,128)(2,1)S(1)} %get-tuple-element.114), channel_id=1, source_target_pairs={{0,3},{1,0},{2,1},{3,2},{4,7},{5,4},{6,5},{7,6},{8,11},{9,8},{10,9... | collective-permute-start | bytes 663560 | tf_op jit(solution)/shard_map/ppermute | solution.py:307
  83.0 11.4 %collective-permute-start.12 = (bf16[48,2304]{1,0:T(8,128)(2,1)S(1)}, bf16[48,2304]{1,0:T(8,128)(2,1)S(1)}, u32[]{:S(2)}, u32[]{:S(2)}) collective-permute-start(bf16[48,2304]{1,0:T(8,128)(2,1)S(1)} %get-tuple-element.111), channel_id=1, source_target_pairs={{0,2},{1,3},{2,0},{3,1},{4,6},{5,7},{6,4},{7,5},{8,10},{9,11},{10,... | collective-permute-start | bytes 663560 | tf_op jit(solution)/shard_map/ppermute | solution.py:307
  83.2 13.3 %collective-permute-start.11 = (bf16[48,2304]{1,0:T(8,128)(2,1)S(1)}, bf16[48,2304]{1,0:T(8,128)(2,1)S(1)}, u32[]{:S(2)}, u32[]{:S(2)}) collective-permute-start(bf16[48,2304]{1,0:T(8,128)(2,1)S(1)} %get-tuple-element.108), channel_id=1, source_target_pairs={{0,1},{1,2},{2,3},{3,0},{4,5},{5,6},{6,7},{7,4},{8,9},{9,10},{10,1... | collective-permute-start | bytes 663560 | tf_op jit(solution)/shard_map/ppermute | solution.py:307
  92.4 6.3 %collective-permute-start.16 = (bf16[32,2304]{1,0:T(8,128)(2,1)S(1)}, bf16[32,2304]{1,0:T(8,128)(2,1)S(1)}, u32[]{:S(2)}, u32[]{:S(2)}) collective-permute-start(bf16[32,2304]{1,0:T(8,128)(2,1)S(1)} %get-tuple-element.119), channel_id=1, source_target_pairs={{0,3},{1,0},{2,1},{3,2},{4,7},{5,4},{6,5},{7,6},{8,11},{9,8},{10,9... | collective-permute-start | bytes 442376 | tf_op jit(solution)/shard_map/ppermute | solution.py:307
  94.4 6.6 %collective-permute-start.15 = (bf16[32,2304]{1,0:T(8,128)(2,1)S(1)}, bf16[32,2304]{1,0:T(8,128)(2,1)S(1)}, u32[]{:S(2)}, u32[]{:S(2)}) collective-permute-start(bf16[32,2304]{1,0:T(8,128)(2,1)S(1)} %get-tuple-element.118), channel_id=1, source_target_pairs={{0,2},{1,3},{2,0},{3,1},{4,6},{5,7},{6,4},{7,5},{8,10},{9,11},{10,... | collective-permute-start | bytes 442376 | tf_op jit(solution)/shard_map/ppermute | solution.py:307
  96.5 6.4 %collective-permute-start.14 = (bf16[32,2304]{1,0:T(8,128)(2,1)S(1)}, bf16[32,2304]{1,0:T(8,128)(2,1)S(1)}, u32[]{:S(2)}, u32[]{:S(2)}) collective-permute-start(bf16[32,2304]{1,0:T(8,128)(2,1)S(1)} %get-tuple-element.117), channel_id=1, source_target_pairs={{0,1},{1,2},{2,3},{3,0},{4,5},{5,6},{6,7},{7,4},{8,9},{9,10},{10,1... | collective-permute-start | bytes 442376 | tf_op jit(solution)/shard_map/ppermute | solution.py:307

commit v4 on v3

--- a/solution.py
+++ b/solution.py
@@ -383,8 +383,8 @@
             out_specs=pl.BlockSpec((1, K, 6 * OV), lambda s: (s, 0, 0)),
         ),
         10,
-        5 * 10**9,
-        5 << 20,
+        10**8,
+        1 << 18,
     )(sent_v, other, back)
 
     stiffness, found = lax.optimization_barrier((stiffness, found))
@@ -402,8 +402,8 @@
             out_specs=a_spec,
         ),
         10,
-        5 * 10**9,
-        5 << 20,
+        10**8,
+        1 << 18,
     )(coup, sent_v, stiffness, center)
 
     below, above, inner = lax.optimization_barrier((below, above, inner))

time: 105 us -> 107 us (1.019)
  waiting for transfers between devices: 10.9 us -> 16.8 us
  starting transfers between devices: 29.3 us -> 27.5 us
  Pallas kernels: 61.5 us -> 60 us
    ppermute x2, waiting for transfers between devices: 0.01 us -> 9.04 us  [on_device(): lax.ppermute(x, 'sub', [(i, (i + by) % n_sub) for i in range(n_sub)])]
    ppermute x1, waiting for transfers between devices: 4.55 us -> 0.01 us  [on_device(): above = lax.ppermute(low, 'row', [(i + 1, i) for i in range(3)])]
    ppermute x1, starting transfers between devices: 4.85 us -> 1.17 us  [on_device(): lax.ppermute(jnp.where(lax.axis_index('sub') % 2 == 0, plus2, minus2), 's...]
    ppermute x9, starting transfers between devices: 11.9 us -> 13.7 us  [row_exchange(): lax.ppermute(shares[s], 'row', [(i, (i + s) % 4) for i in range(4)])]
    ppermute x9, waiting for transfers between devices: 6.37 us -> 7.76 us  [row_exchange(): lax.ppermute(shares[s], 'row', [(i, (i + s) % 4) for i in range(4)])]
    pallas_call x1, Pallas kernels: 3.62 us -> 2.43 us  [on_device(): call(first_pairs_kernel, share_shapes(32), pltpu.PrefetchScalarGridSpec(n...]
  transfers between devices with their start and end apart: 17 -> 17, of which waited for: 4 -> 5; matrix products, arithmetic and copies ran while one was open for 0% -> 0% of each run, Pallas kernels for 54% -> 51%
where the time goes in v4:
time: 107 us
  Pallas kernels  60 us (56%)
  starting transfers between devices  27.5 us (26%)
  waiting for transfers between devices  16.8 us (16%)
  local copies, waits for them, and re-layouts  1.69 us (2%)
    pallas_call x3, Pallas kernels, later_pairs(): call(functools.partial(pairs_kernel, routes, len(earlier)), share_shapes(...  20 us
    pallas_call x4, Pallas kernels, take_rows(): call(functools.partial(own_rows_kernel, s), jax.ShapeDtypeStruct((K, NB *...  17.1 us
    ppermute x9, starting transfers between devices, row_exchange(): lax.ppermute(shares[s], 'row', [(i, (i + s) % 4) for i in range(4)])  13.7 us
    ppermute x2, waiting for transfers between devices, on_device(): lax.ppermute(x, 'sub', [(i, (i + by) % n_sub) for i in range(n_sub)])  9.04 us
    ppermute x9, waiting for transfers between devices, row_exchange(): lax.ppermute(shares[s], 'row', [(i, (i + s) % 4) for i in range(4)])  7.76 us
    ppermute x2, starting transfers between devices, on_device(): lax.ppermute(x, 'sub', [(i, (i + by) % n_sub) for i in range(n_sub)])  6.3 us
    pallas_call x1, Pallas kernels, on_device(): call(inner_kernel, jax.ShapeDtypeStruct((SUBS, G, K, L), f32), pl.GridSpe...  5.94 us
    pallas_call x1, Pallas kernels, on_device(): call(outer_kernel, jax.ShapeDtypeStruct((SUBS, G, K, L), bf16), pl.GridSp...  4.87 us
  transfers between devices with their start and end apart: 17, of which 5 were waited for; matrix products, arithmetic and copies ran while one was open for 0% of the time, Pallas kernels for 51%

profile of v4, /device:TPU:0, one launch (start us, length us, event | category | flops | bytes accessed | tf_op | source)
XLA Modules:
  0.0 107.0 jit_solution(2212411002021171607)
XLA Ops:
  0.7 1.6 %copy.15 = bf16[4,3,2,2,96,128]{5,4,3,2,1,0:T(8,128)(2,1)S(1)} copy(bf16[4,3,2,2,96,128]{5,2,3,1,4,0:T(2,128)(2,1)} %bitcast.8) | data formatting | bytes 2359296 | tf_op jit(solution)/shard_map/transpose | solution.py:318
  2.3 3.3 %shard_map.86 = (s32[26,4,384]{2,1,0:T(4,128)S(1)}, f32[4,16,128]{2,1,0:T(8,128)S(1)}, bf16[4,13,96,128]{3,2,1,0:T(8,128)(2,1)S(1)}, bf16[4,6,96,128]{3,2,1,0:T(...) custom-call(s32[4,26]{1,0:T(4,128)S(1)} %copy-done.3, s32[128]{0:T(128)S(1)} %copy-done.4, ...), custom_call_target="tpu_custom_call" | custom-call | flops 2000000000 | bytes 3145728 | tf_op jit(solution)/shard_map/pallas_call | solution.py:326
  5.6 4.4 %collective-permute-start.1 = (bf16[4,6,96,128]{3,2,1,0:T(8,128)(2,1)}, bf16[4,6,96,128]{3,2,1,0:T(8,128)(2,1)}, u32[]{:S(2)}, u32[]{:S(2)}) collective-permute-start(bf16[4,6,96,128]{3,2,1,0:T(8,128)(2,1)} %get-tuple-element.67), channel_id=1, source_target_pairs={{0,1},{1,2},{2,3},{4,5},{5,6},{6,7},{8,9},{9,10},{10,11},{12,13},{... | collective-permute-start | bytes 1769480 | tf_op jit(solution)/shard_map/ppermute | solution.py:368
  11.3 6.3 %collective-permute-start.3 = (bf16[4,13,96,128]{3,2,1,0:T(8,128)(2,1)S(1)}, bf16[4,13,96,128]{3,2,1,0:T(8,128)(2,1)S(1)}, u32[]{:S(2)}, u32[]{:S(2)}) collective-permute-start(bf16[4,13,96,128]{3,2,1,0:T(8,128)(2,1)S(1)} %get-tuple-element.64.v), channel_id=1, source_target_pairs={{0,120},{4,124},{8,0},{12,4},{16,8},{20,12},{24,16},{28,20},{32,24... | collective-permute-start | bytes 3833864 | tf_op jit(solution)/shard_map/ppermute | solution.py:365
  17.8 4.7 %shard_map.87.found = bf16[4,96,2304]{2,1,0:T(8,128)(2,1)S(1)} custom-call(bf16[4,13,96,128]{3,2,1,0:T(8,128)(2,1)S(1)} %get-tuple-element.64.v, bf16[4,13,96,128]{3,2,1,0:T(8,128)(2,1)} %collective-permute-done.v_other, f32[4,16,128]{2,1,0:T(8,128)S(1)} %get-tuple-element.65.back), custom_call_target="tpu_custom_call" | custom-call | flops 100000000 | bytes 262144 | tf_op jit(solution)/shard_map/pallas_call | solution.py:377
  22.5 5.9 %shard_map.88.inner = f32[4,6,96,256]{3,2,1,0:T(8,128)S(1)} custom-call(f32[26,9]{1,0:T(8,128)S(1)} %copy.17.coup, bf16[4,13,96,128]{3,2,1,0:T(8,128)(2,1)S(1)} %get-tuple-element.64.v, f32[4,26,2,2,128]{4,3,2,1,0:T(2,128)S(1)} %copy-done, f32[4,2,2,128]{3,2,1,0:T(2,128)S(1)} %copy-done.1), custom_call_target="tpu_custom_call" | custom-call | flops 100000000 | bytes 262144 | tf_op jit(solution)/shard_map/pallas_call | solution.py:391
  28.5 4.9 %shard_map.89.a = bf16[4,6,96,256]{3,2,1,0:T(8,128)(2,1)S(1)} custom-call(f32[26,9]{1,0:T(8,128)S(1)} %copy.17.coup, f32[4,6,96,256]{3,2,1,0:T(8,128)S(1)} %shard_map.88.inner, bf16[4,6,96,128]{3,2,1,0:T(8,128)(2,1)} %collective-permute-done.1.below, bf16[4,6,96,128]{3,2,1,0:T(8,128)(2,1)} %collective-permute-done.2.above, f32[4,26,2,2,128]{4,3,2,1,0:T(2,128)S(1)} %copy-done), custom_call_target="tpu_custom_call" | custom-call | flops 3000000000 | bytes 6291456 | tf_op jit(solution)/shard_map/pallas_call | solution.py:410
  33.3 4.3 %shard_map.91.refs_1_.refs_4_.refs_10_.refs_16_.refs_18_.refs_22_.refs_8_.refs_12_.refs_3_.refs_7_.refs_11_.refs_15_ = bf16[96,9984]{1,0:T(8,128)(2,1)S(1)} custom-call(bf16[4,6,96,256]{3,2,1,0:T(8,128)(2,1)S(1)} %shard_map.89.a, s32[26,4,384]{2,1,0:T(4,128)S(1)} %get-tuple-element.75.idx), custom_call_target="tpu_custom_call" | custom-call | flops 6000000000 | bytes 4194304 | tf_op jit(solution)/shard_map/pallas_call | solution.py:424
  37.6 4.3 %shard_map.92.refs_2_.refs_6_.refs_8_.refs_13_.refs_14_.refs_20_.refs_10_.refs_1_.refs_5_.refs_9_ = bf16[96,9984]{1,0:T(8,128)(2,1)S(1)} custom-call(bf16[4,6,96,256]{3,2,1,0:T(8,128)(2,1)S(1)} %shard_map.89.a, s32[26,4,384]{2,1,0:T(4,128)S(1)} %get-tuple-element.75.idx), custom_call_target="tpu_custom_call" | custom-call | flops 6000000000 | bytes 4194304 | tf_op jit(solution)/shard_map/pallas_call | solution.py:424
  41.9 3.4 %collective-permute-done.3.refs_0_ = bf16[4,13,96,128]{3,2,1,0:T(8,128)(2,1)S(1)} collective-permute-done((bf16[4,13,96,128]{3,2,1,0:T(8,128)(2,1)S(1)}, bf16[4,13,96,128]{3,2,1,0:T(8,128)(2,1)S(1)}, u32[]{:S(2)}, u32[]{:S(2)}) %collective-permute-start.3) | collective-permute-done | bytes 1277984 | tf_op jit(solution)/shard_map/ppermute | solution.py:365
  45.3 5.6 %collective-permute-done.4.refs_1_ = bf16[4,13,96,128]{3,2,1,0:T(8,128)(2,1)} collective-permute-done((bf16[4,13,96,128]{3,2,1,0:T(8,128)(2,1)S(1)}, bf16[4,13,96,128]{3,2,1,0:T(8,128)(2,1)}, u32[]{:S(2)}, u32[]{:S(2)}) %collective-permute-start.4) | collective-permute-done | bytes 1277984 | tf_op jit(solution)/shard_map/ppermute | solution.py:365
  52.8 4.3 %shard_map.90.refs_0_.refs_3_.refs_9_.refs_15_.refs_19_.refs_21_.refs_7_.refs_11_.refs_2_.refs_6_.refs_10_.refs_14_ = bf16[96,9984]{1,0:T(8,128)(2,1)S(1)} custom-call(bf16[4,6,96,256]{3,2,1,0:T(8,128)(2,1)S(1)} %shard_map.89.a, s32[26,4,384]{2,1,0:T(4,128)S(1)} %get-tuple-element.75.idx), custom_call_target="tpu_custom_call" | custom-call | flops 6000000000 | bytes 4194304 | tf_op jit(solution)/shard_map/pallas_call | solution.py:424
  57.1 4.3 %shard_map.93.refs_5_.refs_7_.refs_11_.refs_12_.refs_17_.refs_23_.refs_9_.refs_13_.refs_4_.refs_8_.refs_16_ = bf16[96,9984]{1,0:T(8,128)(2,1)S(1)} custom-call(bf16[4,6,96,256]{3,2,1,0:T(8,128)(2,1)S(1)} %shard_map.89.a, s32[26,4,384]{2,1,0:T(4,128)S(1)} %get-tuple-element.75.idx), custom_call_target="tpu_custom_call" | custom-call | flops 6000000000 | bytes 4194304 | tf_op jit(solution)/shard_map/pallas_call | solution.py:424
  61.3 2.4 %shard_map.94 = (f32[32,2304]{1,0:T(8,128)S(1)}, bf16[32,2304]{1,0:T(8,128)(2,1)S(1)}, bf16[32,2304]{1,0:T(8,128)(2,1)S(1)}, bf16[32,2304]{1,0:T(8,128)(2,1)S(1)}) custom-call(s32[128]{0:T(128)S(1)} %get-tuple-element.63.slots, bf16[4,96,2304]{2,1,0:T(8,128)(2,1)S(1)} %shard_map.87.found, bf16[4,6,96,256]{3,2,1,0:T(8,128)(2,1)S(1)} %shard_map.89.a, ...), custom_call_target="tpu_custom_call" | custom-call | flops 3000000000 | bytes 8388608 | tf_op jit(solution)/shard_map/pallas_call | solution.py:461
  63.8 3.9 %collective-permute-start.10 = (bf16[32,2304]{1,0:T(8,128)(2,1)S(1)}, bf16[32,2304]{1,0:T(8,128)(2,1)S(1)}, u32[]{:S(2)}, u32[]{:S(2)}) collective-permute-start(bf16[32,2304]{1,0:T(8,128)(2,1)S(1)} %get-tuple-element.102), channel_id=1, source_target_pairs={{0,3},{1,0},{2,1},{3,2},{4,7},{5,4},{6,5},{7,6},{8,11},{9,8},{10,9... | collective-permute-start | bytes 442376 | tf_op jit(solution)/shard_map/ppermute | solution.py:307
  68.6 8.3 %shard_map.95 = (f32[48,2304]{1,0:T(8,128)S(1)}, bf16[48,2304]{1,0:T(8,128)(2,1)S(1)}, bf16[48,2304]{1,0:T(8,128)(2,1)S(1)}, bf16[48,2304]{1,0:T(8,128)(2,1)S(1)}) custom-call(s32[128]{0:T(128)S(1)} %get-tuple-element.63.slots, bf16[4,13,96,128]{3,2,1,0:T(8,128)(2,1)S(1)} %collective-permute-done.3.refs_0_, ...), custom_call_target="tpu_custom_call" | custom-call | flops 10000000000 | bytes 10485760 | tf_op jit(solution)/shard_map/pallas_call | solution.py:489
  77.0 3.8 %shard_map.96 = (f32[48,2304]{1,0:T(8,128)S(1)}, bf16[48,2304]{1,0:T(8,128)(2,1)S(1)}, bf16[48,2304]{1,0:T(8,128)(2,1)S(1)}, bf16[48,2304]{1,0:T(8,128)(2,1)S(1)}) custom-call(s32[128]{0:T(128)S(1)} %get-tuple-element.63.slots, ...), custom_call_target="tpu_custom_call", output_to_operand_aliasing={{0}: (18, {}), {1}: (19, {}), {2}: (20, {}), {3}: (21, {})} | custom-call | flops 5000000000 | bytes 5242880 | tf_op jit(solution)/shard_map/pallas_call | solution.py:489
  80.8 3.0 %collective-permute-start.13 = (bf16[48,2304]{1,0:T(8,128)(2,1)S(1)}, bf16[48,2304]{1,0:T(8,128)(2,1)S(1)}, u32[]{:S(2)}, u32[]{:S(2)}) collective-permute-start(bf16[48,2304]{1,0:T(8,128)(2,1)S(1)} %get-tuple-element.114), channel_id=1, source_target_pairs={{0,3},{1,0},{2,1},{3,2},{4,7},{5,4},{6,5},{7,6},{8,11},{9,8},{10,9... | collective-permute-start | bytes 663560 | tf_op jit(solution)/shard_map/ppermute | solution.py:307
  83.8 1.7 %collective-permute-start.12 = (bf16[48,2304]{1,0:T(8,128)(2,1)S(1)}, bf16[48,2304]{1,0:T(8,128)(2,1)S(1)}, u32[]{:S(2)}, u32[]{:S(2)}) collective-permute-start(bf16[48,2304]{1,0:T(8,128)(2,1)S(1)} %get-tuple-element.111), channel_id=1, source_target_pairs={{0,2},{1,3},{2,0},{3,1},{4,6},{5,7},{6,4},{7,5},{8,10},{9,11},{10,... | collective-permute-start | bytes 663560 | tf_op jit(solution)/shard_map/ppermute | solution.py:307
  85.5 7.9 %shard_map.97 = (f32[32,2304]{1,0:T(8,128)S(1)}, bf16[32,2304]{1,0:T(8,128)(2,1)S(1)}, bf16[32,2304]{1,0:T(8,128)(2,1)S(1)}, bf16[32,2304]{1,0:T(8,128)(2,1)S(1)}) custom-call(s32[128]{0:T(128)S(1)} %get-tuple-element.63.slots, bf16[4,13,96,128]{3,2,1,0:T(8,128)(2,1)S(1)} %collective-permute-done.5.refs_0_, ...), custom_call_target="tpu_custom_call" | custom-call | flops 10000000000 | bytes 10485760 | tf_op jit(solution)/shard_map/pallas_call | solution.py:489
  93.3 3.3 %collective-permute-start.16 = (bf16[32,2304]{1,0:T(8,128)(2,1)S(1)}, bf16[32,2304]{1,0:T(8,128)(2,1)S(1)}, u32[]{:S(2)}, u32[]{:S(2)}) collective-permute-start(bf16[32,2304]{1,0:T(8,128)(2,1)S(1)} %get-tuple-element.119), channel_id=1, source_target_pairs={{0,3},{1,0},{2,1},{3,2},{4,7},{5,4},{6,5},{7,6},{8,11},{9,8},{10,9... | collective-permute-start | bytes 442376 | tf_op jit(solution)/shard_map/ppermute | solution.py:307
  97.6 4.1 %collective-permute-done.16.refs_11_ = bf16[32,2304]{1,0:T(8,128)(2,1)S(1)} collective-permute-done((bf16[32,2304]{1,0:T(8,128)(2,1)S(1)}, bf16[32,2304]{1,0:T(8,128)(2,1)S(1)}, u32[]{:S(2)}, u32[]{:S(2)}) %collective-permute-start.16) | collective-permute-done | bytes 147488 | tf_op jit(solution)/shard_map/ppermute | solution.py:307
  101.7 2.2 %collective-permute-done.15.refs_10_ = bf16[32,2304]{1,0:T(8,128)(2,1)S(1)} collective-permute-done((bf16[32,2304]{1,0:T(8,128)(2,1)S(1)}, bf16[32,2304]{1,0:T(8,128)(2,1)S(1)}, u32[]{:S(2)}, u32[]{:S(2)}) %collective-permute-start.15) | collective-permute-done | bytes 147488 | tf_op jit(solution)/shard_map/ppermute | solution.py:307
  105.3 1.7 %shard_map.98 = (f32[26,4,2304]{2,1,0:T(4,128)}, f32[4,2304]{1,0:T(4,128)}) custom-call(f32[104,128]{1,0:T(8,128)S(1)} %get-tuple-element.62.order, f32[32,2304]{1,0:T(8,128)S(1)} %get-tuple-element.82.refs_0_, bf16[32,2304]{1,0:T(8,128)(2,1)S(1)} %collective-permute-done.8.refs_1_, bf16[32,2304]{1,0:T(8,128)(2,1)S(1)} %collective-permute-done.9.refs_2_, ...), custom_call_target="tpu_custom_call" | custom-call | flops 10000000 | bytes 4194304 | tf_op jit(solution)/shard_map/pallas_call | solution.py:514
  (39 shorter events, 6.7 us)
Async XLA Ops:
  0.6 1.6 %copy-start.4 = (s32[128]{0:T(128)S(1)}, s32[128]{0:T(128)}, u32[]{:S(2)}) copy-start(s32[128]{0:T(128)} %constant.22.clone.maps) | copy-start | bytes 1540
  0.6 1.6 %copy-start.2 = (s32[4,26,384]{2,0,1:T(4,128)S(1)}, s32[4,26,384]{2,0,1:T(4,128)}, u32[]{:S(2)}) copy-start(s32[4,26,384]{2,0,1:T(4,128)} %param.12) | copy-start | bytes 479236
  0.7 1.6 %copy-start.3 = (s32[4,26]{1,0:T(4,128)S(1)}, s32[4,26]{1,0:T(4,128)}, u32[]{:S(2)}) copy-start(s32[4,26]{1,0:T(4,128)} %neighbours.1) | copy-start | bytes 1252
  2.3 15.4 %copy-start.5 = (f32[26,3,3]{0,2,1:T(4,128)S(1)}, f32[26,3,3]{0,2,1:T(4,128)}, u32[]{:S(2)}) copy-start(f32[26,3,3]{0,2,1:T(4,128)} %param.10) | copy-start | bytes 2812
  5.5 12.2 %collective-permute-start = (bf16[4,13,96,128]{3,2,1,0:T(8,128)(2,1)S(1)}, bf16[4,13,96,128]{3,2,1,0:T(8,128)(2,1)}, u32[]{:S(2)}, u32[]{:S(2)}) collective-permute-start(bf16[4,13,96,128]{3,2,1,0:T(8,128)(2,1)S(1)} %get-tuple-element.64.v), channel_id=1, source_target_pairs={{0,4},{4,0},{8,12},{12,8},{16,20},{20,16},{24,28},{28,24},{32,36},... | collective-permute-start | bytes 3833864 | tf_op jit(solution)/shard_map/ppermute | solution.py:366
  5.6 22.8 %collective-permute-start.1 = (bf16[4,6,96,128]{3,2,1,0:T(8,128)(2,1)}, bf16[4,6,96,128]{3,2,1,0:T(8,128)(2,1)}, u32[]{:S(2)}, u32[]{:S(2)}) collective-permute-start(bf16[4,6,96,128]{3,2,1,0:T(8,128)(2,1)} %get-tuple-element.67), channel_id=1, source_target_pairs={{0,1},{1,2},{2,3},{4,5},{5,6},{6,7},{8,9},{9,10},{10,11},{12,13},{... | collective-permute-start | bytes 1769480 | tf_op jit(solution)/shard_map/ppermute | solution.py:368
  10.0 18.4 %collective-permute-start.2 = (bf16[4,6,96,128]{3,2,1,0:T(8,128)(2,1)S(1)}, bf16[4,6,96,128]{3,2,1,0:T(8,128)(2,1)}, u32[]{:S(2)}, u32[]{:S(2)}) collective-permute-start(bf16[4,6,96,128]{3,2,1,0:T(8,128)(2,1)S(1)} %get-tuple-element.68), channel_id=1, source_target_pairs={{1,0},{2,1},{3,2},{5,4},{6,5},{7,6},{9,8},{10,9},{11,10},{13,12},{... | collective-permute-start | bytes 1769480 | tf_op jit(solution)/shard_map/ppermute | solution.py:369
  11.3 34.0 %collective-permute-start.3 = (bf16[4,13,96,128]{3,2,1,0:T(8,128)(2,1)S(1)}, bf16[4,13,96,128]{3,2,1,0:T(8,128)(2,1)S(1)}, u32[]{:S(2)}, u32[]{:S(2)}) collective-permute-start(bf16[4,13,96,128]{3,2,1,0:T(8,128)(2,1)S(1)} %get-tuple-element.64.v), channel_id=1, source_target_pairs={{0,120},{4,124},{8,0},{12,4},{16,8},{20,12},{24,16},{28,20},{32,24... | collective-permute-start | bytes 3833864 | tf_op jit(solution)/shard_map/ppermute | solution.py:365
  17.6 33.3 %collective-permute-start.4 = (bf16[4,13,96,128]{3,2,1,0:T(8,128)(2,1)S(1)}, bf16[4,13,96,128]{3,2,1,0:T(8,128)(2,1)}, u32[]{:S(2)}, u32[]{:S(2)}) collective-permute-start(bf16[4,13,96,128]{3,2,1,0:T(8,128)(2,1)S(1)} %get-tuple-element.64.v), channel_id=1, source_target_pairs={{0,8},{4,12},{8,16},{12,20},{16,24},{20,28},{24,32},{28,36},{32,40... | collective-permute-start | bytes 3833864 | tf_op jit(solution)/shard_map/ppermute | solution.py:365
  17.7 4.7 %copy-start = (f32[4,26,2,2,128]{4,3,2,1,0:T(2,128)S(1)}, f32[4,26,2,2,128]{4,3,2,1,0:T(2,128)}, u32[]{:S(2)}) copy-start(f32[4,26,2,2,128]{4,3,2,1,0:T(2,128)} %stiff.1) | copy-start | bytes 638980
  17.7 4.7 %copy-start.1 = (f32[4,2,2,128]{3,2,1,0:T(2,128)S(1)}, f32[4,2,2,128]{3,2,1,0:T(2,128)}, u32[]{:S(2)}) copy-start(f32[4,2,2,128]{3,2,1,0:T(2,128)} %center.1) | copy-start | bytes 24580
  51.0 12.8 %collective-permute-start.5 = (bf16[4,13,96,128]{3,2,1,0:T(8,128)(2,1)S(1)}, bf16[4,13,96,128]{3,2,1,0:T(8,128)(2,1)S(1)}, u32[]{:S(2)}, u32[]{:S(2)}) collective-permute-start(bf16[4,13,96,128]{3,2,1,0:T(8,128)(2,1)S(1)} %collective-permute-done.3.refs_0_), channel_id=1, source_target_pairs={{0,4},{4,0},{8,12},{12,8},{16,20},{20,16},{24,28},{28,24},{32,36},... | collective-permute-start | bytes 3833864 | tf_op jit(solution)/shard_map/ppermute | solution.py:366
  51.0 12.8 %collective-permute-start.6 = (bf16[4,13,96,128]{3,2,1,0:T(8,128)(2,1)}, bf16[4,13,96,128]{3,2,1,0:T(8,128)(2,1)S(1)}, u32[]{:S(2)}, u32[]{:S(2)}) collective-permute-start(bf16[4,13,96,128]{3,2,1,0:T(8,128)(2,1)} %collective-permute-done.4.refs_1_), channel_id=1, source_target_pairs={{0,4},{4,0},{8,12},{12,8},{16,20},{20,16},{24,28},{28,24},{32,36},... | collective-permute-start | bytes 3833864 | tf_op jit(solution)/shard_map/ppermute | solution.py:366
  51.6 25.3 %collective-permute-start.7 = (bf16[4,13,96,128]{3,2,1,0:T(8,128)(2,1)S(1)}, bf16[4,13,96,128]{3,2,1,0:T(8,128)(2,1)S(1)}, u32[]{:S(2)}, u32[]{:S(2)}) collective-permute-start(bf16[4,13,96,128]{3,2,1,0:T(8,128)(2,1)S(1)} %broadcast_select_fusion), channel_id=1, source_target_pairs={{0,124},{4,8},{8,4},{12,16},{16,12},{20,24},{24,20},{28,32},{32,28... | collective-permute-start | bytes 3833864 | tf_op jit(solution)/shard_map/ppermute | solution.py:445
  63.8 17.0 %collective-permute-start.10 = (bf16[32,2304]{1,0:T(8,128)(2,1)S(1)}, bf16[32,2304]{1,0:T(8,128)(2,1)S(1)}, u32[]{:S(2)}, u32[]{:S(2)}) collective-permute-start(bf16[32,2304]{1,0:T(8,128)(2,1)S(1)} %get-tuple-element.102), channel_id=1, source_target_pairs={{0,3},{1,0},{2,1},{3,2},{4,7},{5,4},{6,5},{7,6},{8,11},{9,8},{10,9... | collective-permute-start | bytes 442376 | tf_op jit(solution)/shard_map/ppermute | solution.py:307
  67.7 16.1 %collective-permute-start.9 = (bf16[32,2304]{1,0:T(8,128)(2,1)S(1)}, bf16[32,2304]{1,0:T(8,128)(2,1)S(1)}, u32[]{:S(2)}, u32[]{:S(2)}) collective-permute-start(bf16[32,2304]{1,0:T(8,128)(2,1)S(1)} %get-tuple-element.99), channel_id=1, source_target_pairs={{0,2},{1,3},{2,0},{3,1},{4,6},{5,7},{6,4},{7,5},{8,10},{9,11},{10,... | collective-permute-start | bytes 442376 | tf_op jit(solution)/shard_map/ppermute | solution.py:307
  68.3 17.1 %collective-permute-start.8 = (bf16[32,2304]{1,0:T(8,128)(2,1)S(1)}, bf16[32,2304]{1,0:T(8,128)(2,1)S(1)}, u32[]{:S(2)}, u32[]{:S(2)}) collective-permute-start(bf16[32,2304]{1,0:T(8,128)(2,1)S(1)} %get-tuple-element.96), channel_id=1, source_target_pairs={{0,1},{1,2},{2,3},{3,0},{4,5},{5,6},{6,7},{7,4},{8,9},{9,10},{10,1... | collective-permute-start | bytes 442376 | tf_op jit(solution)/shard_map/ppermute | solution.py:307
  80.8 12.6 %collective-permute-start.13 = (bf16[48,2304]{1,0:T(8,128)(2,1)S(1)}, bf16[48,2304]{1,0:T(8,128)(2,1)S(1)}, u32[]{:S(2)}, u32[]{:S(2)}) collective-permute-start(bf16[48,2304]{1,0:T(8,128)(2,1)S(1)} %get-tuple-element.114), channel_id=1, source_target_pairs={{0,3},{1,0},{2,1},{3,2},{4,7},{5,4},{6,5},{7,6},{8,11},{9,8},{10,9... | collective-permute-start | bytes 663560 | tf_op jit(solution)/shard_map/ppermute | solution.py:307
  83.8 12.9 %collective-permute-start.12 = (bf16[48,2304]{1,0:T(8,128)(2,1)S(1)}, bf16[48,2304]{1,0:T(8,128)(2,1)S(1)}, u32[]{:S(2)}, u32[]{:S(2)}) collective-permute-start(bf16[48,2304]{1,0:T(8,128)(2,1)S(1)} %get-tuple-element.111), channel_id=1, source_target_pairs={{0,2},{1,3},{2,0},{3,1},{4,6},{5,7},{6,4},{7,5},{8,10},{9,11},{10,... | collective-permute-start | bytes 663560 | tf_op jit(solution)/shard_map/ppermute | solution.py:307
  85.4 11.9 %collective-permute-start.11 = (bf16[48,2304]{1,0:T(8,128)(2,1)S(1)}, bf16[48,2304]{1,0:T(8,128)(2,1)S(1)}, u32[]{:S(2)}, u32[]{:S(2)}) collective-permute-start(bf16[48,2304]{1,0:T(8,128)(2,1)S(1)} %get-tuple-element.108), channel_id=1, source_target_pairs={{0,1},{1,2},{2,3},{3,0},{4,5},{5,6},{6,7},{7,4},{8,9},{9,10},{10,1... | collective-permute-start | bytes 663560 | tf_op jit(solution)/shard_map/ppermute | solution.py:307
  93.3 8.3 %collective-permute-start.16 = (bf16[32,2304]{1,0:T(8,128)(2,1)S(1)}, bf16[32,2304]{1,0:T(8,128)(2,1)S(1)}, u32[]{:S(2)}, u32[]{:S(2)}) collective-permute-start(bf16[32,2304]{1,0:T(8,128)(2,1)S(1)} %get-tuple-element.119), channel_id=1, source_target_pairs={{0,3},{1,0},{2,1},{3,2},{4,7},{5,4},{6,5},{7,6},{8,11},{9,8},{10,9... | collective-permute-start | bytes 442376 | tf_op jit(solution)/shard_map/ppermute | solution.py:307
  96.6 7.2 %collective-permute-start.15 = (bf16[32,2304]{1,0:T(8,128)(2,1)S(1)}, bf16[32,2304]{1,0:T(8,128)(2,1)S(1)}, u32[]{:S(2)}, u32[]{:S(2)}) collective-permute-start(bf16[32,2304]{1,0:T(8,128)(2,1)S(1)} %get-tuple-element.118), channel_id=1, source_target_pairs={{0,2},{1,3},{2,0},{3,1},{4,6},{5,7},{6,4},{7,5},{8,10},{9,11},{10,... | collective-permute-start | bytes 442376 | tf_op jit(solution)/shard_map/ppermute | solution.py:307
  97.3 8.0 %collective-permute-start.14 = (bf16[32,2304]{1,0:T(8,128)(2,1)S(1)}, bf16[32,2304]{1,0:T(8,128)(2,1)S(1)}, u32[]{:S(2)}, u32[]{:S(2)}) collective-permute-start(bf16[32,2304]{1,0:T(8,128)(2,1)S(1)} %get-tuple-element.117), channel_id=1, source_target_pairs={{0,1},{1,2},{2,3},{3,0},{4,5},{5,6},{6,7},{7,4},{8,9},{9,10},{10,1... | collective-permute-start | bytes 442376 | tf_op jit(solution)/shard_map/ppermute | solution.py:307
